TPU v7x, 32 devices: a whole 2x2x4 slice. The times are simulated.
32 devices in a mesh: rows: 8 (over z, y), bands: 4 (over x, core).
Axes of the slice: x: 2, y: 2, z: 4, core: 2. Of those that a mesh axis runs over, the one named last changes fastest.
Arguments:
- vectors: float32 [8192, 1024], P('rows', 'bands'), may hold values from -6 to 6
- local_blocks: float32 [64, 6, 128, 128], P('rows'), may hold values from -0.078125 to 0.078125
- local_cols: int32 [64, 6], P('rows'), may hold values from 0 to 7
- coupling_blocks: float32 [3, 64, 2, 128, 128], P(None, 'rows'), may hold values from -0.078125 to 0.078125
- coupling_cols: int32 [3, 64, 2], replicated, may hold values from 0 to 7
- partners: int32 [3, 8], replicated, may hold values from 0 to 7, as said below
- bounds: float32 [3], replicated, may hold values from -2.8 to 2.8, as said below
- rotation: float32 [1024, 1024], replicated, may hold values from -1 to 1
Outputs:
- rotated: float32 [8192, 1024], P('rows', 'bands')
Inputs may be any that keep to these rules, and one draw needn't show every extreme that they name: For each colour c there is a bit number b_c, with the three b_c distinct, such that partners[c, i] = i XOR 2 ** b_c for every row shard i. `local_cols`: local block columns count inside the row shard itself. `coupling_cols`: coupling block columns count inside the partner shard of that colour. bounds[0] < bounds[1] < bounds[2].
All inputs are finite; a program needn't handle non-finite values.
Results may differ from a plain program's by a relative error of at most 0.0003.
Values sent between devices are 32-bit elements; how exact they have to be, the bound alone decides.
No kernel may reach another device: no remote copies, remote signals or barrier semaphores. Data moves between devices by JAX's collectives and lax.ppermute only.
A program may use at most 128 MiB of HBM per device.

v0:
```python
import jax
import jax.numpy as jnp
from jax import lax
from jax.sharding import PartitionSpec as P

precise = lax.Precision.HIGHEST


def forward(blocks, block_cols, source):
    picked = jnp.take(source, block_cols, axis=0)
    return jnp.einsum("akij,akjw->aiw", blocks, picked, precision=precise)


def backward(blocks, block_cols, source, block_count):
    products = jnp.einsum("akij,aiw->akjw", blocks, source, precision=precise)
    targets = jnp.arange(block_count, dtype=jnp.int32)
    onehot = (block_cols[:, :, None] == targets[None, None, :]).astype(jnp.float32)
    return jnp.einsum("akc,akjw->cjw", onehot, products, precision=precise)


def route_pair(payload, mate_table):
    kind_count, row_count, band_width = payload.shape
    shard_count = mate_table.shape[0]
    pieces = payload.reshape(kind_count, shard_count, row_count // shard_count, band_width)
    spread = lax.all_to_all(pieces, "rows", split_axis=1, concat_axis=1, tiled=True)
    regrouped = jnp.take(spread, mate_table, axis=1)
    arrived = lax.all_to_all(regrouped, "rows", split_axis=1, concat_axis=1, tiled=True)
    return arrived.reshape(kind_count, row_count, band_width)


def route_blocks(coupling_blocks, partners):
    block_shape = coupling_blocks.shape
    shard_count = partners.shape[1]
    flattened = coupling_blocks.reshape(3, shard_count, -1, block_shape[-1])
    spread = lax.all_to_all(flattened, "rows", split_axis=1, concat_axis=1, tiled=True)
    regrouped = jnp.stack(
        [jnp.take(spread[colour], partners[colour], axis=0) for colour in range(3)]
    )
    arrived = lax.all_to_all(regrouped, "rows", split_axis=1, concat_axis=1, tiled=True)
    return arrived.reshape(block_shape)


def local(
    vectors, local_blocks, local_cols, coupling_blocks, coupling_cols, partners, bounds, rotation
):
    row_count, band_width = vectors.shape
    block_size = local_blocks.shape[2]
    block_count = row_count // block_size
    my_index = lax.axis_index("rows")
    mate_ids = partners[:, my_index]
    colour_cols = lax.dynamic_slice_in_dim(coupling_cols, my_index * block_count, block_count, 1)
    mate_cols = [
        lax.dynamic_slice_in_dim(
            coupling_cols[colour], mate_ids[colour] * block_count, block_count, 0
        )
        for colour in range(3)
    ]
    mate_blocks = route_blocks(coupling_blocks, partners)

    def as_blocks(current):
        return current.reshape(block_count, block_size, band_width)

    def apply_field(current):
        source = as_blocks(current)
        result = forward(local_blocks, local_cols, source) + backward(
            local_blocks, local_cols, source, block_count
        )
        mate_fields = jnp.stack(
            [route_pair(current[None], partners[colour])[0] for colour in range(3)]
        )
        for colour in range(3):
            mate_source = as_blocks(mate_fields[colour])
            result = result + forward(coupling_blocks[colour], colour_cols[colour], mate_source)
            result = result + backward(
                mate_blocks[colour], mate_cols[colour], mate_source, block_count
            )
        return result.reshape(row_count, band_width)

    lowest, lower, upper = (bounds[0], bounds[1], bounds[2])
    half_width = (upper - lower) / 2.0
    centre = (upper + lower) / 2.0
    sigma_one = half_width / (lowest - centre)
    sigma_two = 1.0 / (2.0 / sigma_one - sigma_one)
    filtered = (apply_field(vectors) - centre * vectors) * (sigma_one / half_width)
    second = (apply_field(filtered) - centre * filtered) * (
        2.0 * sigma_two / half_width
    ) - sigma_one * sigma_two * vectors
    row_start = lax.axis_index("bands") * band_width
    weights = lax.dynamic_slice_in_dim(rotation, row_start, band_width, 0)
    partial_sum = jnp.dot(second, weights, precision=precise, preferred_element_type=jnp.float32)
    return lax.psum_scatter(partial_sum, "bands", scatter_dimension=1, tiled=True)


def solution(mesh):
    in_specs = (
        P("rows", "bands"),
        P("rows", None, None, None),
        P("rows", None),
        P(None, "rows", None, None, None),
        P(),
        P(),
        P(),
        P(),
    )
    out_specs = P("rows", "bands")
    return jax.shard_map(local, mesh=mesh, in_specs=in_specs, out_specs=out_specs, check_vma=False)
```

profile of v0, /device:TPU:0, one launch (start us, length us, event | category | flops | bytes accessed | tf_op | source)
XLA Modules:
  0.0 547.2 jit_solution(1673869614671636114)
XLA Ops:
  6.5 7.5 %all-to-all-start = ((f32[1,8,128,256]{3,2,0,1:T(8,128)}), f32[1,8,128,256]{3,2,0,1:T(8,128)}, u32[]{:S(2)}, u32[]{:S(2)}) async-start(f32[1,8,128,256]{3,2,0,1:T(8,128)} %bitcast.305), calls=%async_computation | async-start | bytes 2097152 | tf_op jit(solution)/shard_map/all_to_all | solution.py:25
  14.1 25.8 %all-to-all-done = f32[1,8,128,256]{3,2,0,1:T(8,128)} async-done(((f32[1,8,128,256]{3,2,0,1:T(8,128)}), f32[1,8,128,256]{3,2,0,1:T(8,128)}, u32[]{:S(2)}, u32[]{:S(2)}) %all-to-all-start) | async-done | bytes 1048608 | tf_op jit(solution)/shard_map/all_to_all | solution.py:25
  45.2 4.2 all-to-all-start.1
  54.6 20.4 %all-to-all-done.1 = f32[1,8,128,256]{3,2,0,1:T(8,128)} async-done(((f32[1,8,128,256]{3,2,0,1:T(8,128)}), f32[1,8,128,256]{3,2,0,1:T(8,128)}, u32[]{:S(2)}, u32[]{:S(2)}) %all-to-all-start.1) | async-done | bytes 1048608 | tf_op jit(solution)/shard_map/all_to_all | solution.py:27
  75.0 4.2 all-to-all-start.4
  79.3 3.9 copy.97
  83.2 21.5 %all-to-all-done.4 = f32[1,8,128,256]{3,2,0,1:T(8,128)} async-done(((f32[1,8,128,256]{3,2,0,1:T(8,128)}), f32[1,8,128,256]{3,2,0,1:T(8,128)}, u32[]{:S(2)}, u32[]{:S(2)}) %all-to-all-start.4) | async-done | bytes 1048608 | tf_op jit(solution)/shard_map/all_to_all | solution.py:27
  104.7 4.5 all-to-all-start.2
  114.3 64.7 %all-to-all-done.2 = f32[3,8,256,128]{3,2,0,1:T(8,128)} async-done(((f32[3,8,256,128]{3,2,0,1:T(8,128)}), f32[3,8,256,128]{3,2,0,1:T(8,128)}, u32[]{:S(2)}, u32[]{:S(2)}) %all-to-all-start.2) | async-done | bytes 3145760 | tf_op jit(solution)/shard_map/all_to_all | solution.py:35
  179.1 4.2 all-to-all-start.5
  183.3 3.6 slice_bitcast_fusion.2
  199.8 9.2 %all-to-all-done.5 = f32[1,8,128,256]{3,2,0,1:T(8,128)} async-done(((f32[1,8,128,256]{3,2,0,1:T(8,128)}), f32[1,8,128,256]{3,2,0,1:T(8,128)}, u32[]{:S(2)}, u32[]{:S(2)}) %all-to-all-start.5) | async-done | bytes 1048608 | tf_op jit(solution)/shard_map/all_to_all | solution.py:27
  208.9 4.7 all-to-all-start.3
  221.1 4.9 gather_fusion
  226.2 6.8 %fusion.207 = f32[8,6,128,256]{3,2,1,0:T(8,128)S(1)} fusion(f32[8,6,128,128]{3,2,1,0:T(8,128)S(1)} %copy-done, f32[8,128,256,1]{2,1,3,0:T(8,128)} %bitcast.307), kind=kOutput, calls=%fused_computation.207 | convolution fusion | flops 2415919104 | bytes 10485760 | tf_op jit(solution)/shard_map/akij,aiw->akjw/dot_general | solution.py:15
  233.0 8.7 %fusion.76 = f32[8,128,256]{2,0,1:T(8,128)} fusion(f32[8,6,128,256]{3,2,1,0:T(8,128)S(1)} %fusion.207, s32[8,6]{0,1:T(8,128)S(1)} %copy.90), kind=kOutput, calls=%fused_computation.67 | convolution fusion | flops 150995328 | bytes 7340224 | tf_op jit(solution)/shard_map/akc,akjw->cjw/dot_general | solution.py:18
  241.7 3.2 gather_fusion.2
  244.9 3.2 gather_fusion.7
  248.2 3.2 gather_fusion.9
  251.4 4.5 fusion.34
  255.9 4.3 fusion.37
  262.8 20.6 %all-to-all-done.3 = f32[3,8,256,128]{3,2,0,1:T(8,128)} async-done(((f32[3,8,256,128]{3,2,0,1:T(8,128)}), f32[3,8,256,128]{3,2,0,1:T(8,128)}, u32[]{:S(2)}, u32[]{:S(2)}) %all-to-all-start.3) | async-done | bytes 3145760 | tf_op jit(solution)/shard_map/all_to_all | solution.py:39
  285.4 3.9 fusion.131
  291.4 3.3 fusion.129
  296.8 3.2 fusion.127
  302.1 5.8 %fusion.106 = f32[8,128,256]{2,1,0:T(8,128)S(1)} fusion(f32[8,128,256]{2,1,0:T(8,128)S(1)} %copy-done.16, f32[8,128,256]{2,1,0:T(8,128)S(1)} %copy-done.15, f32[8,128,256]{2,1,0:T(8,128)S(1)} %copy-done.14, f32[8,6,128,128]{3,2,1,0:T(8,128)S(1)} %copy-done, f32[8,6,128,256]{3,2,1,0:T(8,128)S(1)} %bitcast.313, pred[8,6]{1,0:T(8,128)(4,1)S(1)} %compare_and_fusion, ...), kind=kOutput, calls=%fused_computation.78 | convolution fusion | flops 2419326976 | bytes 17825840 | tf_op jit(solution)/shard_map/akij,akjw->aiw/dot_general | solution.py:11
  309.0 29.4 %all_to_all.54 = f32[1,8,128,256]{3,2,0,1:T(8,128)} all-to-all(f32[1,8,128,256]{3,2,0,1:T(8,128)S(1)} %bitcast.308), channel_id=1, replica_groups=mesh['rows'=8,'bands'=4] {'rows'}, dimensions={1} | all-to-all | bytes 2097152 | tf_op jit(solution)/shard_map/all_to_all | solution.py:25
  343.7 4.2 all-to-all-start.7
  353.1 20.0 %all-to-all-done.7 = f32[1,8,128,256]{3,2,0,1:T(8,128)} async-done(((f32[1,8,128,256]{3,2,0,1:T(8,128)}), f32[1,8,128,256]{3,2,0,1:T(8,128)}, u32[]{:S(2)}, u32[]{:S(2)}) %all-to-all-start.7) | async-done | bytes 1048608 | tf_op jit(solution)/shard_map/all_to_all | solution.py:27
  373.0 4.2 all-to-all-start.8
  382.6 20.0 %all-to-all-done.8 = f32[1,8,128,256]{3,2,0,1:T(8,128)} async-done(((f32[1,8,128,256]{3,2,0,1:T(8,128)}), f32[1,8,128,256]{3,2,0,1:T(8,128)}, u32[]{:S(2)}, u32[]{:S(2)}) %all-to-all-start.8) | async-done | bytes 1048608 | tf_op jit(solution)/shard_map/all_to_all | solution.py:27
  402.7 4.2 all-to-all-start.9
  407.0 8.3 %convolution_bitcast_fusion = f32[8,6,128,256]{2,3,1,0:T(8,128)} fusion(f32[8,128,256,1]{2,1,3,0:T(8,128)} %bitcast.309, f32[8,6,128,128]{3,2,1,0:T(8,128)S(1)} %copy-done), kind=kOutput, calls=%fused_computation.28 | convolution fusion | flops 2415919104 | bytes 10485760 | tf_op jit(solution)/shard_map/akij,aiw->akjw/dot_general | solution.py:15
  415.3 6.6 %copy.118 = f32[8,6,128,256]{3,0,1,2:T(8,128)} copy(f32[8,6,128,256]{2,3,1,0:T(8,128)} %convolution_bitcast_fusion) | data formatting | bytes 12582912 | tf_op jit(solution)/shard_map/akij,aiw->akjw/dot_general | solution.py:15
  422.0 4.9 gather_fusion.10
  426.8 8.0 %convolution_bitcast_fusion.1 = f32[8,128,256]{2,0,1:T(8,128)} fusion(f32[8,6,128,256]{3,0,1,2:T(8,128)} %copy.118, s32[8,6]{0,1:T(8,128)S(1)} %copy.90), kind=kOutput, calls=%fused_computation.68 | convolution fusion | flops 150995328 | bytes 7340224 | tf_op jit(solution)/shard_map/akc,akjw->cjw/dot_general | solution.py:18
  434.8 3.1 fusion.125
  444.1 3.2 fusion.64
  447.3 3.4 fusion.121
  453.7 3.3 gather_fusion.12
  457.0 4.3 fusion.43
  461.4 3.3 gather_fusion.14
  464.6 4.3 fusion.46
  469.0 3.3 gather_fusion.16
  472.3 3.5 fusion.49
  475.9 11.7 %fusion.118 = f32[8,128,256]{2,1,0:T(8,128)S(1)} fusion(f32[8,128,256]{2,1,0:T(8,128)S(1)} %fusion.49, f32[8,128,256]{2,1,0:T(8,128)S(1)} %copy-done.18, f32[8,128,256]{2,1,0:T(8,128)S(1)} %copy-done.17, f32[8,6,128,128]{3,2,1,0:T(8,128)S(1)} %copy-done, f32[8,6,128,256]{3,2,1,0:T(8,128)} %bitcast.314, pred[8,6]{1,0:T(8,128)(4,1)S(1)} %compare_and_fusion, ...), kind=kOutput, calls=%fused_computation.82 | convolution fusion | flops 2419326976 | bytes 17825840 | tf_op jit(solution)/shard_map/akij,akjw->aiw/dot_general | solution.py:11
  487.8 6.3 %fusion.154 = f32[1024,1024]{1,0:T(8,128)} fusion(f32[1024,256]{1,0:T(8,128)S(1)} %fusion.134, f32[1024,1024]{1,0:T(8,128)} %param.23, s32[]{:T(128)S(6)} %select_n.58), kind=kOutput, calls=%fused_computation.130 | convolution fusion | flops 3221225472 | bytes 6291460 | tf_op jit(solution)/shard_map/dot_general | solution.py:90
  494.2 45.9 %reduce-scatter.2.cloned.1.call-done = f32[1024,256]{1,0:T(8,128)} async-done(((f32[1024,1024]{1,0:T(8,128)}), f32[1024,256]{1,0:T(8,128)}) %reduce-scatter.2.cloned.1.call-update) | async-done | bytes 1048592 | tf_op jit(solution)/shard_map/reduce_scatter | solution.py:91
  (117 shorter events, 67.7 us)
Async XLA Ops:
  6.5 219.6 %copy-start = (f32[8,6,128,128]{3,2,1,0:T(8,128)S(1)}, f32[8,6,128,128]{3,2,1,0:T(8,128)}, u32[]{:S(2)}) copy-start(f32[8,6,128,128]{3,2,1,0:T(8,128)} %param.17) | copy-start | bytes 9437188
  6.5 7.5 %copy-start.24 = (s32[3,8]{1,0:T(4,128)S(1)}, s32[3,8]{1,0:T(4,128)}, u32[]{:S(2)}) copy-start(s32[3,8]{1,0:T(4,128)} %param.21) | copy-start | bytes 292
  6.5 33.4 %all-to-all-start = ((f32[1,8,128,256]{3,2,0,1:T(8,128)}), f32[1,8,128,256]{3,2,0,1:T(8,128)}, u32[]{:S(2)}, u32[]{:S(2)}) async-start(f32[1,8,128,256]{3,2,0,1:T(8,128)} %bitcast.305), calls=%async_computation | async-start | bytes 2097152 | tf_op jit(solution)/shard_map/all_to_all | solution.py:25
  45.2 29.9 %all-to-all-start.1 = ((f32[1,8,128,256]{3,2,0,1:T(8,128)}), f32[1,8,128,256]{3,2,0,1:T(8,128)}, u32[]{:S(2)}, u32[]{:S(2)}) async-start(f32[1,8,128,256]{3,2,0,1:T(8,128)} %fusion.147), calls=%async_computation.1 | async-start | bytes 2097152 | tf_op jit(solution)/shard_map/all_to_all | solution.py:27
  75.0 29.7 %all-to-all-start.4 = ((f32[1,8,128,256]{3,2,0,1:T(8,128)}), f32[1,8,128,256]{3,2,0,1:T(8,128)}, u32[]{:S(2)}, u32[]{:S(2)}) async-start(f32[1,8,128,256]{3,2,0,1:T(8,128)} %fusion.144), calls=%async_computation.4 | async-start | bytes 2097152 | tf_op jit(solution)/shard_map/all_to_all | solution.py:27
  104.7 74.4 %all-to-all-start.2 = ((f32[3,8,256,128]{3,2,0,1:T(8,128)}), f32[3,8,256,128]{3,2,0,1:T(8,128)}, u32[]{:S(2)}, u32[]{:S(2)}) async-start(f32[3,8,256,128]{3,2,0,1:T(8,128)} %bitcast.318), calls=%async_computation.2 | async-start | bytes 6291456 | tf_op jit(solution)/shard_map/all_to_all | solution.py:35
  179.1 29.9 %all-to-all-start.5 = ((f32[1,8,128,256]{3,2,0,1:T(8,128)}), f32[1,8,128,256]{3,2,0,1:T(8,128)}, u32[]{:S(2)}, u32[]{:S(2)}) async-start(f32[1,8,128,256]{3,2,0,1:T(8,128)} %fusion.141), calls=%async_computation.5 | async-start | bytes 2097152 | tf_op jit(solution)/shard_map/all_to_all | solution.py:27
  195.4 1.5 copy-start.19
  195.4 1.9 copy-start.20
  199.8 16.4 %copy-start.25 = (f32[3]{0:T(128)S(1)}, f32[3]{0:T(128)}, u32[]{:S(2)}) copy-start(f32[3]{0:T(128)} %param.22) | copy-start | bytes 40
  199.8 19.6 %copy-start.23 = (s32[3,64,2]{1,2,0:T(2,128)S(1)}, s32[3,64,2]{1,2,0:T(2,128)}, u32[]{:S(2)}) copy-start(s32[3,64,2]{1,2,0:T(2,128)} %param.20) | copy-start | bytes 4612
  199.8 20.5 %copy-start.22 = (s32[8,6]{1,0:T(8,128)S(1)}, s32[8,6]{1,0:T(8,128)}, u32[]{:S(2)}) copy-start(s32[8,6]{1,0:T(8,128)} %param.18) | copy-start | bytes 580
  208.9 74.4 %all-to-all-start.3 = ((f32[3,8,256,128]{3,2,0,1:T(8,128)}), f32[3,8,256,128]{3,2,0,1:T(8,128)}, u32[]{:S(2)}, u32[]{:S(2)}) async-start(f32[3,8,256,128]{3,2,0,1:T(8,128)} %copy.98), calls=%async_computation.3 | async-start | bytes 6291456 | tf_op jit(solution)/shard_map/all_to_all | solution.py:39
  251.4 4.5 copy-start.5
  255.9 4.3 copy-start.11
  285.4 4.0 copy-start.9
  285.4 6.0 %copy-start.7 = (f32[1,8,256,128]{3,2,0,1:T(8,128)}, f32[1,8,256,128]{3,2,0,1:T(8,128)S(1)}, u32[]{:S(2)}) copy-start(f32[1,8,256,128]{3,2,0,1:T(8,128)S(1)} %get-tuple-element.22) | copy-start | bytes 3145732
  285.4 11.3 %copy-start.6 = (f32[1,8,256,128]{3,2,0,1:T(8,128)}, f32[1,8,256,128]{3,2,0,1:T(8,128)S(1)}, u32[]{:S(2)}) copy-start(f32[1,8,256,128]{3,2,0,1:T(8,128)S(1)} %get-tuple-element.23) | copy-start | bytes 3145732
  289.4 12.6 %slice-start = ((s8[6291456]{0:T(1024)(128)(4,1)}), s8[4194304]{0:T(1024)(128)(4,1)S(1)}, s32[]{:S(2)}) async-start(s8[6291456]{0:T(1024)(128)(4,1)} %bitcast.311), calls=%async_computation.12 | async-start | bytes 8388608
  294.8 7.3 %slice-start.1 = ((s8[6291456]{0:T(1024)(128)(4,1)}), s8[2097152]{0:T(1024)(128)(4,1)S(1)}, s32[]{:S(2)}) async-start(s8[6291456]{0:T(1024)(128)(4,1)} %bitcast.311), calls=%async_computation.13 | async-start | bytes 4194304
  296.8 5.3 copy-start.16
  300.0 2.0 copy-start.13
  300.0 2.0 copy-start.14
  300.0 2.0 copy-start.15
  302.1 5.8 %copy-start.1 = (f32[1024,256]{1,0:T(8,128)S(1)}, f32[1024,256]{1,0:T(8,128)}, u32[]{:S(2)}) copy-start(f32[1024,256]{1,0:T(8,128)} %param.16) | copy-start | bytes 3145732
  308.0 1.0 copy-start.3
  343.7 29.4 %all-to-all-start.7 = ((f32[1,8,128,256]{3,2,0,1:T(8,128)}), f32[1,8,128,256]{3,2,0,1:T(8,128)}, u32[]{:S(2)}, u32[]{:S(2)}) async-start(f32[1,8,128,256]{3,2,0,1:T(8,128)} %fusion.137), calls=%async_computation.7 | async-start | bytes 2097152 | tf_op jit(solution)/shard_map/all_to_all | solution.py:27
  373.0 29.6 %all-to-all-start.8 = ((f32[1,8,128,256]{3,2,0,1:T(8,128)}), f32[1,8,128,256]{3,2,0,1:T(8,128)}, u32[]{:S(2)}, u32[]{:S(2)}) async-start(f32[1,8,128,256]{3,2,0,1:T(8,128)} %fusion.136), calls=%async_computation.8 | async-start | bytes 2097152 | tf_op jit(solution)/shard_map/all_to_all | solution.py:27
  402.7 44.6 %all-to-all-start.9 = ((f32[1,8,128,256]{3,2,0,1:T(8,128)}), f32[1,8,128,256]{3,2,0,1:T(8,128)}, u32[]{:S(2)}, u32[]{:S(2)}) async-start(f32[1,8,128,256]{3,2,0,1:T(8,128)} %fusion.135), calls=%async_computation.9 | async-start | bytes 2097152 | tf_op jit(solution)/shard_map/all_to_all | solution.py:27
  406.9 133.2 %reduce-scatter.2.cloned.1.call-start = ((), (), s32[]{:S(2)}) async-start(), calls=%async_computation.11 | async-start | bytes 5242880 | tf_op jit(solution)/shard_map/reduce_scatter | solution.py:91
  426.8 8.0 %copy-start.10 = (f32[1,8,256,128]{3,2,0,1:T(8,128)S(1)}, f32[1,8,256,128]{3,2,0,1:T(8,128)}, u32[]{:S(2)}) copy-start(f32[1,8,256,128]{3,2,0,1:T(8,128)} %copy-done.9) | copy-start | bytes 3145732
  438.0 3.0 copy-start.8
  472.2 3.5 copy-start.12
  472.2 3.6 copy-start.17
  472.2 3.6 copy-start.18
  472.3 3.6 copy-start.21
  475.8 11.7 %copy-start.2 = (f32[1024,256]{1,0:T(8,128)S(1)}, f32[1024,256]{1,0:T(8,128)}, u32[]{:S(2)}) copy-start(f32[1024,256]{1,0:T(8,128)} %param.16) | copy-start | bytes 3145732
  475.8 11.7 %copy-start.4 = (f32[1024,256]{1,0:T(8,128)S(1)}, f32[1024,256]{1,0:T(8,128)}, u32[]{:S(2)}) copy-start(f32[1024,256]{1,0:T(8,128)} %copy-done.3) | copy-start | bytes 3145732
Sparse Core Ops, SparseCore 0:
  494.3 45.7 reduce-scatter.1
where the time goes:
time: 552 us; the launch traced here: 547 us
  waiting for transfers between devices  248 us (45%)
  matrix products  115 us (21%)
  local copies, waits for them, and re-layouts  76.5 us (14%)
  starting transfers between devices  42.1 us (8%)
  blocking collectives  29.4 us (5%)
  between operations  19.5 us (4%)
  other arithmetic  16.9 us (3%)
    all_to_all x6, waiting for transfers between devices, route_pair(): lax.all_to_all(regrouped, 'rows', split_axis=1, concat_axis=1, tiled=True)  91.1 us
    all_to_all x1, waiting for transfers between devices, route_blocks(): lax.all_to_all(flattened, 'rows', split_axis=1, concat_axis=1, tiled=True)  64.7 us
    reduce_scatter x1, waiting for transfers between devices, local(): lax.psum_scatter(partial_sum, 'bands', scatter_dimension=1, tiled=True)  45.9 us
    dot_general x8, matrix products, forward(): return jnp.einsum('akij,akjw->aiw', blocks, picked, precision=precise)  41.1 us
    dot_general x8, matrix products, backward(): products = jnp.einsum('akij,aiw->akjw', blocks, source, precision=precise)  35.3 us
    dot_general x8, matrix products, backward(): return jnp.einsum('akc,akjw->cjw', onehot, products, precision=precise)  31.9 us
    all_to_all x1, blocking collectives, route_pair(): lax.all_to_all(pieces, 'rows', split_axis=1, concat_axis=1, tiled=True)  29.4 us
    gather x8, local copies, waits for them, and re-layouts, forward(): picked = jnp.take(source, block_cols, axis=0)  29.2 us
  transfers between devices with their start and end apart: 10, of which 9 were waited for; matrix products, arithmetic and copies ran while one was open for 23% of the time, Pallas kernels for 0%

commit v1 on v0

v1 whole, which is shorter than its diff:
```python
import functools

import jax
import jax.numpy as jnp
from jax import lax
from jax.experimental import pallas as pl
from jax.experimental.pallas import tpu as pltpu
from jax.sharding import PartitionSpec as P

f32 = jnp.float32
bf16 = jnp.bfloat16
ANY = pl.BlockSpec(memory_space=pl.ANY)
VMEM = pl.BlockSpec(memory_space=pltpu.VMEM)
SMEM = pl.BlockSpec(memory_space=pltpu.SMEM)
PARAMS = pltpu.CompilerParams(vmem_limit_bytes=44 * 1024 * 1024)


def split(x):
    hi = x.astype(bf16)
    return hi, (x - hi.astype(f32)).astype(bf16)


def dot(a, b):
    return jnp.dot(a, b, preferred_element_type=f32)


def rotate_kernel(pick_ref, own_ref, mate_ref, r_own_ref, r_mate_ref, *outs):
    total = None
    for v_ref, r_ref in ((own_ref, r_own_ref), (mate_ref, r_mate_ref)):
        v_hi, v_lo = split(v_ref[...])
        r_hi, r_lo = split(r_ref[...])
        part = dot(v_hi, r_hi) + dot(v_lo, r_hi) + dot(v_hi, r_lo)
        total = part if total is None else total + part
    halves = len(outs)
    rows = outs[0][0].shape[0] if isinstance(outs[0], tuple) else outs[0].shape[0]
    width = outs[0].shape[1]
    per_col = total.shape[0] // rows
    for n in range(halves):
        c, r = n // per_col, n % per_col
        outs[n][...] = total[r * rows:(r + 1) * rows, c * width:(c + 1) * width]


def rotate(own, mate, rotation, pick, chunk_rows, width):
    rows, band = own.shape
    count = (rows // chunk_rows) * (band // width)
    full = pl.BlockSpec((rows, band), lambda i, p: (0, 0))
    return pl.pallas_call(
        rotate_kernel,
        grid_spec=pltpu.PrefetchScalarGridSpec(
            num_scalar_prefetch=1,
            grid=(1,),
            in_specs=[
                full,
                full,
                pl.BlockSpec((band, band), lambda i, p: (p[0], p[2])),
                pl.BlockSpec((band, band), lambda i, p: (p[1], p[2])),
            ],
            out_specs=[pl.BlockSpec((chunk_rows, width), lambda i, p: (0, 0))] * count,
        ),
        out_shape=[jax.ShapeDtypeStruct((chunk_rows, width), f32)] * count,
        compiler_params=PARAMS,
        cost_estimate=pl.CostEstimate(
            flops=6 * 2 * rows * band * band, bytes_accessed=3 * rows * band * 4, transcendentals=0
        ),
        name="rotate",
    )(pick, own, mate, rotation, rotation)


def write_parts(acc, hi_ref, lo_ref):
    count, _, size, _ = acc.shape

    def one(i, carry):
        for j in range(count):
            hi, lo = split(acc[i, j])
            rows = pl.ds(pl.multiple_of(i * size, size), size)
            hi_ref[rows, j * size:(j + 1) * size] = hi
            lo_ref[rows, j * size:(j + 1) * size] = lo
        return carry

    lax.fori_loop(0, count, one, 0)


def local_kernel(cols_ref, bounds_ref, blocks_ref, hi_ref, lo_ref, acc):
    count, _, size, _ = acc.shape
    stored = blocks_ref.shape[1]
    acc[...] = jnp.zeros_like(acc)
    centre = (bounds_ref[2] + bounds_ref[1]) / 2.0
    eye = lax.broadcasted_iota(jnp.int32, (size, size), 0) == lax.broadcasted_iota(
        jnp.int32, (size, size), 1
    )
    shift = jnp.where(eye, -centre, 0.0).astype(f32)
    for i in range(count):
        acc[i, i] = shift

    def one(a, carry):
        for k in range(stored):
            block = blocks_ref[a, k]
            col = cols_ref[a, k]
            acc[a, col] += block
            acc[col, a] += block.T
        return carry

    lax.fori_loop(0, count, one, 0)
    write_parts(acc, hi_ref, lo_ref)


def build_local(blocks, cols, bounds):
    count, stored, size, _ = blocks.shape
    rows = count * size
    return pl.pallas_call(
        local_kernel,
        in_specs=[SMEM, SMEM, VMEM],
        out_specs=[VMEM, VMEM],
        out_shape=[jax.ShapeDtypeStruct((rows, rows), bf16)] * 2,
        scratch_shapes=[pltpu.VMEM((count, count, size, size), f32)],
        compiler_params=PARAMS,
        cost_estimate=pl.CostEstimate(
            flops=rows * rows, bytes_accessed=rows * rows * 12, transcendentals=0
        ),
        name="build_local",
    )(cols, bounds, blocks)


def couple_kernel(pieces, meta_ref, own_cols_ref, mate_cols_ref, blocks_ref, *rest):
    piece_refs, (hi_ref, lo_ref, acc) = rest[:pieces], rest[pieces:]
    count = acc.shape[0]
    stored = blocks_ref.shape[2]
    acc[...] = jnp.zeros_like(acc)

    def own(a, carry):
        for k in range(stored):
            acc[a, own_cols_ref[a, k]] += blocks_ref[0, a, k]
        return carry

    lax.fori_loop(0, count, own, 0)
    for n, piece in enumerate(piece_refs):
        for i in range(piece.shape[0]):
            a = meta_ref[1 + n] + i
            for k in range(stored):
                acc[mate_cols_ref[a, k], a] += piece[i, k].T
    write_parts(acc, hi_ref, lo_ref)


def build_couple(meta, own_cols, mate_cols, coupling_blocks, pieces):
    _, count, stored, size, _ = coupling_blocks.shape
    rows = count * size
    whole = pl.BlockSpec((rows, rows), lambda i, *_: (0, 0))
    return pl.pallas_call(
        functools.partial(couple_kernel, len(pieces)),
        grid_spec=pltpu.PrefetchScalarGridSpec(
            num_scalar_prefetch=3,
            grid=(1,),
            in_specs=[pl.BlockSpec((1, count, stored, size, size), lambda i, m, *_: (m[0], 0, 0, 0, 0))]
            + [pl.BlockSpec(p.shape, lambda i, *_: (0, 0, 0, 0)) for p in pieces],
            out_specs=[whole, whole],
            scratch_shapes=[pltpu.VMEM((count, count, size, size), f32)],
        ),
        out_shape=[jax.ShapeDtypeStruct((rows, rows), bf16)] * 2,
        compiler_params=PARAMS,
        cost_estimate=pl.CostEstimate(
            flops=rows * rows, bytes_accessed=rows * rows * 8, transcendentals=0
        ),
        name="build_couple",
    )(meta, own_cols, mate_cols, coupling_blocks, *pieces)


def apply_kernel(chunk_counts, has_base, column, scale_ref, *refs):
    refs = list(refs)
    mats = []
    for chunks in chunk_counts:
        hi, lo = refs.pop(0), refs.pop(0)
        mats.append((hi, lo, [refs.pop(0) for _ in range(chunks)]))
    base = [refs.pop(0) for _ in range(has_base)]
    if column is not None and column > 0:
        refs.pop(0)
    out_ref, hi_buf, lo_buf, u_buf, base_buf, w_buf, acc, sems, out_sem = refs
    copies = []
    n = 0
    for m, (hi, lo, chunks) in enumerate(mats):
        mine = [(hi, hi_buf.at[m]), (lo, lo_buf.at[m])]
        at = 0
        for chunk in chunks:
            mine.append((chunk, u_buf.at[m, at:at + chunk.shape[0]]))
            at += chunk.shape[0]
        group = []
        for src, dst in mine:
            group.append(pltpu.make_async_copy(src, dst, sems.at[n]))
            n += 1
        copies.append(group)
    base_group = []
    at = 0
    for chunk in base:
        base_group.append(
            pltpu.make_async_copy(chunk, base_buf.at[at:at + chunk.shape[0]], sems.at[n])
        )
        at += chunk.shape[0]
        n += 1
    for group in copies + [base_group]:
        for c in group:
            c.start()
    rows, width = acc.shape
    for m in range(len(mats)):
        for c in copies[m]:
            c.wait()
        u_hi, u_lo = split(u_buf[m])
        w_buf[:, :width] = u_hi
        w_buf[:, width:] = u_lo
        both = dot(hi_buf[m], w_buf[...])
        part = both[:, :width] + both[:, width:] + dot(lo_buf[m], w_buf[:, :width])
        if m == 0:
            acc[...] = part
        else:
            acc[...] += part
    for c in base_group:
        c.wait()
    result = acc[...] * scale_ref[0]
    if base_group:
        result = result + base_buf[...] * scale_ref[1]
    if column is None:
        out_ref[...] = result
    else:
        acc[...] = result
        c = pltpu.make_async_copy(acc, out_ref.at[:, column:column + width], out_sem)
        c.start()
        c.wait()


def apply(mats, scale, base=(), column=None, out_width=None, into=None):
    rows = mats[0][0].shape[0]
    width = mats[0][2][0].shape[1]
    operands = [scale]
    specs = [SMEM]
    for hi, lo, chunks in mats:
        operands += [hi, lo, *chunks]
        specs += [ANY] * (2 + len(chunks))
    operands += list(base)
    specs += [ANY] * len(base)
    aliases = {}
    if into is not None:
        aliases = {len(operands): 0}
        operands.append(into)
        specs.append(ANY)
    count = len(mats)
    sem_count = sum(2 + len(m[2]) for m in mats) + max(1, len(base))
    shape = (rows, width if column is None else out_width)
    return pl.pallas_call(
        functools.partial(apply_kernel, [len(m[2]) for m in mats], len(base), column),
        in_specs=specs,
        out_specs=VMEM if column is None else ANY,
        out_shape=jax.ShapeDtypeStruct(shape, f32),
        scratch_shapes=[
            pltpu.VMEM((count, rows, rows), bf16),
            pltpu.VMEM((count, rows, rows), bf16),
            pltpu.VMEM((count, rows, width), f32),
            pltpu.VMEM((rows, width), f32),
            pltpu.VMEM((rows, 2 * width), bf16),
            pltpu.VMEM((rows, width), f32),
            pltpu.SemaphoreType.DMA((sem_count,)),
            pltpu.SemaphoreType.DMA,
        ],
        input_output_aliases=aliases,
        compiler_params=PARAMS,
        cost_estimate=pl.CostEstimate(
            flops=count * 6 * rows * rows * width,
            bytes_accessed=count * rows * (rows * 4 + width * 4),
            transcendentals=0,
        ),
        name="apply",
    )(*operands)


def local(
    n_rows, n_bands,
    vectors, local_blocks, local_cols, coupling_blocks, coupling_cols, partners, bounds, rotation
):
    rows, band = vectors.shape
    colours, block_count, stored, size, _ = coupling_blocks.shape
    half = band // 2
    part_rows = rows // 2
    my_row = lax.axis_index("rows")
    my_band = lax.axis_index("bands")
    bits = n_rows.bit_length() - 1
    static = bits == colours
    masks = partners[:, 0]
    slots = range(colours)
    if static:
        colour_of = [
            sum(jnp.where(masks[c] == (1 << k), c, 0) for c in range(colours)).astype(jnp.int32)
            for k in slots
        ]
    else:
        colour_of = [jnp.int32(k) for k in slots]

    def to_band(x, mask):
        return lax.ppermute(x, "bands", [(i, i ^ mask) for i in range(n_bands)])

    def to_row(x, bit):
        return lax.ppermute(x, "rows", [(i, i ^ (1 << bit)) for i in range(n_rows)])

    def exchange(x, slot):
        if static:
            return to_row(x, slot)
        taken = jnp.zeros_like(x)
        for bit in range(bits):
            taken = jnp.where(masks[slot] == (1 << bit), to_row(x, bit), taken)
        return taken

    share = block_count // n_bands
    couple_parts = []
    near = [k for k in slots if static and k == 0]
    for k in slots:
        if k in near:
            count, first = block_count // 2, (my_band % 2) * (block_count // 2)
        else:
            count, first = share, my_band * share
        mine = lax.dynamic_slice(
            coupling_blocks,
            (colour_of[k], first, 0, 0, 0),
            (1, count, stored, size, size),
        )[0]
        couple_parts.append(exchange(mine, k))

    chip_mate = to_band(vectors, 1)

    others = list(range(2, n_bands, 2))

    def rotated_for(mask):
        pick = jnp.stack([my_band, my_band ^ 1, my_band ^ mask]).astype(jnp.int32)
        return rotate(vectors, chip_mate, rotation, pick, part_rows, half)

    sums = [[to_band(c, mask) for c in rotated_for(mask)] for mask in others]
    own = rotated_for(0)
    chunks = []
    for n, c in enumerate(own):
        for other in sums:
            c = c + other[n]
        chunks.append(c)
    per = rows // part_rows
    field = [chunks[h * per:(h + 1) * per] for h in range(band // half)]

    def send(parts):
        return [[exchange(c, k) for c in parts] for k in slots]

    arrived = [send(parts) for parts in field]

    far = [k for k in slots if k not in near]
    gathered = {k: [] for k in slots}
    firsts = {k: [] for k in slots}
    for k in near:
        gathered[k] = [couple_parts[k], to_band(couple_parts[k], 1)]
        firsts[k] = [(my_band % 2) * (block_count // 2), (1 - my_band % 2) * (block_count // 2)]
    joined = jnp.concatenate([couple_parts[k] for k in far], axis=0)
    for mask in range(0, n_bands, 2):
        here = joined if mask == 0 else to_band(joined, mask)
        there = to_band(here, 1)
        for which, got in ((mask, here), (mask ^ 1, there)):
            for n, k in enumerate(far):
                gathered[k].append(got[n * share:(n + 1) * share])
                firsts[k].append((my_band ^ which) * share)

    local_parts = build_local(local_blocks, local_cols, bounds)
    couple_mats = []
    for k in slots:
        if static:
            mate = my_row ^ (1 << k)
        else:
            mate = my_row ^ masks[k]
        cols = lax.dynamic_index_in_dim(coupling_cols, colour_of[k], 0, keepdims=False)
        own_cols = lax.dynamic_slice_in_dim(cols, my_row * block_count, block_count, 0)
        mate_cols = lax.dynamic_slice_in_dim(cols, mate * block_count, block_count, 0)
        meta = jnp.stack([colour_of[k], *firsts[k]]).astype(jnp.int32)
        couple_mats.append(build_couple(meta, own_cols, mate_cols, coupling_blocks, gathered[k]))

    lowest, lower, upper = (bounds[0], bounds[1], bounds[2])
    half_width = (upper - lower) / 2.0
    centre = (upper + lower) / 2.0
    sigma_one = half_width / (lowest - centre)
    sigma_two = 1.0 / (2.0 / sigma_one - sigma_one)
    scale_one = jnp.stack([sigma_one / half_width, jnp.zeros((), f32)])
    scale_two = jnp.stack([2.0 * sigma_two / half_width, -sigma_one * sigma_two])

    def terms(mine, theirs):
        return [(*local_parts, mine)] + [(*couple_mats[k], theirs[k]) for k in slots]

    first = [[apply(terms(field[h], arrived[h]), scale_one)] for h in range(2)]
    arrived = [send(parts) for parts in first]
    out = apply(terms(first[0], arrived[0]), scale_two, field[0], 0, band)
    return apply(terms(first[1], arrived[1]), scale_two, field[1], half, band, out)


def solution(mesh):
    in_specs = (
        P("rows", "bands"),
        P("rows", None, None, None),
        P("rows", None),
        P(None, "rows", None, None, None),
        P(),
        P(),
        P(),
        P(),
    )
    body = functools.partial(local, mesh.shape["rows"], mesh.shape["bands"])
    return jax.shard_map(
        body, mesh=mesh, in_specs=in_specs, out_specs=P("rows", "bands"), check_vma=False
    )
```

time: 552 us -> 167 us (0.30)
  waiting for transfers between devices: 248 us -> 43.7 us
  matrix products: 115 us -> 0 us
  Pallas kernels: 0 us -> 47.9 us
  local copies, waits for them, and re-layouts: 76.5 us -> 29 us
  blocking collectives: 29.4 us -> 0 us
  other arithmetic: 16.9 us -> 1.58 us
  between operations: 19.5 us -> 7.6 us
    all_to_all x9 -> x0, waiting for transfers between devices: 202 us -> none  [the longest x6 91.1 us: route_pair(): lax.all_to_all(regrouped, 'rows', split_axis=1, concat_axis=1, tiled=True)]
    dot_general x25 -> x0, matrix products: 115 us -> none  [the longest x8 41.1 us: forward(): return jnp.einsum('akij,akjw->aiw', blocks, picked, precision=precise)]
    gather x17 -> x0, local copies, waits for them, and re-layouts: 54.5 us -> none  [the longest x8 29.2 us: forward(): picked = jnp.take(source, block_cols, axis=0)]
    pallas_call x0 -> x10, Pallas kernels: none -> 47.9 us  [the longest x4 31.7 us: apply(): pl.pallas_call(functools.partial(apply_kernel, [len(m[2]) for m in mats],...]
    reduce_scatter x1 -> x0, waiting for transfers between devices: 45.9 us -> none  [local(): lax.psum_scatter(partial_sum, 'bands', scatter_dimension=1, tiled=True)]
    ppermute x0 -> x30, waiting for transfers between devices: none -> 43.7 us  [the longest x21 33 us: to_row(): return lax.ppermute(x, 'rows', [(i, i ^ 1 << bit) for i in range(n_rows)])]
    all_to_all x9 -> x0, starting transfers between devices: 42.1 us -> none  [the longest x6 25.4 us: route_pair(): lax.all_to_all(regrouped, 'rows', split_axis=1, concat_axis=1, tiled=True)]
    ppermute x0 -> x30, starting transfers between devices: none -> 37 us  [the longest x21 30.7 us: to_row(): return lax.ppermute(x, 'rows', [(i, i ^ 1 << bit) for i in range(n_rows)])]
  transfers between devices with their start and end apart: 10 -> 30, of which waited for: 9 -> 10; matrix products, arithmetic and copies ran while one was open for 23% -> 7% of each run, Pallas kernels for 0% -> 24%
where the time goes in v1:
time: 167 us
  Pallas kernels  47.9 us (29%)
  waiting for transfers between devices  43.7 us (26%)
  starting transfers between devices  37 us (22%)
  local copies, waits for them, and re-layouts  29 us (17%)
  between operations  7.6 us (5%)
    ppermute x21, waiting for transfers between devices, to_row(): return lax.ppermute(x, 'rows', [(i, i ^ 1 << bit) for i in range(n_rows)])  33 us
    pallas_call x4, Pallas kernels, apply(): pl.pallas_call(functools.partial(apply_kernel, [len(m[2]) for m in mats],...  31.7 us
    ppermute x21, starting transfers between devices, to_row(): return lax.ppermute(x, 'rows', [(i, i ^ 1 << bit) for i in range(n_rows)])  30.7 us
    unnamed x63, local copies, waits for them, and re-layouts  18.9 us
    ppermute x9, waiting for transfers between devices, to_band(): return lax.ppermute(x, 'bands', [(i, i ^ mask) for i in range(n_bands)])  10.6 us
    pallas_call x3, Pallas kernels, build_couple(): pl.pallas_call(functools.partial(couple_kernel, len(pieces)), grid_spec=p...  8.78 us
    ppermute x9, starting transfers between devices, to_band(): return lax.ppermute(x, 'bands', [(i, i ^ mask) for i in range(n_bands)])  6.27 us
    pallas_call x2, Pallas kernels, rotate(): pl.pallas_call(rotate_kernel, grid_spec=pltpu.PrefetchScalarGridSpec(num_...  3.87 us
  transfers between devices with their start and end apart: 30, of which 10 were waited for; matrix products, arithmetic and copies ran while one was open for 7% of the time, Pallas kernels for 24%

profile of v1, /device:TPU:0, one launch (start us, length us, event | category | flops | bytes accessed | tf_op | source)
XLA Modules:
  0.0 166.8 jit_solution(14798917000393291581)
XLA Ops:
  0.5 1.3 fusion.9
  4.2 1.8 %dynamic-slice_bitcast_fusion.1 = (f32[2,2,128,128]{3,2,1,0:T(8,128)S(1)}, f32[2,2,128,128]{3,2,1,0:T(8,128)}) fusion(f32[3,8,2,128,128]{4,3,2,1,0:T(8,128)} %blocks_ref.7, s32[]{:T(128)S(6)} %select_n.106, s32[]{:T(128)S(6)} %select_n.103, s32[]{:T(128)S(6)} %select_n.99), kind=kLoop, calls=%fused_computation.1 | loop fusion | bytes 1048588 | tf_op jit(solution)/shard_map/squeeze | solution.py:316
  6.0 2.6 %collective-permute-start.7 = (f32[2,2,128,128]{3,2,1,0:T(8,128)}, f32[2,2,128,128]{3,2,1,0:T(8,128)S(1)}, u32[]{:S(2)}, u32[]{:S(2)}) collective-permute-start(f32[2,2,128,128]{3,2,1,0:T(8,128)} %get-tuple-element.38), channel_id=1, source_target_pairs={{0,8},{4,12},{8,0},{12,4},{16,24},{20,28},{24,16},{28,20},{1,9},{5... | collective-permute-start | bytes 786440 | tf_op jit(solution)/shard_map/ppermute | solution.py:298
  8.6 2.6 %collective-permute-start.8 = (f32[2,2,128,128]{3,2,1,0:T(8,128)S(1)}, f32[2,2,128,128]{3,2,1,0:T(8,128)S(1)}, u32[]{:S(2)}, u32[]{:S(2)}) collective-permute-start(f32[2,2,128,128]{3,2,1,0:T(8,128)S(1)} %get-tuple-element.37), channel_id=1, source_target_pairs={{0,16},{4,20},{8,24},{12,28},{16,0},{20,4},{24,8},{28,12},{1,17},{... | collective-permute-start | bytes 786440 | tf_op jit(solution)/shard_map/ppermute | solution.py:298
  13.5 1.6 collective-permute-start.3
  15.1 6.3 %collective-permute-done.7.rest_0_ = f32[2,2,128,128]{3,2,1,0:T(8,128)S(1)} collective-permute-done((f32[2,2,128,128]{3,2,1,0:T(8,128)}, f32[2,2,128,128]{3,2,1,0:T(8,128)S(1)}, u32[]{:S(2)}, u32[]{:S(2)}) %collective-permute-start.7) | collective-permute-done | bytes 262176 | tf_op jit(solution)/shard_map/ppermute | solution.py:298
  22.8 1.7 collective-permute-start.10
  24.6 2.2 %copy-done = f32[1024,1024]{1,0:T(8,128)S(1)} copy-done((f32[1024,1024]{1,0:T(8,128)S(1)}, f32[1024,1024]{1,0:T(8,128)}, u32[]{:S(2)}) %copy-start) | copy-done | bytes 4194328
  26.8 2.3 %rotate.3 = (f32[512,128]{1,0:T(8,128)S(1)}, f32[512,128]{1,0:T(8,128)}, f32[512,128]{1,0:T(8,128)}, f32[512,128]{1,0:T(8,128)}) custom-call(s32[3]{0:T(128)S(1)} %get-tuple-element.57.pick_ref, f32[1024,256]{1,0:T(8,128)S(1)} %copy-done.12, f32[1024,256]{1,0:T(8,128)S(1)} %collective-permute-done.mate_ref, f32[1024,1024]{1,0:T(8,128)S(1)} %copy-done, ...), custom_call_target="tpu_custom_call" | custom-call | flops 805306368 | bytes 3145728 | tf_op jit(solution)/shard_map/rotate/pallas_call | solution.py:47
  33.4 1.7 %collective-permute-start.20 = (f32[512,128]{1,0:T(8,128)}, f32[512,128]{1,0:T(8,128)S(1)}, u32[]{:S(2)}, u32[]{:S(2)}) collective-permute-start(f32[512,128]{1,0:T(8,128)} %get-tuple-element.36), channel_id=1, source_target_pairs={{0,2},{1,3},{2,0},{3,1},{4,6},{5,7},{6,4},{7,5},{8,10},{9,11},{10,... | collective-permute-start | bytes 786440 | tf_op jit(solution)/shard_map/ppermute | solution.py:295
  35.5 2.4 %collective-permute-done.10 = f32[4,2,128,128]{3,2,1,0:T(8,128)} collective-permute-done((f32[4,2,128,128]{3,2,1,0:T(8,128)}, f32[4,2,128,128]{3,2,1,0:T(8,128)}, u32[]{:S(2)}, u32[]{:S(2)}) %collective-permute-start.10) | collective-permute-done | bytes 524320 | tf_op jit(solution)/shard_map/ppermute | solution.py:295
  37.9 5.5 %collective-permute-done.19 = f32[512,128]{1,0:T(8,128)S(1)} collective-permute-done((f32[512,128]{1,0:T(8,128)S(1)}, f32[512,128]{1,0:T(8,128)S(1)}, u32[]{:S(2)}, u32[]{:S(2)}) %collective-permute-start.19) | collective-permute-done | bytes 262176 | tf_op jit(solution)/shard_map/ppermute | solution.py:295
  44.2 2.2 %copy-done.1 = f32[1024,1024]{1,0:T(8,128)S(1)} copy-done((f32[1024,1024]{1,0:T(8,128)S(1)}, f32[1024,1024]{1,0:T(8,128)}, u32[]{:S(2)}) %copy-start.1) | copy-done | bytes 4194328
  46.4 1.5 rotate.2
  49.1 1.7 %collective-permute-start.2 = (f32[512,128]{1,0:T(8,128)}, f32[512,128]{1,0:T(8,128)}, u32[]{:S(2)}, u32[]{:S(2)}) collective-permute-start(f32[512,128]{1,0:T(8,128)} %get-tuple-element.26), channel_id=1, source_target_pairs={{0,2},{1,3},{2,0},{3,1},{4,6},{5,7},{6,4},{7,5},{8,10},{9,11},{10,... | collective-permute-start | bytes 786440 | tf_op jit(solution)/shard_map/ppermute | solution.py:295
  50.8 1.6 collective-permute-start.21
  52.4 2.3 %collective-permute-done.1 = f32[512,128]{1,0:T(8,128)S(1)} collective-permute-done((f32[512,128]{1,0:T(8,128)}, f32[512,128]{1,0:T(8,128)S(1)}, u32[]{:S(2)}, u32[]{:S(2)}) %collective-permute-start.1) | collective-permute-done | bytes 262176 | tf_op jit(solution)/shard_map/ppermute | solution.py:295
  54.7 1.7 %collective-permute-start.22 = (f32[512,128]{1,0:T(8,128)S(1)}, f32[512,128]{1,0:T(8,128)}, u32[]{:S(2)}, u32[]{:S(2)}) collective-permute-start(f32[512,128]{1,0:T(8,128)S(1)} %add.115.refs_3_.refs_13_), channel_id=1, source_target_pairs={{0,4},{4,0},{8,12},{12,8},{16,20},{20,16},{24,28},{28,24},{1,5},{5... | collective-permute-start | bytes 786440 | tf_op jit(solution)/shard_map/ppermute | solution.py:298
  57.1 1.9 %copy-done.13 = f32[8,6,128,128]{3,2,1,0:T(8,128)S(1)} copy-done((f32[8,6,128,128]{3,2,1,0:T(8,128)S(1)}, f32[8,6,128,128]{3,2,1,0:T(8,128)}, u32[]{:S(2)}) %copy-start.13) | copy-done | bytes 3145752
  59.0 3.5 %build_local.1 = (bf16[1024,1024]{1,0:T(8,128)(2,1)S(1)}, bf16[1024,1024]{1,0:T(8,128)(2,1)S(1)}) custom-call(s32[8,6]{1,0:T(8,128)S(1)} %copy-done.25, f32[3]{0:T(128)S(1)} %copy-done.24, f32[8,6,128,128]{3,2,1,0:T(8,128)S(1)} %copy-done.13), custom_call_target="tpu_custom_call" | custom-call | flops 1048576 | bytes 12582912 | tf_op jit(solution)/shard_map/build_local/pallas_call | solution.py:110
  62.6 1.4 fusion.7
  64.1 1.9 %collective-permute-start.23 = (f32[512,128]{1,0:T(8,128)S(1)}, f32[512,128]{1,0:T(8,128)S(1)}, u32[]{:S(2)}, u32[]{:S(2)}) collective-permute-start(f32[512,128]{1,0:T(8,128)S(1)} %add.114.refs_2_.refs_12_), channel_id=1, source_target_pairs={{0,8},{4,12},{8,0},{12,4},{16,24},{20,28},{24,16},{28,20},{1,9},{5... | collective-permute-start | bytes 786440 | tf_op jit(solution)/shard_map/ppermute | solution.py:298
  66.2 2.3 %collective-permute-start.25 = (f32[512,128]{1,0:T(8,128)S(1)}, f32[512,128]{1,0:T(8,128)S(1)}, u32[]{:S(2)}, u32[]{:S(2)}) collective-permute-start(f32[512,128]{1,0:T(8,128)S(1)} %add.114.refs_2_.refs_12_), channel_id=1, source_target_pairs={{0,16},{4,20},{8,24},{12,28},{16,0},{20,4},{24,8},{28,12},{1,17},{... | collective-permute-start | bytes 786440 | tf_op jit(solution)/shard_map/ppermute | solution.py:298
  69.2 1.8 %collective-permute-start.12 = (f32[512,128]{1,0:T(8,128)S(1)}, f32[512,128]{1,0:T(8,128)S(1)}, u32[]{:S(2)}, u32[]{:S(2)}) collective-permute-start(f32[512,128]{1,0:T(8,128)S(1)} %add.96.refs_2_.refs_12_), channel_id=1, source_target_pairs={{0,8},{4,12},{8,0},{12,4},{16,24},{20,28},{24,16},{28,20},{1,9},{5... | collective-permute-start | bytes 786440 | tf_op jit(solution)/shard_map/ppermute | solution.py:298
  72.1 3.7 %build_couple.3 = (bf16[1024,1024]{1,0:T(8,128)(2,1)S(1)}, bf16[1024,1024]{1,0:T(8,128)(2,1)S(1)}) custom-call(s32[3]{0:T(128)S(1)} %pad_add_fusion.3.meta_ref, s32[8,2]{1,0:T(8,128)S(1)} %copy.10.own_cols_ref, s32[8,2]{1,0:T(8,128)S(1)} %copy.11.mate_cols_ref, f32[3,8,2,128,128]{4,3,2,1,0:T(8,128)S(1)} %copy-done.2, ...), custom_call_target="tpu_custom_call" | custom-call | flops 1048576 | bytes 8388608 | tf_op jit(solution)/shard_map/build_couple/pallas_call | solution.py:148
  75.9 1.2 add.97.refs_3_.refs_13_
  77.0 1.4 fusion.6
  78.4 2.5 %build_couple.4 = (bf16[1024,1024]{1,0:T(8,128)(2,1)S(1)}, bf16[1024,1024]{1,0:T(8,128)(2,1)S(1)}) custom-call(s32[5]{0:T(128)S(1)} %stack.92.meta_ref, s32[8,2]{1,0:T(8,128)S(1)} %copy.12.own_cols_ref, s32[8,2]{1,0:T(8,128)S(1)} %copy.13.mate_cols_ref, f32[3,8,2,128,128]{4,3,2,1,0:T(8,128)S(1)} %copy-done.2, f32[2,2,128,128]{3,2,1,0:T(8,128)S(1)} %copy-done.15, ...), custom_call_target="tpu_custom_call" | custom-call | flops 1048576 | bytes 8388608 | tf_op jit(solution)/shard_map/build_couple/pallas_call | solution.py:148
  81.0 1.3 copy-done.8
  82.3 1.4 copy-done.9
  83.7 2.5 %build_couple.5 = (bf16[1024,1024]{1,0:T(8,128)(2,1)S(1)}, bf16[1024,1024]{1,0:T(8,128)(2,1)S(1)}) custom-call(s32[5]{0:T(128)S(1)} %stack.94.meta_ref, s32[8,2]{1,0:T(8,128)S(1)} %copy.14.own_cols_ref, s32[8,2]{1,0:T(8,128)S(1)} %copy.15.mate_cols_ref, f32[3,8,2,128,128]{4,3,2,1,0:T(8,128)S(1)} %copy-done.2, ...), custom_call_target="tpu_custom_call" | custom-call | flops 1048576 | bytes 8388608 | tf_op jit(solution)/shard_map/build_couple/pallas_call | solution.py:148
  86.3 1.3 copy-done.10
  87.6 1.4 copy-done.11
  89.0 2.4 %collective-permute-start.14 = (f32[512,128]{1,0:T(8,128)S(1)}, f32[512,128]{1,0:T(8,128)S(1)}, u32[]{:S(2)}, u32[]{:S(2)}) collective-permute-start(f32[512,128]{1,0:T(8,128)S(1)} %add.96.refs_2_.refs_12_), channel_id=1, source_target_pairs={{0,16},{4,20},{8,24},{12,28},{16,0},{20,4},{24,8},{28,12},{1,17},{... | collective-permute-start | bytes 786440 | tf_op jit(solution)/shard_map/ppermute | solution.py:298
  91.5 2.1 %collective-permute-start.15 = (f32[512,128]{1,0:T(8,128)S(1)}, f32[512,128]{1,0:T(8,128)S(1)}, u32[]{:S(2)}, u32[]{:S(2)}) collective-permute-start(f32[512,128]{1,0:T(8,128)S(1)} %add.97.refs_3_.refs_13_), channel_id=1, source_target_pairs={{0,16},{4,20},{8,24},{12,28},{16,0},{20,4},{24,8},{28,12},{1,17},{... | collective-permute-start | bytes 786440 | tf_op jit(solution)/shard_map/ppermute | solution.py:298
  94.6 6.4 %collective-permute-done.12.refs_10_ = f32[512,128]{1,0:T(8,128)S(1)} collective-permute-done((f32[512,128]{1,0:T(8,128)S(1)}, f32[512,128]{1,0:T(8,128)S(1)}, u32[]{:S(2)}, u32[]{:S(2)}) %collective-permute-start.12) | collective-permute-done | bytes 262176 | tf_op jit(solution)/shard_map/ppermute | solution.py:298
  102.2 7.6 %apply.5.refs_2_ = f32[1024,128]{1,0:T(8,128)} custom-call(f32[2]{0:T(128)S(1)} %pad_maximum_fusion.1.scale_ref, bf16[1024,1024]{1,0:T(8,128)(2,1)S(1)} %get-tuple-element.21.refs_0_, bf16[1024,1024]{1,0:T(8,128)(2,1)S(1)} %get-tuple-element.22.refs_1_, f32[512,128]{1,0:T(8,128)S(1)} %add.114.refs_2_.refs_12_, f32[512,128]{1,0:T(8,128)S(1)} %add.115.refs_3_.refs_13_, ...), custom_call_target="tpu_custom_call" | custom-call | flops 3221225472 | bytes 18874368 | tf_op jit(solution)/shard_map/apply/pallas_call | solution.py:246
  110.7 1.4 collective-permute-done.15.refs_15_
  112.2 3.4 %collective-permute-start.29 = (f32[1024,128]{1,0:T(8,128)}, f32[1024,128]{1,0:T(8,128)}, u32[]{:S(2)}, u32[]{:S(2)}) collective-permute-start(f32[1024,128]{1,0:T(8,128)} %apply.5.refs_2_), channel_id=1, source_target_pairs={{0,16},{4,20},{8,24},{12,28},{16,0},{20,4},{24,8},{28,12},{1,17},{... | collective-permute-start | bytes 1572872 | tf_op jit(solution)/shard_map/ppermute | solution.py:298
  115.6 7.7 %apply.4.refs_2_ = f32[1024,128]{1,0:T(8,128)} custom-call(f32[2]{0:T(128)S(1)} %pad_maximum_fusion.1.scale_ref, bf16[1024,1024]{1,0:T(8,128)(2,1)S(1)} %get-tuple-element.21.refs_0_, bf16[1024,1024]{1,0:T(8,128)(2,1)S(1)} %get-tuple-element.22.refs_1_, f32[512,128]{1,0:T(8,128)S(1)} %add.96.refs_2_.refs_12_, f32[512,128]{1,0:T(8,128)S(1)} %add.97.refs_3_.refs_13_, ...), custom_call_target="tpu_custom_call" | custom-call | flops 3221225472 | bytes 18874368 | tf_op jit(solution)/shard_map/apply/pallas_call | solution.py:246
  124.8 2.0 %collective-permute-start.18 = (f32[1024,128]{1,0:T(8,128)}, f32[1024,128]{1,0:T(8,128)}, u32[]{:S(2)}, u32[]{:S(2)}) collective-permute-start(f32[1024,128]{1,0:T(8,128)} %apply.4.refs_2_), channel_id=1, source_target_pairs={{0,16},{4,20},{8,24},{12,28},{16,0},{20,4},{24,8},{28,12},{1,17},{... | collective-permute-start | bytes 1572872 | tf_op jit(solution)/shard_map/ppermute | solution.py:298
  127.0 11.8 %collective-permute-done.28.refs_8_ = f32[1024,128]{1,0:T(8,128)} collective-permute-done((f32[1024,128]{1,0:T(8,128)}, f32[1024,128]{1,0:T(8,128)}, u32[]{:S(2)}, u32[]{:S(2)}) %collective-permute-start.28) | collective-permute-done | bytes 524320 | tf_op jit(solution)/shard_map/ppermute | solution.py:298
  138.9 1.2 collective-permute-done.29.refs_11_
  140.0 1.6 copy-done.4
  141.6 1.6 copy-done.6
  144.2 8.2 %apply.6.refs_14_ = f32[1024,256]{1,0:T(8,128)} custom-call(f32[2]{0:T(128)S(1)} %pad_maximum_fusion.scale_ref, bf16[1024,1024]{1,0:T(8,128)(2,1)S(1)} %get-tuple-element.21.refs_0_, bf16[1024,1024]{1,0:T(8,128)(2,1)S(1)} %copy-done.4, f32[1024,128]{1,0:T(8,128)} %apply.5.refs_2_, bf16[1024,1024]{1,0:T(8,128)(2,1)S(1)} %copy-done.6, ...), custom_call_target="tpu_custom_call" | custom-call | flops 3221225472 | bytes 18874368 | tf_op jit(solution)/shard_map/apply/pallas_call | solution.py:246
  152.5 5.9 %collective-permute-done.18.refs_11_ = f32[1024,128]{1,0:T(8,128)} collective-permute-done((f32[1024,128]{1,0:T(8,128)}, f32[1024,128]{1,0:T(8,128)}, u32[]{:S(2)}, u32[]{:S(2)}) %collective-permute-start.18) | collective-permute-done | bytes 524320 | tf_op jit(solution)/shard_map/ppermute | solution.py:298
  158.4 8.2 %apply.7 = f32[1024,256]{1,0:T(8,128)} custom-call(f32[2]{0:T(128)S(1)} %pad_maximum_fusion.scale_ref, bf16[1024,1024]{1,0:T(8,128)(2,1)S(1)} %get-tuple-element.21.refs_0_, bf16[1024,1024]{1,0:T(8,128)(2,1)S(1)} %copy-done.4, f32[1024,128]{1,0:T(8,128)} %apply.4.refs_2_, bf16[1024,1024]{1,0:T(8,128)(2,1)S(1)} %copy-done.6, ...), custom_call_target="tpu_custom_call", output_to_operand_aliasing={{}: (15, {})} | custom-call | flops 3221225472 | bytes 18874368 | tf_op jit(solution)/shard_map/apply/pallas_call | solution.py:246
  (110 shorter events, 15.1 us)
Async XLA Ops:
  0.0 24.6 %copy-start.12 = (f32[1024,256]{1,0:T(8,128)S(1)}, f32[1024,256]{1,0:T(8,128)}, u32[]{:S(2)}) copy-start(f32[1024,256]{1,0:T(8,128)} %own_ref.3) | copy-start | bytes 3145732
  0.0 24.6 %collective-permute-start = (f32[1024,256]{1,0:T(8,128)}, f32[1024,256]{1,0:T(8,128)S(1)}, u32[]{:S(2)}, u32[]{:S(2)}) collective-permute-start(f32[1024,256]{1,0:T(8,128)} %own_ref.3), channel_id=1, source_target_pairs={{0,1},{1,0},{2,3},{3,2},{4,5},{5,4},{6,7},{7,6},{8,9},{9,8},{10,11... | collective-permute-start | bytes 3145736 | tf_op jit(solution)/shard_map/ppermute | solution.py:295
  6.0 15.4 %collective-permute-start.7 = (f32[2,2,128,128]{3,2,1,0:T(8,128)}, f32[2,2,128,128]{3,2,1,0:T(8,128)S(1)}, u32[]{:S(2)}, u32[]{:S(2)}) collective-permute-start(f32[2,2,128,128]{3,2,1,0:T(8,128)} %get-tuple-element.38), channel_id=1, source_target_pairs={{0,8},{4,12},{8,0},{12,4},{16,24},{20,28},{24,16},{28,20},{1,9},{5... | collective-permute-start | bytes 786440 | tf_op jit(solution)/shard_map/ppermute | solution.py:298
  8.6 13.6 %collective-permute-start.8 = (f32[2,2,128,128]{3,2,1,0:T(8,128)S(1)}, f32[2,2,128,128]{3,2,1,0:T(8,128)S(1)}, u32[]{:S(2)}, u32[]{:S(2)}) collective-permute-start(f32[2,2,128,128]{3,2,1,0:T(8,128)S(1)} %get-tuple-element.37), channel_id=1, source_target_pairs={{0,16},{4,20},{8,24},{12,28},{16,0},{20,4},{24,8},{28,12},{1,17},{... | collective-permute-start | bytes 786440 | tf_op jit(solution)/shard_map/ppermute | solution.py:298
  13.5 21.6 %collective-permute-start.3 = (f32[4,2,128,128]{3,2,1,0:T(8,128)S(1)}, f32[4,2,128,128]{3,2,1,0:T(8,128)}, u32[]{:S(2)}, u32[]{:S(2)}) collective-permute-start(f32[4,2,128,128]{3,2,1,0:T(8,128)S(1)} %dynamic-slice_bitcast_fusion), channel_id=1, source_target_pairs={{0,4},{4,0},{8,12},{12,8},{16,20},{20,16},{24,28},{28,24},{1,5},{5... | collective-permute-start | bytes 1572872 | tf_op jit(solution)/shard_map/ppermute | solution.py:298
  21.3 7.8 %copy-start.14 = (f32[2,2,128,128]{3,2,1,0:T(8,128)}, f32[2,2,128,128]{3,2,1,0:T(8,128)S(1)}, u32[]{:S(2)}) copy-start(f32[2,2,128,128]{3,2,1,0:T(8,128)S(1)} %collective-permute-done.7.rest_0_) | copy-start | bytes 786436
  22.8 15.1 %collective-permute-start.10 = (f32[4,2,128,128]{3,2,1,0:T(8,128)}, f32[4,2,128,128]{3,2,1,0:T(8,128)}, u32[]{:S(2)}, u32[]{:S(2)}) collective-permute-start(f32[4,2,128,128]{3,2,1,0:T(8,128)} %constant_dynamic-update-slice_fusion), channel_id=1, source_target_pairs={{0,2},{1,3},{2,0},{3,1},{4,6},{5,7},{6,4},{7,5},{8,10},{9,11},{10,... | collective-permute-start | bytes 1572872 | tf_op jit(solution)/shard_map/ppermute | solution.py:295
  24.6 26.2 %collective-permute-start.9 = (f32[4,2,128,128]{3,2,1,0:T(8,128)}, f32[4,2,128,128]{3,2,1,0:T(8,128)}, u32[]{:S(2)}, u32[]{:S(2)}) collective-permute-start(f32[4,2,128,128]{3,2,1,0:T(8,128)} %constant_dynamic-update-slice_fusion), channel_id=1, source_target_pairs={{0,1},{1,0},{2,3},{3,2},{4,5},{5,4},{6,7},{7,6},{8,9},{9,8},{10,11... | collective-permute-start | bytes 1572872 | tf_op jit(solution)/shard_map/ppermute | solution.py:295
  24.6 2.2 %copy-start = (f32[1024,1024]{1,0:T(8,128)S(1)}, f32[1024,1024]{1,0:T(8,128)}, u32[]{:S(2)}) copy-start(f32[1024,1024]{1,0:T(8,128)} %r_mate_ref.3) | copy-start | bytes 12582916
  26.8 2.7 %copy-start.24 = (f32[3]{0:T(128)S(1)}, f32[3]{0:T(128)}, u32[]{:S(2)}) copy-start(f32[3]{0:T(128)} %bounds_ref.1) | copy-start | bytes 40
  26.8 8.7 %copy-start.30 = (s32[3,64,2]{1,2,0:T(2,128)S(1)}, s32[3,64,2]{1,2,0:T(2,128)}, u32[]{:S(2)}) copy-start(s32[3,64,2]{1,2,0:T(2,128)} %param.12) | copy-start | bytes 4612
  29.1 14.3 %collective-permute-start.19 = (f32[512,128]{1,0:T(8,128)S(1)}, f32[512,128]{1,0:T(8,128)S(1)}, u32[]{:S(2)}, u32[]{:S(2)}) collective-permute-start(f32[512,128]{1,0:T(8,128)S(1)} %get-tuple-element.34), channel_id=1, source_target_pairs={{0,2},{1,3},{2,0},{3,1},{4,6},{5,7},{6,4},{7,5},{8,10},{9,11},{10,... | collective-permute-start | bytes 786440 | tf_op jit(solution)/shard_map/ppermute | solution.py:295
  33.4 15.7 %collective-permute-start.20 = (f32[512,128]{1,0:T(8,128)}, f32[512,128]{1,0:T(8,128)S(1)}, u32[]{:S(2)}, u32[]{:S(2)}) collective-permute-start(f32[512,128]{1,0:T(8,128)} %get-tuple-element.36), channel_id=1, source_target_pairs={{0,2},{1,3},{2,0},{3,1},{4,6},{5,7},{6,4},{7,5},{8,10},{9,11},{10,... | collective-permute-start | bytes 786440 | tf_op jit(solution)/shard_map/ppermute | solution.py:295
  35.1 19.6 %collective-permute-start.1 = (f32[512,128]{1,0:T(8,128)}, f32[512,128]{1,0:T(8,128)S(1)}, u32[]{:S(2)}, u32[]{:S(2)}) collective-permute-start(f32[512,128]{1,0:T(8,128)} %get-tuple-element.24), channel_id=1, source_target_pairs={{0,2},{1,3},{2,0},{3,1},{4,6},{5,7},{6,4},{7,5},{8,10},{9,11},{10,... | collective-permute-start | bytes 786440 | tf_op jit(solution)/shard_map/ppermute | solution.py:295
  37.9 26.2 %collective-permute-start.4 = (f32[4,2,128,128]{3,2,1,0:T(8,128)}, f32[4,2,128,128]{3,2,1,0:T(8,128)}, u32[]{:S(2)}, u32[]{:S(2)}) collective-permute-start(f32[4,2,128,128]{3,2,1,0:T(8,128)} %collective-permute-done.3.rest_0_), channel_id=1, source_target_pairs={{0,1},{1,0},{2,3},{3,2},{4,5},{5,4},{6,7},{7,6},{8,9},{9,8},{10,11... | collective-permute-start | bytes 1572872 | tf_op jit(solution)/shard_map/ppermute | solution.py:295
  43.5 22.6 %collective-permute-start.11 = (f32[4,2,128,128]{3,2,1,0:T(8,128)}, f32[4,2,128,128]{3,2,1,0:T(8,128)}, u32[]{:S(2)}, u32[]{:S(2)}) collective-permute-start(f32[4,2,128,128]{3,2,1,0:T(8,128)} %collective-permute-done.10), channel_id=1, source_target_pairs={{0,1},{1,0},{2,3},{3,2},{4,5},{5,4},{6,7},{7,6},{8,9},{9,8},{10,11... | collective-permute-start | bytes 1572872 | tf_op jit(solution)/shard_map/ppermute | solution.py:295
  44.2 2.2 %copy-start.1 = (f32[1024,1024]{1,0:T(8,128)S(1)}, f32[1024,1024]{1,0:T(8,128)}, u32[]{:S(2)}) copy-start(f32[1024,1024]{1,0:T(8,128)} %r_mate_ref.3) | copy-start | bytes 12582916
  46.4 2.3 %copy-start.27 = (f32[512,128]{1,0:T(8,128)S(1)}, f32[512,128]{1,0:T(8,128)}, u32[]{:S(2)}) copy-start(f32[512,128]{1,0:T(8,128)} %copy-done.26) | copy-start | bytes 786436
  46.4 10.8 %copy-start.25 = (s32[8,6]{1,0:T(8,128)S(1)}, s32[8,6]{1,0:T(8,128)}, u32[]{:S(2)}) copy-start(s32[8,6]{1,0:T(8,128)} %cols_ref.1) | copy-start | bytes 580
  49.1 17.1 %collective-permute-start.2 = (f32[512,128]{1,0:T(8,128)}, f32[512,128]{1,0:T(8,128)}, u32[]{:S(2)}, u32[]{:S(2)}) collective-permute-start(f32[512,128]{1,0:T(8,128)} %get-tuple-element.26), channel_id=1, source_target_pairs={{0,2},{1,3},{2,0},{3,1},{4,6},{5,7},{6,4},{7,5},{8,10},{9,11},{10,... | collective-permute-start | bytes 786440 | tf_op jit(solution)/shard_map/ppermute | solution.py:295
  50.8 17.7 %collective-permute-start.21 = (f32[512,128]{1,0:T(8,128)S(1)}, f32[512,128]{1,0:T(8,128)S(1)}, u32[]{:S(2)}, u32[]{:S(2)}) collective-permute-start(f32[512,128]{1,0:T(8,128)S(1)} %add.114.refs_2_.refs_12_), channel_id=1, source_target_pairs={{0,4},{4,0},{8,12},{12,8},{16,20},{20,16},{24,28},{28,24},{1,5},{5... | collective-permute-start | bytes 786440 | tf_op jit(solution)/shard_map/ppermute | solution.py:298
  54.7 14.5 %collective-permute-start.22 = (f32[512,128]{1,0:T(8,128)S(1)}, f32[512,128]{1,0:T(8,128)}, u32[]{:S(2)}, u32[]{:S(2)}) collective-permute-start(f32[512,128]{1,0:T(8,128)S(1)} %add.115.refs_3_.refs_13_), channel_id=1, source_target_pairs={{0,4},{4,0},{8,12},{12,8},{16,20},{20,16},{24,28},{28,24},{1,5},{5... | collective-permute-start | bytes 786440 | tf_op jit(solution)/shard_map/ppermute | solution.py:298
  59.0 5.0 %copy-start.23 = (f32[512,128]{1,0:T(8,128)S(1)}, f32[512,128]{1,0:T(8,128)}, u32[]{:S(2)}) copy-start(f32[512,128]{1,0:T(8,128)} %copy-done.22) | copy-start | bytes 786436
  59.0 5.0 %copy-start.29 = (f32[512,128]{1,0:T(8,128)S(1)}, f32[512,128]{1,0:T(8,128)}, u32[]{:S(2)}) copy-start(f32[512,128]{1,0:T(8,128)} %copy-done.28) | copy-start | bytes 786436
  59.0 13.0 %copy-start.2 = (f32[3,8,2,128,128]{4,3,2,1,0:T(8,128)S(1)}, f32[3,8,2,128,128]{4,3,2,1,0:T(8,128)}, u32[]{:S(2)}) copy-start(f32[3,8,2,128,128]{4,3,2,1,0:T(8,128)} %blocks_ref.7) | copy-start | bytes 9437188
  62.6 53.0 %copy-start.3 = (bf16[1024,1024]{1,0:T(8,128)(2,1)}, bf16[1024,1024]{1,0:T(8,128)(2,1)S(1)}, u32[]{:S(2)}) copy-start(bf16[1024,1024]{1,0:T(8,128)(2,1)S(1)} %get-tuple-element.22.refs_1_) | copy-start | bytes 6291460
  64.1 24.9 %collective-permute-start.23 = (f32[512,128]{1,0:T(8,128)S(1)}, f32[512,128]{1,0:T(8,128)S(1)}, u32[]{:S(2)}, u32[]{:S(2)}) collective-permute-start(f32[512,128]{1,0:T(8,128)S(1)} %add.114.refs_2_.refs_12_), channel_id=1, source_target_pairs={{0,8},{4,12},{8,0},{12,4},{16,24},{20,28},{24,16},{28,20},{1,9},{5... | collective-permute-start | bytes 786440 | tf_op jit(solution)/shard_map/ppermute | solution.py:298
  66.0 25.4 %collective-permute-start.24 = (f32[512,128]{1,0:T(8,128)S(1)}, f32[512,128]{1,0:T(8,128)S(1)}, u32[]{:S(2)}, u32[]{:S(2)}) collective-permute-start(f32[512,128]{1,0:T(8,128)S(1)} %add.115.refs_3_.refs_13_), channel_id=1, source_target_pairs={{0,8},{4,12},{8,0},{12,4},{16,24},{20,28},{24,16},{28,20},{1,9},{5... | collective-permute-start | bytes 786440 | tf_op jit(solution)/shard_map/ppermute | solution.py:298
  66.2 25.3 %collective-permute-start.25 = (f32[512,128]{1,0:T(8,128)S(1)}, f32[512,128]{1,0:T(8,128)S(1)}, u32[]{:S(2)}, u32[]{:S(2)}) collective-permute-start(f32[512,128]{1,0:T(8,128)S(1)} %add.114.refs_2_.refs_12_), channel_id=1, source_target_pairs={{0,16},{4,20},{8,24},{12,28},{16,0},{20,4},{24,8},{28,12},{1,17},{... | collective-permute-start | bytes 786440 | tf_op jit(solution)/shard_map/ppermute | solution.py:298
  68.5 7.3 %copy-start.18 = (f32[512,128]{1,0:T(8,128)}, f32[512,128]{1,0:T(8,128)S(1)}, u32[]{:S(2)}) copy-start(f32[512,128]{1,0:T(8,128)S(1)} %collective-permute-done.21.refs_6_) | copy-start | bytes 786436
  68.5 25.1 %collective-permute-start.26 = (f32[512,128]{1,0:T(8,128)S(1)}, f32[512,128]{1,0:T(8,128)}, u32[]{:S(2)}, u32[]{:S(2)}) collective-permute-start(f32[512,128]{1,0:T(8,128)S(1)} %add.115.refs_3_.refs_13_), channel_id=1, source_target_pairs={{0,16},{4,20},{8,24},{12,28},{16,0},{20,4},{24,8},{28,12},{1,17},{... | collective-permute-start | bytes 786440 | tf_op jit(solution)/shard_map/ppermute | solution.py:298
  69.2 31.9 %collective-permute-start.12 = (f32[512,128]{1,0:T(8,128)S(1)}, f32[512,128]{1,0:T(8,128)S(1)}, u32[]{:S(2)}, u32[]{:S(2)}) collective-permute-start(f32[512,128]{1,0:T(8,128)S(1)} %add.96.refs_2_.refs_12_), channel_id=1, source_target_pairs={{0,8},{4,12},{8,0},{12,4},{16,24},{20,28},{24,16},{28,20},{1,9},{5... | collective-permute-start | bytes 786440 | tf_op jit(solution)/shard_map/ppermute | solution.py:298
  72.1 3.8 %copy-start.21 = (f32[512,128]{1,0:T(8,128)S(1)}, f32[512,128]{1,0:T(8,128)}, u32[]{:S(2)}) copy-start(f32[512,128]{1,0:T(8,128)} %copy-done.20) | copy-start | bytes 786436
  72.1 6.3 %copy-start.15 = (f32[2,2,128,128]{3,2,1,0:T(8,128)S(1)}, f32[2,2,128,128]{3,2,1,0:T(8,128)}, u32[]{:S(2)}) copy-start(f32[2,2,128,128]{3,2,1,0:T(8,128)} %copy-done.14) | copy-start | bytes 786436
  75.8 5.1 %copy-start.7 = (bf16[1024,1024]{1,0:T(8,128)(2,1)}, bf16[1024,1024]{1,0:T(8,128)(2,1)S(1)}, u32[]{:S(2)}) copy-start(bf16[1024,1024]{1,0:T(8,128)(2,1)S(1)} %get-tuple-element.28.refs_5_.refs_4_) | copy-start | bytes 6291460
  75.8 39.8 %copy-start.5 = (bf16[1024,1024]{1,0:T(8,128)(2,1)}, bf16[1024,1024]{1,0:T(8,128)(2,1)S(1)}, u32[]{:S(2)}) copy-start(bf16[1024,1024]{1,0:T(8,128)(2,1)S(1)} %get-tuple-element.27.refs_4_.refs_3_) | copy-start | bytes 6291460
  83.7 18.4 %copy-start.19 = (f32[512,128]{1,0:T(8,128)S(1)}, f32[512,128]{1,0:T(8,128)}, u32[]{:S(2)}) copy-start(f32[512,128]{1,0:T(8,128)} %copy-done.18) | copy-start | bytes 786436
  89.0 21.7 %collective-permute-start.14 = (f32[512,128]{1,0:T(8,128)S(1)}, f32[512,128]{1,0:T(8,128)S(1)}, u32[]{:S(2)}, u32[]{:S(2)}) collective-permute-start(f32[512,128]{1,0:T(8,128)S(1)} %add.96.refs_2_.refs_12_), channel_id=1, source_target_pairs={{0,16},{4,20},{8,24},{12,28},{16,0},{20,4},{24,8},{28,12},{1,17},{... | collective-permute-start | bytes 786440 | tf_op jit(solution)/shard_map/ppermute | solution.py:298
  91.4 18.3 %collective-permute-start.13 = (f32[512,128]{1,0:T(8,128)S(1)}, f32[512,128]{1,0:T(8,128)S(1)}, u32[]{:S(2)}, u32[]{:S(2)}) collective-permute-start(f32[512,128]{1,0:T(8,128)S(1)} %add.97.refs_3_.refs_13_), channel_id=1, source_target_pairs={{0,8},{4,12},{8,0},{12,4},{16,24},{20,28},{24,16},{28,20},{1,9},{5... | collective-permute-start | bytes 786440 | tf_op jit(solution)/shard_map/ppermute | solution.py:298
  91.5 20.7 %collective-permute-start.15 = (f32[512,128]{1,0:T(8,128)S(1)}, f32[512,128]{1,0:T(8,128)S(1)}, u32[]{:S(2)}, u32[]{:S(2)}) collective-permute-start(f32[512,128]{1,0:T(8,128)S(1)} %add.97.refs_3_.refs_13_), channel_id=1, source_target_pairs={{0,16},{4,20},{8,24},{12,28},{16,0},{20,4},{24,8},{28,12},{1,17},{... | collective-permute-start | bytes 786440 | tf_op jit(solution)/shard_map/ppermute | solution.py:298
  93.6 22.0 %collective-permute-start.5 = (f32[512,128]{1,0:T(8,128)S(1)}, f32[512,128]{1,0:T(8,128)S(1)}, u32[]{:S(2)}, u32[]{:S(2)}) collective-permute-start(f32[512,128]{1,0:T(8,128)S(1)} %add.96.refs_2_.refs_12_), channel_id=1, source_target_pairs={{0,4},{4,0},{8,12},{12,8},{16,20},{20,16},{24,28},{28,24},{1,5},{5... | collective-permute-start | bytes 786440 | tf_op jit(solution)/shard_map/ppermute | solution.py:298
  101.0 14.5 %collective-permute-start.6 = (f32[512,128]{1,0:T(8,128)S(1)}, f32[512,128]{1,0:T(8,128)S(1)}, u32[]{:S(2)}, u32[]{:S(2)}) collective-permute-start(f32[512,128]{1,0:T(8,128)S(1)} %add.97.refs_3_.refs_13_), channel_id=1, source_target_pairs={{0,4},{4,0},{8,12},{12,8},{16,20},{20,16},{24,28},{28,24},{1,5},{5... | collective-permute-start | bytes 786440 | tf_op jit(solution)/shard_map/ppermute | solution.py:298
  109.8 14.3 %collective-permute-start.27 = (f32[1024,128]{1,0:T(8,128)}, f32[1024,128]{1,0:T(8,128)S(1)}, u32[]{:S(2)}, u32[]{:S(2)}) collective-permute-start(f32[1024,128]{1,0:T(8,128)} %apply.5.refs_2_), channel_id=1, source_target_pairs={{0,4},{4,0},{8,12},{12,8},{16,20},{20,16},{24,28},{28,24},{1,5},{5... | collective-permute-start | bytes 1572872 | tf_op jit(solution)/shard_map/ppermute | solution.py:298
  110.7 28.1 %collective-permute-start.28 = (f32[1024,128]{1,0:T(8,128)}, f32[1024,128]{1,0:T(8,128)}, u32[]{:S(2)}, u32[]{:S(2)}) collective-permute-start(f32[1024,128]{1,0:T(8,128)} %apply.5.refs_2_), channel_id=1, source_target_pairs={{0,8},{4,12},{8,0},{12,4},{16,24},{20,28},{24,16},{28,20},{1,9},{5... | collective-permute-start | bytes 1572872 | tf_op jit(solution)/shard_map/ppermute | solution.py:298
  112.2 27.8 %collective-permute-start.29 = (f32[1024,128]{1,0:T(8,128)}, f32[1024,128]{1,0:T(8,128)}, u32[]{:S(2)}, u32[]{:S(2)}) collective-permute-start(f32[1024,128]{1,0:T(8,128)} %apply.5.refs_2_), channel_id=1, source_target_pairs={{0,16},{4,20},{8,24},{12,28},{16,0},{20,4},{24,8},{28,12},{1,17},{... | collective-permute-start | bytes 1572872 | tf_op jit(solution)/shard_map/ppermute | solution.py:298
  123.3 29.2 %collective-permute-start.16 = (f32[1024,128]{1,0:T(8,128)}, f32[1024,128]{1,0:T(8,128)}, u32[]{:S(2)}, u32[]{:S(2)}) collective-permute-start(f32[1024,128]{1,0:T(8,128)} %apply.4.refs_2_), channel_id=1, source_target_pairs={{0,4},{4,0},{8,12},{12,8},{16,20},{20,16},{24,28},{28,24},{1,5},{5... | collective-permute-start | bytes 1572872 | tf_op jit(solution)/shard_map/ppermute | solution.py:298
  124.0 28.5 %collective-permute-start.17 = (f32[1024,128]{1,0:T(8,128)}, f32[1024,128]{1,0:T(8,128)}, u32[]{:S(2)}, u32[]{:S(2)}) collective-permute-start(f32[1024,128]{1,0:T(8,128)} %apply.4.refs_2_), channel_id=1, source_target_pairs={{0,8},{4,12},{8,0},{12,4},{16,24},{20,28},{24,16},{28,20},{1,9},{5... | collective-permute-start | bytes 1572872 | tf_op jit(solution)/shard_map/ppermute | solution.py:298
  124.8 33.5 %collective-permute-start.18 = (f32[1024,128]{1,0:T(8,128)}, f32[1024,128]{1,0:T(8,128)}, u32[]{:S(2)}, u32[]{:S(2)}) collective-permute-start(f32[1024,128]{1,0:T(8,128)} %apply.4.refs_2_), channel_id=1, source_target_pairs={{0,16},{4,20},{8,24},{12,28},{16,0},{20,4},{24,8},{28,12},{1,17},{... | collective-permute-start | bytes 1572872 | tf_op jit(solution)/shard_map/ppermute | solution.py:298
  (13 other events, 17.7 us)

commit v2 on v0

v2 whole, which is shorter than its diff:
```python
import functools

import jax
import jax.numpy as jnp
from jax import lax
from jax.experimental import pallas as pl
from jax.experimental.pallas import tpu as pltpu
from jax.sharding import PartitionSpec as P

f32 = jnp.float32
bf16 = jnp.bfloat16
HBM = pl.BlockSpec(memory_space=pltpu.HBM)
VMEM = pl.BlockSpec(memory_space=pltpu.VMEM)
SMEM = pl.BlockSpec(memory_space=pltpu.SMEM)
PARAMS = pltpu.CompilerParams(vmem_limit_bytes=20 * 1024 * 1024)


def split(x):
    hi = x.astype(bf16)
    return hi, (x - hi.astype(f32)).astype(bf16)


def dot(a, b):
    return jnp.dot(a, b, preferred_element_type=f32)


def call(
    token, kernel, operands, specs, out_specs, out_shape, scratch, name,
    flops=0, nbytes=0, aliases=None, waits=(),
):
    ins, outs = len(operands), len(out_shape)
    first = ins + 1 + len(waits)

    def body(*refs):
        refs[first + outs][...] = jnp.zeros(token.shape, f32)
        kernel(*refs[:ins], *refs[first:first + outs], *refs[first + outs + 1:])

    *results, token = pl.pallas_call(
        body,
        in_specs=[*specs, *[pl.BlockSpec(memory_space=pl.ANY)] * (1 + len(waits))],
        out_specs=[*out_specs, VMEM],
        out_shape=[*out_shape, jax.ShapeDtypeStruct(token.shape, f32)],
        scratch_shapes=scratch,
        input_output_aliases=aliases or {},
        compiler_params=PARAMS,
        cost_estimate=pl.CostEstimate(flops=flops, bytes_accessed=nbytes, transcendentals=0),
        name=name,
    )(*operands, token, *waits)
    return results, token


def in_hbm(x):
    return pltpu.with_memory_space_constraint(x, pltpu.HBM)


def array(*shape):
    return jax.ShapeDtypeStruct(shape, f32)


def colour_of(partners_ref, slot, by_bit):
    if not by_bit:
        return jnp.int32(slot)
    colour = jnp.int32(0)
    for c in range(1, partners_ref.shape[0]):
        colour = jnp.where(partners_ref[c, 0] == (1 << slot), c, colour)
    return colour


def product(v, r):
    v_hi, v_lo = split(v)
    r_hi, r_lo = split(r)
    return dot(
        jnp.concatenate([v_hi, v_lo, v_hi], axis=1), jnp.concatenate([r_hi, r_hi, r_lo], axis=0)
    )


def band_block(index, band, width=None, part=0):
    width = width or band
    return pl.ds(pl.multiple_of(index * band + part * width, width), width)


def begin(token, vectors, rotation, partners, blocks, masks, heights, by_bit):
    rows, band = vectors.shape
    half = band // 2
    slots, tail = blocks.shape[0], blocks.shape[2:]
    wide = len(masks) * half

    def kernel(partners_ref, v_ref, rotation_ref, blocks_ref, part_ref, mate_r_ref, *refs):
        shares, (v_buf, r_buf, sems) = refs[:slots], refs[slots:]
        me = lax.axis_index("bands")
        copies = [pltpu.make_async_copy(v_ref, v_buf, sems.at[0])]
        for n, mask in enumerate(masks):
            cols = band_block(me ^ mask, band, half)
            for m, (who, dst) in enumerate(((me, r_buf), (me ^ 1, mate_r_ref))):
                src = rotation_ref.at[band_block(who, band), cols]
                dst = dst.at[:, n * half:(n + 1) * half]
                copies.append(pltpu.make_async_copy(src, dst, sems.at[1 + 2 * n + m]))
        first = len(copies)
        for slot, out in enumerate(shares):
            height = heights[slot]
            at = lax.rem(me, blocks_ref.shape[1] // height) * height
            src = blocks_ref.at[colour_of(partners_ref, slot, by_bit), pl.ds(at, height)]
            copies.append(pltpu.make_async_copy(src, out, sems.at[first + slot]))
        for c in copies:
            c.start()
        for c in copies[:first]:
            c.wait()
        part_ref[...] = product(v_buf[...], r_buf[...])
        for c in copies[first:]:
            c.wait()

    (part, mate_r, *shares), token = call(
        token, kernel,
        [in_hbm(partners), in_hbm(vectors), rotation, blocks], [SMEM, HBM, HBM, HBM],
        [VMEM] * (2 + slots),
        [array(rows, wide), array(band, wide)] + [array(n, *tail) for n in heights],
        [
            pltpu.VMEM((rows, band), f32),
            pltpu.VMEM((band, wide), f32),
            pltpu.SemaphoreType.DMA((1 + 2 * len(masks) + slots,)),
        ],
        "begin",
    )
    return part, mate_r, shares, token


def rotate_first(token, part, mate, mate_r, count):
    rows = mate.shape[0]
    half = part.shape[1] // count

    def kernel(part_ref, mate_ref, r_ref, *outs):
        total = part_ref[...] + product(mate_ref[...], r_ref[...])
        for n, out in enumerate(outs):
            out[...] = total[:, n * half:(n + 1) * half]

    return call(
        token, kernel, [part, mate, mate_r], [VMEM] * 3, [VMEM] * count,
        [array(rows, half)] * count, [], "rotate_first",
    )


def rotate_rest(token, vectors, mate, rotation, masks):
    rows, band = mate.shape
    half = band // 2
    wide = (len(masks) + 2) * half

    def kernel(v_ref, mate_ref, rotation_ref, *refs):
        others, (own_first, own_second, v_buf, r_buf, sems) = refs[:len(masks)], refs[len(masks):]
        me = lax.axis_index("bands")
        copies = [pltpu.make_async_copy(v_ref, v_buf, sems.at[0])]
        for m, who in enumerate((me, me ^ 1)):
            picks = [band_block(me ^ mask, band, half, 1) for mask in masks]
            picks += [band_block(me, band, half, h) for h in range(2)]
            for n, cols in enumerate(picks):
                src = rotation_ref.at[band_block(who, band), cols]
                dst = r_buf.at[m, :, n * half:(n + 1) * half]
                copies.append(pltpu.make_async_copy(src, dst, sems.at[1 + m * len(picks) + n]))
        for c in copies:
            c.start()
        for c in copies:
            c.wait()
        total = product(v_buf[...], r_buf[0]) + product(mate_ref[...], r_buf[1])
        for n, out in enumerate(others):
            out[...] = total[:, n * half:(n + 1) * half]
        own_first[...] = total[:, wide - 2 * half:wide - half]
        own_second[...] = total[:, wide - half:]

    out, token = call(
        token, kernel, [vectors, mate, rotation], [HBM, VMEM, HBM],
        [VMEM] * (len(masks) + 2), [array(rows, half)] * (len(masks) + 2),
        [
            pltpu.VMEM((rows, band), f32),
            pltpu.VMEM((2, band, wide), f32),
            pltpu.SemaphoreType.DMA((1 + 2 * (len(masks) + 2),)),
        ],
        "rotate_rest",
    )
    return out[:-2], out[-2], out[-1], token


def meet(token, parts, blocks=()):
    height = blocks[0].shape[0] if blocks else 0

    def kernel(*refs):
        total = refs[0][...]
        for ref in refs[1:len(parts)]:
            total = total + ref[...]
        refs[len(parts) + len(blocks)][...] = total
        for n, ref in enumerate(refs[len(parts):len(parts) + len(blocks)]):
            refs[-1][n * height:(n + 1) * height] = ref[...]

    shapes = [array(*parts[0].shape)]
    if blocks:
        shapes.append(array(len(blocks) * height, blocks[0].shape[1]))
    ins = [*parts, *blocks]
    return call(token, kernel, ins, [VMEM] * len(ins), [VMEM] * len(shapes), shapes, [], "meet")


def touch(token, waits):
    return call(token, lambda: None, [], [], [], [], [], "touch", waits=waits)[1]


def write_parts(acc, hi_ref, lo_ref):
    count, _, size, _ = acc.shape

    def one(i, carry):
        rows = pl.ds(pl.multiple_of(i * size, size), size)
        for j in range(count):
            hi, lo = split(acc[i, j])
            hi_ref[rows, j * size:(j + 1) * size] = hi
            lo_ref[rows, j * size:(j + 1) * size] = lo
        return carry

    lax.fori_loop(0, count, one, 0)


def local_kernel(cols_ref, bounds_ref, blocks_ref, hi_ref, lo_ref, acc):
    count, _, size, _ = acc.shape
    stored = blocks_ref.shape[1]
    acc[...] = jnp.zeros_like(acc)
    centre = (bounds_ref[2] + bounds_ref[1]) / 2.0
    eye = lax.broadcasted_iota(jnp.int32, (size, size), 0) == lax.broadcasted_iota(
        jnp.int32, (size, size), 1
    )
    shift = jnp.where(eye, -centre, 0.0).astype(f32)
    for i in range(count):
        acc[i, i] = shift

    def one(a, carry):
        for k in range(stored):
            block = blocks_ref[a, k]
            col = cols_ref[a * stored + k]
            acc[a, col] += block
            acc[col, a] += block.T
        return carry

    lax.fori_loop(0, count, one, 0)
    write_parts(acc, hi_ref, lo_ref)


def build_local(token, blocks, cols, bounds):
    count, stored, size, _ = blocks.shape
    rows = count * size
    return call(
        token, local_kernel, [cols, bounds, blocks], [SMEM, SMEM, VMEM],
        [VMEM, VMEM], [jax.ShapeDtypeStruct((rows, rows), bf16)] * 2,
        [pltpu.VMEM((count, count, size, size), f32)], "build_local",
    )


def build_couple(token, slot, by_bit, cols, partners, blocks, places):
    colours, count, stored, size, _ = blocks.shape
    rows = count * size
    shards = partners.shape[1]

    def kernel(cols_ref, partners_ref, blocks_ref, *refs):
        pieces, (hi_ref, lo_ref, own_buf, mate_buf, acc, sems) = refs[:len(places)], refs[len(places):]
        colour = colour_of(partners_ref, slot, by_bit)
        me = lax.axis_index("rows")
        band = lax.axis_index("bands")
        mate = me ^ (1 << slot) if by_bit else me ^ partners_ref[slot, 0]
        own_at = (colour * shards + me) * count
        mate_at = (colour * shards + mate) * count
        copies = [pltpu.make_async_copy(blocks_ref.at[colour], own_buf, sems.at[0])]
        for n, (_, start, height, _) in enumerate(places):
            long = height * stored * size
            src, dst = pieces[n].at[start:start + long], mate_buf.at[n * long:(n + 1) * long]
            copies.append(pltpu.make_async_copy(src, dst, sems.at[1 + n]))
        for c in copies:
            c.start()
        acc[...] = jnp.zeros_like(acc)
        for c in copies:
            c.wait()
        for n, (_, _, height, mask) in enumerate(places):
            first = lax.rem(band ^ mask, count // height) * height
            for i in range(height):
                a = first + i
                for k in range(stored):
                    at = ((n * height + i) * stored + k) * size
                    acc[cols_ref[(mate_at + a) * stored + k], a] += mate_buf[at:at + size].T

        def own(a, carry):
            for k in range(stored):
                acc[a, cols_ref[(own_at + a) * stored + k]] += own_buf[a, k]
            return carry

        lax.fori_loop(0, count, own, 0)
        write_parts(acc, hi_ref, lo_ref)

    return call(
        token, kernel, [cols, partners, blocks, *[in_hbm(p[0]) for p in places]],
        [SMEM, SMEM, HBM] + [HBM] * len(places),
        [VMEM, VMEM], [jax.ShapeDtypeStruct((rows, rows), bf16)] * 2,
        [
            pltpu.VMEM((count, stored, size, size), f32),
            pltpu.VMEM((count * stored * size, size), f32),
            pltpu.VMEM((count, count, size, size), f32),
            pltpu.SemaphoreType.DMA((1 + len(places),)),
        ],
        "build_couple",
    )


def scales(bounds_ref, step, shape):
    lowest, lower, upper = (jnp.full(shape, bounds_ref[i], f32) for i in range(3))
    half_width = (upper - lower) / 2.0
    centre = (upper + lower) / 2.0
    sigma_one = half_width / (lowest - centre)
    sigma_two = 1.0 / (2.0 / sigma_one - sigma_one)
    if step == 1:
        return sigma_one / half_width, None
    return 2.0 * sigma_two / half_width, -sigma_one * sigma_two


def apply_kernel(counts, step, has_partial, base_count, column, bounds_ref, *refs):
    refs = list(refs)
    mats = []
    for chunks in counts:
        hi, lo = refs.pop(0), refs.pop(0)
        mats.append((hi, lo, [refs.pop(0) for _ in range(chunks)]))
    partial = refs.pop(0) if has_partial else None
    base = [refs.pop(0) for _ in range(base_count)]
    if column is not None and column > 0:
        refs.pop(0)
    out_ref, w_buf, acc, sem = refs
    rows, width = acc.shape
    for m, (hi, lo, chunks) in enumerate(mats):
        at = 0
        for chunk in chunks:
            u_hi, u_lo = split(chunk[...])
            w_buf[at:at + chunk.shape[0], :width] = u_hi
            w_buf[at:at + chunk.shape[0], width:] = u_lo
            at += chunk.shape[0]
        both = dot(hi[...], w_buf[...])
        part = both[:, :width] + both[:, width:] + dot(lo[...], w_buf[:, :width])
        if m == 0:
            acc[...] = part
        else:
            acc[...] += part
    if step is not None:
        s_sum, s_base = scales(bounds_ref, step, (1, width))
        acc[...] = acc[...] * s_sum
    if partial is not None:
        acc[...] += partial[...]
    at = 0
    for chunk in base:
        piece = slice(at, at + chunk.shape[0])
        acc[piece] += chunk[...] * s_base
        at += chunk.shape[0]
    if column is None:
        out_ref[...] = acc[...]
    else:
        c = pltpu.make_async_copy(acc, out_ref.at[:, column:column + width], sem)
        c.start()
        c.wait()


def apply(
    token, bounds, mats, step=None, partial=None, base=(), column=None, out_width=None, into=None,
    late=False, waits=()):
    rows = mats[0][0].shape[0]
    width = mats[0][2][0].shape[1]
    operands = [bounds]
    specs = [SMEM]
    for hi, lo, chunks in mats:
        operands += [hi, lo, *chunks]
        specs += [VMEM] * (2 + len(chunks))
    if partial is not None:
        operands.append(partial)
        specs.append(VMEM)
    operands += list(base)
    specs += [VMEM] * len(base)
    aliases = {}
    if into is not None:
        aliases = {len(operands): 0}
        operands.append(into)
        specs.append(HBM)
    shape = array(rows, width if column is None else out_width)
    kernel = functools.partial(
        apply_kernel, [len(m[2]) for m in mats], step, partial is not None, len(base), column
    )
    (out,), token = call(
        token, kernel, operands, specs, [VMEM if column is None else HBM], [shape],
        [
            pltpu.VMEM((rows, 2 * width), bf16),
            pltpu.VMEM((rows, width), f32),
            pltpu.SemaphoreType.DMA,
        ],
        "apply",
        len(mats) * 6 * rows * rows * width if late else 0,
        len(mats) * rows * rows * 4 if late else 0,
        aliases,
        waits,
    )
    return out, token


def gate(x, *after):
    return lax.optimization_barrier((x, *after))[0]


def local(
    n_rows, n_bands,
    vectors, local_blocks, local_cols, coupling_blocks, coupling_cols, partners, bounds, rotation
):
    rows, band = vectors.shape
    colours, block_count = coupling_blocks.shape[:2]
    half = band // 2
    bits = n_rows.bit_length() - 1
    by_bit = bits == colours
    slots = range(colours)

    def to_band(x, mask):
        return lax.ppermute(x, "bands", [(i, i ^ mask) for i in range(n_bands)])

    def to_row(x, bit):
        return lax.ppermute(x, "rows", [(i, i ^ (1 << bit)) for i in range(n_rows)])

    def exchange(x, slot):
        if by_bit:
            return to_row(x, slot)
        taken = jnp.zeros_like(x)
        for bit in range(bits):
            taken = jnp.where(partners[slot, 0] == (1 << bit), to_row(x, bit), taken)
        return taken

    blocks = in_hbm(coupling_blocks)
    spin = in_hbm(rotation)
    flat_cols = coupling_cols.reshape(-1)
    token = jnp.zeros((8, 128), f32)

    chip_mate = to_band(vectors, 1)

    masks = list(range(2, n_bands, 2))
    order = list(slots)[::-1]
    near = [k for k in slots if by_bit and k == 0]
    far = [k for k in slots if k not in near]
    heights = [block_count // (2 if k in near else n_bands) for k in slots]
    stored = coupling_blocks.shape[2]
    vecs = in_hbm(vectors)
    part, mate_r, shares, token = begin(token, vecs, spin, partners, blocks, masks, heights, by_bit)
    sent, token = rotate_first(token, part, chip_mate, mate_r, len(masks))
    came = [to_band(c, mask) for c, mask in zip(sent, masks)]
    second, own_first, own_second, token = rotate_rest(token, vecs, chip_mate, spin, masks)
    shares = [s.reshape(-1, s.shape[-1]) for s in shares]
    shares = {k: exchange(gate(shares[k], token) if k in near else shares[k], k) for k in order}
    (total, joined), token = meet(token, [own_first, *came], [shares[k] for k in far])
    later = [to_band(gate(c, token), mask) for c, mask in zip(second, masks)]
    field = [total]
    held = {0: joined, 1: to_band(joined, 1)}
    passed = [to_band(joined, mask) for mask in masks]

    def send(part, after=None):
        return {k: exchange(gate(part, after) if k in near and after is not None else part, k) for k in order}

    def part_sum(terms, *rest, **options):
        nonlocal token
        out, token = apply(token, bounds, terms, *rest, **options)
        return out

    arrived = [send(total)]
    (total,), token = meet(token, [own_second, *later])
    field.append(total)
    local_parts, token = build_local(token, local_blocks, local_cols.reshape(-1), bounds)
    waits = [shares[k] for k in near] + [held[1]]
    partial = [part_sum([(*local_parts, [field[0]])], 1, waits=waits)]
    partial.append(part_sum([(*local_parts, [field[1]])], 1))
    token = touch(token, [arrived[0][k] for k in slots])

    for mask, x in zip(masks, passed):
        held[mask] = gate(x, token)
        held[mask ^ 1] = to_band(held[mask], 1)
    for k in near:
        shares[k] = gate(shares[k], token)
    total = gate(total, token)
    size = coupling_blocks.shape[-1]
    mats = {}
    for k in far + near:
        if k in near:
            places = [(shares[k], 0, heights[k], 0), (to_band(shares[k], 1), 0, heights[k], 1)]
        else:
            at = far.index(k) * heights[k] * stored * size
            places = [(x, at, heights[k], m) for m, x in held.items()]
        mats[k], token = build_couple(token, k, by_bit, flat_cols, partners, blocks, places)
        if k == far[0]:
            arrived.append(send(total, token))
    first = []
    for h in range(2):
        terms = [(*mats[k], [arrived[h][k]]) for k in slots]
        first.append(part_sum(terms, 1, partial[h]))
    arrived = [send(f) for f in first]
    out = None
    for h in range(2):
        terms = [(*local_parts, [first[h]])] + [(*mats[k], [arrived[h][k]]) for k in near]
        early = part_sum(terms, 2, None, [field[h]], late=True)
        for k in far[:-1]:
            early = part_sum([(*mats[k], [arrived[h][k]])], 2, early, late=True)
        k = far[-1]
        out = part_sum([(*mats[k], [arrived[h][k]])], 2, early, (), h * half, band, out, late=True)
    return out


def solution(mesh):
    in_specs = (
        P("rows", "bands"),
        P("rows", None, None, None),
        P("rows", None),
        P(None, "rows", None, None, None),
        P(),
        P(),
        P(),
        P(),
    )
    body = functools.partial(local, mesh.shape["rows"], mesh.shape["bands"])
    return jax.shard_map(
        body, mesh=mesh, in_specs=in_specs, out_specs=P("rows", "bands"), check_vma=False
    )
```

time: 552 us -> 129 us (0.23)
  waiting for transfers between devices: 248 us -> 48 us
  matrix products: 115 us -> 0 us
  local copies, waits for them, and re-layouts: 76.5 us -> 3.06 us
  Pallas kernels: 0 us -> 55.4 us
  blocking collectives: 29.4 us -> 0 us
  starting transfers between devices: 42.1 us -> 21.2 us
  between operations: 19.5 us -> 0.43 us
  other arithmetic: 16.9 us -> 0 us
    all_to_all x9 -> x0, waiting for transfers between devices: 202 us -> none  [the longest x6 91.1 us: route_pair(): lax.all_to_all(regrouped, 'rows', split_axis=1, concat_axis=1, tiled=True)]
    dot_general x25 -> x0, matrix products: 115 us -> none  [the longest x8 41.1 us: forward(): return jnp.einsum('akij,akjw->aiw', blocks, picked, precision=precise)]
    pallas_call x0 -> x20, Pallas kernels: none -> 55.4 us  [call(): pl.pallas_call(body, in_specs=[*specs, *[pl.BlockSpec(memory_space=pl.ANY...]
    gather x17 -> x0, local copies, waits for them, and re-layouts: 54.5 us -> none  [the longest x8 29.2 us: forward(): picked = jnp.take(source, block_cols, axis=0)]
    ppermute x0 -> x22, waiting for transfers between devices: none -> 48 us  [the longest x15 41.3 us: to_row(): return lax.ppermute(x, 'rows', [(i, i ^ 1 << bit) for i in range(n_rows)])]
    reduce_scatter x1 -> x0, waiting for transfers between devices: 45.9 us -> none  [local(): lax.psum_scatter(partial_sum, 'bands', scatter_dimension=1, tiled=True)]
    all_to_all x9 -> x0, starting transfers between devices: 42.1 us -> none  [the longest x6 25.4 us: route_pair(): lax.all_to_all(regrouped, 'rows', split_axis=1, concat_axis=1, tiled=True)]
    all_to_all x1 -> x0, blocking collectives: 29.4 us -> none  [route_pair(): lax.all_to_all(pieces, 'rows', split_axis=1, concat_axis=1, tiled=True)]
  transfers between devices with their start and end apart: 10 -> 22, of which waited for: 9 -> 12; matrix products, arithmetic and copies ran while one was open for 23% -> 0% of each run, Pallas kernels for 0% -> 40%
where the time goes in v2:
time: 129 us; the launch traced here: 128 us
  Pallas kernels  55.4 us (43%)
  waiting for transfers between devices  48 us (37%)
  starting transfers between devices  21.2 us (16%)
  local copies, waits for them, and re-layouts  3.06 us (2%)
    pallas_call x20, Pallas kernels, call(): pl.pallas_call(body, in_specs=[*specs, *[pl.BlockSpec(memory_space=pl.ANY...  55.4 us
    ppermute x15, waiting for transfers between devices, to_row(): return lax.ppermute(x, 'rows', [(i, i ^ 1 << bit) for i in range(n_rows)])  41.3 us
    ppermute x15, starting transfers between devices, to_row(): return lax.ppermute(x, 'rows', [(i, i ^ 1 << bit) for i in range(n_rows)])  16.3 us
    ppermute x7, waiting for transfers between devices, to_band(): return lax.ppermute(x, 'bands', [(i, i ^ mask) for i in range(n_bands)])  6.69 us
    ppermute x7, starting transfers between devices, to_band(): return lax.ppermute(x, 'bands', [(i, i ^ mask) for i in range(n_bands)])  4.85 us
    unnamed x21, local copies, waits for them, and re-layouts  2.84 us
  transfers between devices with their start and end apart: 22, of which 12 were waited for; matrix products, arithmetic and copies ran while one was open for 0% of the time, Pallas kernels for 40%

profile of v2, /device:TPU:0, one launch (start us, length us, event | category | flops | bytes accessed | tf_op | source)
XLA Modules:
  0.0 128.0 jit_solution(740048534642795302)
XLA Ops:
  0.5 2.6 %begin.1 = (f32[1024,128]{1,0:T(8,128)S(1)}, f32[256,128]{1,0:T(8,128)S(1)}, f32[4,2,128,128]{3,2,1,0:T(8,128)S(1)}, f32[2,2,128,128]{3,2,1,0:T(8,128)S(1)}, f32...) custom-call(s32[3,8]{1,0:T(4,128)} %refs_1_.9, f32[1024,256]{1,0:T(8,128)} %refs_0_.13, f32[1024,1024]{1,0:T(8,128)} %refs_2_.7, ...), custom_call_target="tpu_custom_call" | custom-call | tf_op jit(solution)/shard_map/begin/pallas_call | solution.py:38
  3.1 0.6 rotate_first.1
  3.7 2.8 %collective-permute-start.1 = (f32[1024,128]{1,0:T(8,128)S(1)}, f32[1024,128]{1,0:T(8,128)S(1)}, u32[]{:S(2)}, u32[]{:S(2)}) collective-permute-start(f32[1024,128]{1,0:T(8,128)S(1)} %get-tuple-element.64), channel_id=1, source_target_pairs={{0,2},{1,3},{2,0},{3,1},{4,6},{5,7},{6,4},{7,5},{8,10},{9,11},{10,... | collective-permute-start | bytes 1572872 | tf_op jit(solution)/shard_map/ppermute | solution.py:414
  6.5 1.6 %collective-permute-start.2 = (f32[512,128]{1,0:T(8,128)S(1)}, f32[512,128]{1,0:T(8,128)S(1)}, u32[]{:S(2)}, u32[]{:S(2)}) collective-permute-start(f32[512,128]{1,0:T(8,128)S(1)} %bitcast.5), channel_id=1, source_target_pairs={{0,8},{4,12},{8,0},{12,4},{16,24},{20,28},{24,16},{28,20},{1,9},{5... | collective-permute-start | bytes 786440 | tf_op jit(solution)/shard_map/ppermute | solution.py:417
  8.0 2.6 %collective-permute-start.3 = (f32[512,128]{1,0:T(8,128)S(1)}, f32[512,128]{1,0:T(8,128)S(1)}, u32[]{:S(2)}, u32[]{:S(2)}) collective-permute-start(f32[512,128]{1,0:T(8,128)S(1)} %bitcast.4), channel_id=1, source_target_pairs={{0,16},{4,20},{8,24},{12,28},{16,0},{20,4},{24,8},{28,12},{1,17},{... | collective-permute-start | bytes 786440 | tf_op jit(solution)/shard_map/ppermute | solution.py:417
  10.6 3.3 %rotate_rest.1 = (f32[1024,128]{1,0:T(8,128)S(1)}, f32[1024,128]{1,0:T(8,128)S(1)}, f32[1024,128]{1,0:T(8,128)S(1)}, f32[8,128]{1,0:T(8,128)S(1)}) custom-call(f32[1024,256]{1,0:T(8,128)} %refs_0_.13, f32[1024,256]{1,0:T(8,128)S(1)} %collective-permute-done.refs_1_, f32[1024,1024]{1,0:T(8,128)} %refs_2_.7, f32[8,128]{1,0:T(8,128)S(1)} %get-tuple-element.62.refs_3_), custom_call_target="tpu_custom_call" | custom-call | tf_op jit(solution)/shard_map/rotate_rest/pallas_call | solution.py:38
  14.0 1.6 %collective-permute-start.7 = (f32[1024,128]{1,0:T(8,128)S(1)}, f32[1024,128]{1,0:T(8,128)}, u32[]{:S(2)}, u32[]{:S(2)}) collective-permute-start(f32[1024,128]{1,0:T(8,128)S(1)} %bitcast.3), channel_id=1, source_target_pairs={{0,4},{4,0},{8,12},{12,8},{16,20},{20,16},{24,28},{28,24},{1,5},{5... | collective-permute-start | bytes 1572872 | tf_op jit(solution)/shard_map/ppermute | solution.py:417
  15.5 4.6 %collective-permute-done.2.refs_2_ = f32[512,128]{1,0:T(8,128)S(1)} collective-permute-done((f32[512,128]{1,0:T(8,128)S(1)}, f32[512,128]{1,0:T(8,128)S(1)}, u32[]{:S(2)}, u32[]{:S(2)}) %collective-permute-start.2) | collective-permute-done | bytes 262176 | tf_op jit(solution)/shard_map/ppermute | solution.py:417
  20.1 2.4 %collective-permute-done.3.refs_3_ = f32[512,128]{1,0:T(8,128)S(1)} collective-permute-done((f32[512,128]{1,0:T(8,128)S(1)}, f32[512,128]{1,0:T(8,128)S(1)}, u32[]{:S(2)}, u32[]{:S(2)}) %collective-permute-start.3) | collective-permute-done | bytes 262176 | tf_op jit(solution)/shard_map/ppermute | solution.py:417
  22.5 1.1 meet.2
  23.6 0.5 collective-permute-start.6
  24.5 1.5 %collective-permute-start.8 = (f32[1024,128]{1,0:T(8,128)}, f32[1024,128]{1,0:T(8,128)}, u32[]{:S(2)}, u32[]{:S(2)}) collective-permute-start(f32[1024,128]{1,0:T(8,128)} %get-tuple-element.77.refs_3_.refs_7_), channel_id=1, source_target_pairs={{0,4},{4,0},{8,12},{12,8},{16,20},{20,16},{24,28},{28,24},{1,5},{5... | collective-permute-start | bytes 1572872 | tf_op jit(solution)/shard_map/ppermute | solution.py:417
  26.0 1.4 %collective-permute-done.7.refs_5_.refs_3_ = f32[1024,128]{1,0:T(8,128)} collective-permute-done((f32[1024,128]{1,0:T(8,128)S(1)}, f32[1024,128]{1,0:T(8,128)}, u32[]{:S(2)}, u32[]{:S(2)}) %collective-permute-start.7) | collective-permute-done | bytes 524320 | tf_op jit(solution)/shard_map/ppermute | solution.py:417
  27.4 1.3 %collective-permute-start.9 = (f32[1024,128]{1,0:T(8,128)}, f32[1024,128]{1,0:T(8,128)}, u32[]{:S(2)}, u32[]{:S(2)}) collective-permute-start(f32[1024,128]{1,0:T(8,128)} %get-tuple-element.77.refs_3_.refs_7_), channel_id=1, source_target_pairs={{0,8},{4,12},{8,0},{12,4},{16,24},{20,28},{24,16},{28,20},{1,9},{5... | collective-permute-start | bytes 1572872 | tf_op jit(solution)/shard_map/ppermute | solution.py:417
  28.7 6.7 %collective-permute-done.6.refs_1_ = f32[1024,128]{1,0:T(8,128)S(1)} collective-permute-done((f32[1024,128]{1,0:T(8,128)S(1)}, f32[1024,128]{1,0:T(8,128)S(1)}, u32[]{:S(2)}, u32[]{:S(2)}) %collective-permute-start.6) | collective-permute-done | bytes 524320 | tf_op jit(solution)/shard_map/ppermute | solution.py:414
  35.4 0.5 collective-permute-start.5
  36.0 0.9 meet.3
  36.8 1.9 %copy-done.3 = f32[8,6,128,128]{3,2,1,0:T(8,128)S(1)} copy-done((f32[8,6,128,128]{3,2,1,0:T(8,128)S(1)}, f32[8,6,128,128]{3,2,1,0:T(8,128)}, u32[]{:S(2)}) %copy-start.3) | copy-done | bytes 3145752
  38.7 3.4 %build_local.1 = (bf16[1024,1024]{1,0:T(8,128)(2,1)S(1)}, bf16[1024,1024]{1,0:T(8,128)(2,1)S(1)}, f32[8,128]{1,0:T(8,128)S(1)}) custom-call(s32[48]{0:T(128)S(1)} %reshape.18.refs_0_, f32[3]{0:T(128)S(1)} %copy-done.6, f32[8,6,128,128]{3,2,1,0:T(8,128)S(1)} %copy-done.3, f32[8,128]{1,0:T(8,128)S(1)} %get-tuple-element.73.refs_3_), custom_call_target="tpu_custom_call" | custom-call | tf_op jit(solution)/shard_map/build_local/pallas_call | solution.py:38
  42.2 2.8 %apply.10 = (f32[1024,128]{1,0:T(8,128)S(1)}, f32[8,128]{1,0:T(8,128)S(1)}) custom-call(f32[3]{0:T(128)S(1)} %copy-done.6, bf16[1024,1024]{1,0:T(8,128)(2,1)S(1)} %get-tuple-element.74.refs_1_, bf16[1024,1024]{1,0:T(8,128)(2,1)S(1)} %get-tuple-element.75.refs_2_, f32[1024,128]{1,0:T(8,128)} %get-tuple-element.77.refs_3_.refs_7_, ...), custom_call_target="tpu_custom_call" | custom-call | tf_op jit(solution)/shard_map/apply/pallas_call | solution.py:38
  45.0 0.8 copy-done.4
  45.8 2.5 %apply.11 = (f32[1024,128]{1,0:T(8,128)S(1)}, f32[8,128]{1,0:T(8,128)S(1)}) custom-call(f32[3]{0:T(128)S(1)} %copy-done.6, bf16[1024,1024]{1,0:T(8,128)(2,1)S(1)} %get-tuple-element.74.refs_1_, bf16[1024,1024]{1,0:T(8,128)(2,1)S(1)} %get-tuple-element.75.refs_2_, f32[1024,128]{1,0:T(8,128)} %get-tuple-element.92.refs_3_.refs_7_, ...), custom_call_target="tpu_custom_call" | custom-call | tf_op jit(solution)/shard_map/apply/pallas_call | solution.py:38
  48.3 2.5 %collective-permute-done.10.refs_3_.refs_9_ = f32[1024,128]{1,0:T(8,128)S(1)} collective-permute-done((f32[1024,128]{1,0:T(8,128)}, f32[1024,128]{1,0:T(8,128)S(1)}, u32[]{:S(2)}, u32[]{:S(2)}) %collective-permute-start.10) | collective-permute-done | bytes 524320 | tf_op jit(solution)/shard_map/ppermute | solution.py:417
  50.8 1.4 %collective-permute-done.9.refs_2_.refs_6_ = f32[1024,128]{1,0:T(8,128)} collective-permute-done((f32[1024,128]{1,0:T(8,128)}, f32[1024,128]{1,0:T(8,128)}, u32[]{:S(2)}, u32[]{:S(2)}) %collective-permute-start.9) | collective-permute-done | bytes 524320 | tf_op jit(solution)/shard_map/ppermute | solution.py:417
  52.2 0.5 collective-permute-start.12
  53.0 2.2 %collective-permute-start.15 = (f32[1024,128]{1,0:T(8,128)}, f32[1024,128]{1,0:T(8,128)S(1)}, u32[]{:S(2)}, u32[]{:S(2)}) collective-permute-start(f32[1024,128]{1,0:T(8,128)} %get-tuple-element.92.refs_3_.refs_7_), channel_id=1, source_target_pairs={{0,16},{4,20},{8,24},{12,28},{16,0},{20,4},{24,8},{28,12},{1,17},{... | collective-permute-start | bytes 1572872 | tf_op jit(solution)/shard_map/ppermute | solution.py:417
  55.2 3.7 %build_couple.3 = (bf16[1024,1024]{1,0:T(8,128)(2,1)S(1)}, bf16[1024,1024]{1,0:T(8,128)(2,1)S(1)}, f32[8,128]{1,0:T(8,128)S(1)}) custom-call(s32[384]{0:T(512)S(1)} %reshape.15.refs_0_, s32[3,8]{1,0:T(4,128)S(1)} %copy-done.7, f32[3,8,2,128,128]{4,3,2,1,0:T(8,128)} %refs_2_.11, f32[1024,128]{1,0:T(8,128)} %get-tuple-element.68.refs_3_, ...), custom_call_target="tpu_custom_call" | custom-call | tf_op jit(solution)/shard_map/build_couple/pallas_call | solution.py:38
  58.9 0.6 collective-permute-start.13
  59.5 3.7 %build_couple.4 = (bf16[1024,1024]{1,0:T(8,128)(2,1)S(1)}, bf16[1024,1024]{1,0:T(8,128)(2,1)S(1)}, f32[8,128]{1,0:T(8,128)S(1)}) custom-call(s32[384]{0:T(512)S(1)} %reshape.15.refs_0_, s32[3,8]{1,0:T(4,128)S(1)} %copy-done.7, f32[3,8,2,128,128]{4,3,2,1,0:T(8,128)} %refs_2_.11, f32[1024,128]{1,0:T(8,128)} %get-tuple-element.68.refs_3_, ...), custom_call_target="tpu_custom_call" | custom-call | tf_op jit(solution)/shard_map/build_couple/pallas_call | solution.py:38
  63.2 3.9 %build_couple.5 = (bf16[1024,1024]{1,0:T(8,128)(2,1)S(1)}, bf16[1024,1024]{1,0:T(8,128)(2,1)S(1)}, f32[8,128]{1,0:T(8,128)S(1)}) custom-call(s32[384]{0:T(512)S(1)} %reshape.15.refs_0_, s32[3,8]{1,0:T(4,128)S(1)} %copy-done.7, f32[3,8,2,128,128]{4,3,2,1,0:T(8,128)} %refs_2_.11, f32[1024,128]{1,0:T(8,128)} %collective-permute-done.7.refs_5_.refs_3_, ...), custom_call_target="tpu_custom_call" | custom-call | tf_op jit(solution)/shard_map/build_couple/pallas_call | solution.py:38
  67.2 4.9 %apply.12 = (f32[1024,128]{1,0:T(8,128)S(1)}, f32[8,128]{1,0:T(8,128)S(1)}) custom-call(f32[3]{0:T(128)S(1)} %copy-done.6, bf16[1024,1024]{1,0:T(8,128)(2,1)S(1)} %get-tuple-element.89.refs_1_.refs_4_, bf16[1024,1024]{1,0:T(8,128)(2,1)S(1)} %get-tuple-element.90.refs_2_.refs_5_, f32[1024,128]{1,0:T(8,128)} %collective-permute-done.8.refs_1_.refs_3_, ...), custom_call_target="tpu_custom_call" | custom-call | tf_op jit(solution)/shard_map/apply/pallas_call | solution.py:38
  72.0 1.5 %collective-permute-start.21 = (f32[1024,128]{1,0:T(8,128)S(1)}, f32[1024,128]{1,0:T(8,128)S(1)}, u32[]{:S(2)}, u32[]{:S(2)}) collective-permute-start(f32[1024,128]{1,0:T(8,128)S(1)} %get-tuple-element.100.refs_3_), channel_id=1, source_target_pairs={{0,4},{4,0},{8,12},{12,8},{16,20},{20,16},{24,28},{28,24},{1,5},{5... | collective-permute-start | bytes 1572872 | tf_op jit(solution)/shard_map/ppermute | solution.py:417
  73.6 4.2 %collective-permute-done.14.refs_6_ = f32[1024,128]{1,0:T(8,128)} collective-permute-done((f32[1024,128]{1,0:T(8,128)}, f32[1024,128]{1,0:T(8,128)}, u32[]{:S(2)}, u32[]{:S(2)}) %collective-permute-start.14) | collective-permute-done | bytes 524320 | tf_op jit(solution)/shard_map/ppermute | solution.py:417
  78.1 1.3 %collective-permute-done.15.refs_9_ = f32[1024,128]{1,0:T(8,128)S(1)} collective-permute-done((f32[1024,128]{1,0:T(8,128)}, f32[1024,128]{1,0:T(8,128)S(1)}, u32[]{:S(2)}, u32[]{:S(2)}) %collective-permute-start.15) | collective-permute-done | bytes 524320 | tf_op jit(solution)/shard_map/ppermute | solution.py:417
  79.5 4.9 %apply.13 = (f32[1024,128]{1,0:T(8,128)S(1)}, f32[8,128]{1,0:T(8,128)S(1)}) custom-call(f32[3]{0:T(128)S(1)} %copy-done.6, bf16[1024,1024]{1,0:T(8,128)(2,1)S(1)} %get-tuple-element.89.refs_1_.refs_4_, bf16[1024,1024]{1,0:T(8,128)(2,1)S(1)} %get-tuple-element.90.refs_2_.refs_5_, f32[1024,128]{1,0:T(8,128)S(1)} %collective-permute-done.13.refs_3_, ...), custom_call_target="tpu_custom_call" | custom-call | tf_op jit(solution)/shard_map/apply/pallas_call | solution.py:38
  84.3 0.6 collective-permute-start.18
  85.0 1.2 collective-permute-start.17
  86.2 0.9 collective-permute-start.16
  87.1 3.5 %apply.14 = (f32[1024,128]{1,0:T(8,128)S(1)}, f32[8,128]{1,0:T(8,128)S(1)}) custom-call(f32[3]{0:T(128)S(1)} %copy-done.6, bf16[1024,1024]{1,0:T(8,128)(2,1)S(1)} %get-tuple-element.74.refs_1_, bf16[1024,1024]{1,0:T(8,128)(2,1)S(1)} %copy-done.1, f32[1024,128]{1,0:T(8,128)S(1)} %get-tuple-element.100.refs_3_, ...), custom_call_target="tpu_custom_call" | custom-call | flops 1610612736 | bytes 8388608 | tf_op jit(solution)/shard_map/apply/pallas_call | solution.py:38
  90.6 9.3 %collective-permute-done.20.refs_3_ = f32[1024,128]{1,0:T(8,128)S(1)} collective-permute-done((f32[1024,128]{1,0:T(8,128)S(1)}, f32[1024,128]{1,0:T(8,128)S(1)}, u32[]{:S(2)}, u32[]{:S(2)}) %collective-permute-start.20) | collective-permute-done | bytes 524320 | tf_op jit(solution)/shard_map/ppermute | solution.py:417
  99.9 1.9 %apply.15 = (f32[1024,128]{1,0:T(8,128)S(1)}, f32[8,128]{1,0:T(8,128)S(1)}) custom-call(f32[3]{0:T(128)S(1)} %copy-done.6, bf16[1024,1024]{1,0:T(8,128)(2,1)S(1)} %get-tuple-element.93.refs_4_.refs_1_, bf16[1024,1024]{1,0:T(8,128)(2,1)S(1)} %get-tuple-element.94.refs_5_.refs_2_, f32[1024,128]{1,0:T(8,128)S(1)} %collective-permute-done.20.refs_3_, ...), custom_call_target="tpu_custom_call" | custom-call | flops 805306368 | bytes 4194304 | tf_op jit(solution)/shard_map/apply/pallas_call | solution.py:38
  101.9 3.0 %collective-permute-done.19.refs_3_ = f32[1024,128]{1,0:T(8,128)S(1)} collective-permute-done((f32[1024,128]{1,0:T(8,128)S(1)}, f32[1024,128]{1,0:T(8,128)S(1)}, u32[]{:S(2)}, u32[]{:S(2)}) %collective-permute-start.19) | collective-permute-done | bytes 524320 | tf_op jit(solution)/shard_map/ppermute | solution.py:417
  104.9 2.7 %apply.16 = (f32[1024,256]{1,0:T(8,128)}, f32[8,128]{1,0:T(8,128)S(1)}) custom-call(f32[3]{0:T(128)S(1)} %copy-done.6, bf16[1024,1024]{1,0:T(8,128)(2,1)S(1)} %get-tuple-element.85.refs_7_.refs_1_, bf16[1024,1024]{1,0:T(8,128)(2,1)S(1)} %get-tuple-element.86.refs_8_.refs_2_, f32[1024,128]{1,0:T(8,128)S(1)} %collective-permute-done.19.refs_3_, ...), custom_call_target="tpu_custom_call" | custom-call | flops 805306368 | bytes 4194304 | tf_op jit(solution)/shard_map/apply/pallas_call | solution.py:38
  107.7 3.8 %apply.17 = (f32[1024,128]{1,0:T(8,128)S(1)}, f32[8,128]{1,0:T(8,128)S(1)}) custom-call(f32[3]{0:T(128)S(1)} %copy-done.6, bf16[1024,1024]{1,0:T(8,128)(2,1)S(1)} %get-tuple-element.74.refs_1_, bf16[1024,1024]{1,0:T(8,128)(2,1)S(1)} %copy-done.1, f32[1024,128]{1,0:T(8,128)S(1)} %get-tuple-element.99.refs_3_, ...), custom_call_target="tpu_custom_call" | custom-call | flops 1610612736 | bytes 8388608 | tf_op jit(solution)/shard_map/apply/pallas_call | solution.py:38
  111.4 10.1 %collective-permute-done.17.refs_3_ = f32[1024,128]{1,0:T(8,128)S(1)} collective-permute-done((f32[1024,128]{1,0:T(8,128)S(1)}, f32[1024,128]{1,0:T(8,128)S(1)}, u32[]{:S(2)}, u32[]{:S(2)}) %collective-permute-start.17) | collective-permute-done | bytes 524320 | tf_op jit(solution)/shard_map/ppermute | solution.py:417
  121.5 1.9 %apply.18 = (f32[1024,128]{1,0:T(8,128)S(1)}, f32[8,128]{1,0:T(8,128)S(1)}) custom-call(f32[3]{0:T(128)S(1)} %copy-done.6, bf16[1024,1024]{1,0:T(8,128)(2,1)S(1)} %get-tuple-element.93.refs_4_.refs_1_, bf16[1024,1024]{1,0:T(8,128)(2,1)S(1)} %get-tuple-element.94.refs_5_.refs_2_, f32[1024,128]{1,0:T(8,128)S(1)} %collective-permute-done.17.refs_3_, ...), custom_call_target="tpu_custom_call" | custom-call | flops 805306368 | bytes 4194304 | tf_op jit(solution)/shard_map/apply/pallas_call | solution.py:38
  123.5 1.0 collective-permute-done.16.refs_3_
  124.5 3.3 %apply.19 = (f32[1024,256]{1,0:T(8,128)}, f32[8,128]{1,0:T(8,128)}) custom-call(f32[3]{0:T(128)S(1)} %copy-done.6, bf16[1024,1024]{1,0:T(8,128)(2,1)S(1)} %get-tuple-element.85.refs_7_.refs_1_, bf16[1024,1024]{1,0:T(8,128)(2,1)S(1)} %get-tuple-element.86.refs_8_.refs_2_, ...), custom_call_target="tpu_custom_call", output_to_operand_aliasing={{0}: (5, {})} | custom-call | flops 805306368 | bytes 4194304 | tf_op jit(solution)/shard_map/apply/pallas_call | solution.py:38
  (40 shorter events, 1.5 us)
Async XLA Ops:
  0.0 3.1 %collective-permute-start = (f32[1024,256]{1,0:T(8,128)}, f32[1024,256]{1,0:T(8,128)S(1)}, u32[]{:S(2)}, u32[]{:S(2)}) collective-permute-start(f32[1024,256]{1,0:T(8,128)} %refs_0_.13), channel_id=1, source_target_pairs={{0,1},{1,0},{2,3},{3,2},{4,5},{5,4},{6,7},{7,6},{8,9},{9,8},{10,11... | collective-permute-start | bytes 3145736 | tf_op jit(solution)/shard_map/ppermute | solution.py:414
  3.7 18.9 %collective-permute-start.1 = (f32[1024,128]{1,0:T(8,128)S(1)}, f32[1024,128]{1,0:T(8,128)S(1)}, u32[]{:S(2)}, u32[]{:S(2)}) collective-permute-start(f32[1024,128]{1,0:T(8,128)S(1)} %get-tuple-element.64), channel_id=1, source_target_pairs={{0,2},{1,3},{2,0},{3,1},{4,6},{5,7},{6,4},{7,5},{8,10},{9,11},{10,... | collective-permute-start | bytes 1572872 | tf_op jit(solution)/shard_map/ppermute | solution.py:414
  6.5 13.7 %collective-permute-start.2 = (f32[512,128]{1,0:T(8,128)S(1)}, f32[512,128]{1,0:T(8,128)S(1)}, u32[]{:S(2)}, u32[]{:S(2)}) collective-permute-start(f32[512,128]{1,0:T(8,128)S(1)} %bitcast.5), channel_id=1, source_target_pairs={{0,8},{4,12},{8,0},{12,4},{16,24},{20,28},{24,16},{28,20},{1,9},{5... | collective-permute-start | bytes 786440 | tf_op jit(solution)/shard_map/ppermute | solution.py:417
  8.0 14.5 %collective-permute-start.3 = (f32[512,128]{1,0:T(8,128)S(1)}, f32[512,128]{1,0:T(8,128)S(1)}, u32[]{:S(2)}, u32[]{:S(2)}) collective-permute-start(f32[512,128]{1,0:T(8,128)S(1)} %bitcast.4), channel_id=1, source_target_pairs={{0,16},{4,20},{8,24},{12,28},{16,0},{20,4},{24,8},{28,12},{1,17},{... | collective-permute-start | bytes 786440 | tf_op jit(solution)/shard_map/ppermute | solution.py:417
  10.6 25.3 %copy-start.8 = (s32[8,6]{1,0:T(8,128)S(1)}, s32[8,6]{1,0:T(8,128)}, u32[]{:S(2)}) copy-start(s32[8,6]{1,0:T(8,128)} %param.10) | copy-start | bytes 580
  13.9 22.9 %copy-start.6 = (f32[3]{0:T(128)S(1)}, f32[3]{0:T(128)}, u32[]{:S(2)}) copy-start(f32[3]{0:T(128)} %refs_0_.23) | copy-start | bytes 40
  14.0 13.4 %collective-permute-start.7 = (f32[1024,128]{1,0:T(8,128)S(1)}, f32[1024,128]{1,0:T(8,128)}, u32[]{:S(2)}, u32[]{:S(2)}) collective-permute-start(f32[1024,128]{1,0:T(8,128)S(1)} %bitcast.3), channel_id=1, source_target_pairs={{0,4},{4,0},{8,12},{12,8},{16,20},{20,16},{24,28},{28,24},{1,5},{5... | collective-permute-start | bytes 1572872 | tf_op jit(solution)/shard_map/ppermute | solution.py:417
  23.6 11.8 %collective-permute-start.6 = (f32[1024,128]{1,0:T(8,128)S(1)}, f32[1024,128]{1,0:T(8,128)S(1)}, u32[]{:S(2)}, u32[]{:S(2)}) collective-permute-start(f32[1024,128]{1,0:T(8,128)S(1)} %get-tuple-element.72), channel_id=1, source_target_pairs={{0,2},{1,3},{2,0},{3,1},{4,6},{5,7},{6,4},{7,5},{8,10},{9,11},{10,... | collective-permute-start | bytes 1572872 | tf_op jit(solution)/shard_map/ppermute | solution.py:414
  24.1 18.0 %collective-permute-start.4 = (f32[1024,128]{1,0:T(8,128)}, f32[1024,128]{1,0:T(8,128)S(1)}, u32[]{:S(2)}, u32[]{:S(2)}) collective-permute-start(f32[1024,128]{1,0:T(8,128)} %get-tuple-element.68.refs_3_), channel_id=1, source_target_pairs={{0,1},{1,0},{2,3},{3,2},{4,5},{5,4},{6,7},{7,6},{8,9},{9,8},{10,11... | collective-permute-start | bytes 1572872 | tf_op jit(solution)/shard_map/ppermute | solution.py:414
  24.1 26.7 %collective-permute-start.10 = (f32[1024,128]{1,0:T(8,128)}, f32[1024,128]{1,0:T(8,128)S(1)}, u32[]{:S(2)}, u32[]{:S(2)}) collective-permute-start(f32[1024,128]{1,0:T(8,128)} %get-tuple-element.77.refs_3_.refs_7_), channel_id=1, source_target_pairs={{0,16},{4,20},{8,24},{12,28},{16,0},{20,4},{24,8},{28,12},{1,17},{... | collective-permute-start | bytes 1572872 | tf_op jit(solution)/shard_map/ppermute | solution.py:417
  24.5 26.3 %collective-permute-start.8 = (f32[1024,128]{1,0:T(8,128)}, f32[1024,128]{1,0:T(8,128)}, u32[]{:S(2)}, u32[]{:S(2)}) collective-permute-start(f32[1024,128]{1,0:T(8,128)} %get-tuple-element.77.refs_3_.refs_7_), channel_id=1, source_target_pairs={{0,4},{4,0},{8,12},{12,8},{16,20},{20,16},{24,28},{28,24},{1,5},{5... | collective-permute-start | bytes 1572872 | tf_op jit(solution)/shard_map/ppermute | solution.py:417
  27.4 24.8 %collective-permute-start.9 = (f32[1024,128]{1,0:T(8,128)}, f32[1024,128]{1,0:T(8,128)}, u32[]{:S(2)}, u32[]{:S(2)}) collective-permute-start(f32[1024,128]{1,0:T(8,128)} %get-tuple-element.77.refs_3_.refs_7_), channel_id=1, source_target_pairs={{0,8},{4,12},{8,0},{12,4},{16,24},{20,28},{24,16},{28,20},{1,9},{5... | collective-permute-start | bytes 1572872 | tf_op jit(solution)/shard_map/ppermute | solution.py:417
  35.4 16.8 %collective-permute-start.5 = (f32[1024,128]{1,0:T(8,128)}, f32[1024,128]{1,0:T(8,128)}, u32[]{:S(2)}, u32[]{:S(2)}) collective-permute-start(f32[1024,128]{1,0:T(8,128)} %get-tuple-element.68.refs_3_), channel_id=1, source_target_pairs={{0,2},{1,3},{2,0},{3,1},{4,6},{5,7},{6,4},{7,5},{8,10},{9,11},{10,... | collective-permute-start | bytes 1572872 | tf_op jit(solution)/shard_map/ppermute | solution.py:414
  36.8 1.9 %copy-start.3 = (f32[8,6,128,128]{3,2,1,0:T(8,128)S(1)}, f32[8,6,128,128]{3,2,1,0:T(8,128)}, u32[]{:S(2)}) copy-start(f32[8,6,128,128]{3,2,1,0:T(8,128)} %refs_2_.8) | copy-start | bytes 9437188
  42.1 3.7 %copy-start = (bf16[1024,1024]{1,0:T(8,128)(2,1)}, bf16[1024,1024]{1,0:T(8,128)(2,1)S(1)}, u32[]{:S(2)}) copy-start(bf16[1024,1024]{1,0:T(8,128)(2,1)S(1)} %get-tuple-element.75.refs_2_) | copy-start | bytes 6291460
  42.2 2.9 %copy-start.2 = (f32[1024,128]{1,0:T(8,128)}, f32[1024,128]{1,0:T(8,128)S(1)}, u32[]{:S(2)}) copy-start(f32[1024,128]{1,0:T(8,128)S(1)} %collective-permute-done.4.refs_6_.refs_4_) | copy-start | bytes 1572868
  45.0 0.8 copy-start.4
  45.8 6.9 %copy-start.9 = (s32[3,64,2]{1,2,0:T(2,128)S(1)}, s32[3,64,2]{1,2,0:T(2,128)}, u32[]{:S(2)}) copy-start(s32[3,64,2]{1,2,0:T(2,128)} %param.12) | copy-start | bytes 4612
  45.8 9.3 %copy-start.7 = (s32[3,8]{1,0:T(4,128)S(1)}, s32[3,8]{1,0:T(4,128)}, u32[]{:S(2)}) copy-start(s32[3,8]{1,0:T(4,128)} %refs_1_.9) | copy-start | bytes 292
  52.2 2.9 %collective-permute-start.11 = (f32[1024,128]{1,0:T(8,128)}, f32[1024,128]{1,0:T(8,128)}, u32[]{:S(2)}, u32[]{:S(2)}) collective-permute-start(f32[1024,128]{1,0:T(8,128)} %collective-permute-done.5.refs_5_), channel_id=1, source_target_pairs={{0,1},{1,0},{2,3},{3,2},{4,5},{5,4},{6,7},{7,6},{8,9},{9,8},{10,11... | collective-permute-start | bytes 1572872 | tf_op jit(solution)/shard_map/ppermute | solution.py:414
  52.2 11.0 %collective-permute-start.12 = (f32[1024,128]{1,0:T(8,128)}, f32[1024,128]{1,0:T(8,128)}, u32[]{:S(2)}, u32[]{:S(2)}) collective-permute-start(f32[1024,128]{1,0:T(8,128)} %collective-permute-done.7.refs_5_.refs_3_), channel_id=1, source_target_pairs={{0,1},{1,0},{2,3},{3,2},{4,5},{5,4},{6,7},{7,6},{8,9},{9,8},{10,11... | collective-permute-start | bytes 1572872 | tf_op jit(solution)/shard_map/ppermute | solution.py:414
  52.7 25.1 %collective-permute-start.14 = (f32[1024,128]{1,0:T(8,128)}, f32[1024,128]{1,0:T(8,128)}, u32[]{:S(2)}, u32[]{:S(2)}) collective-permute-start(f32[1024,128]{1,0:T(8,128)} %get-tuple-element.92.refs_3_.refs_7_), channel_id=1, source_target_pairs={{0,8},{4,12},{8,0},{12,4},{16,24},{20,28},{24,16},{28,20},{1,9},{5... | collective-permute-start | bytes 1572872 | tf_op jit(solution)/shard_map/ppermute | solution.py:417
  53.0 26.5 %collective-permute-start.15 = (f32[1024,128]{1,0:T(8,128)}, f32[1024,128]{1,0:T(8,128)S(1)}, u32[]{:S(2)}, u32[]{:S(2)}) collective-permute-start(f32[1024,128]{1,0:T(8,128)} %get-tuple-element.92.refs_3_.refs_7_), channel_id=1, source_target_pairs={{0,16},{4,20},{8,24},{12,28},{16,0},{20,4},{24,8},{28,12},{1,17},{... | collective-permute-start | bytes 1572872 | tf_op jit(solution)/shard_map/ppermute | solution.py:417
  58.9 20.6 %collective-permute-start.13 = (f32[1024,128]{1,0:T(8,128)}, f32[1024,128]{1,0:T(8,128)S(1)}, u32[]{:S(2)}, u32[]{:S(2)}) collective-permute-start(f32[1024,128]{1,0:T(8,128)} %get-tuple-element.92.refs_3_.refs_7_), channel_id=1, source_target_pairs={{0,4},{4,0},{8,12},{12,8},{16,20},{20,16},{24,28},{28,24},{1,5},{5... | collective-permute-start | bytes 1572872 | tf_op jit(solution)/shard_map/ppermute | solution.py:417
  63.2 3.9 %copy-start.5 = (f32[1024,128]{1,0:T(8,128)S(1)}, f32[1024,128]{1,0:T(8,128)}, u32[]{:S(2)}) copy-start(f32[1024,128]{1,0:T(8,128)} %copy-done.4) | copy-start | bytes 1572868
  72.0 14.1 %collective-permute-start.21 = (f32[1024,128]{1,0:T(8,128)S(1)}, f32[1024,128]{1,0:T(8,128)S(1)}, u32[]{:S(2)}, u32[]{:S(2)}) collective-permute-start(f32[1024,128]{1,0:T(8,128)S(1)} %get-tuple-element.100.refs_3_), channel_id=1, source_target_pairs={{0,4},{4,0},{8,12},{12,8},{16,20},{20,16},{24,28},{28,24},{1,5},{5... | collective-permute-start | bytes 1572872 | tf_op jit(solution)/shard_map/ppermute | solution.py:417
  73.6 26.3 %collective-permute-start.20 = (f32[1024,128]{1,0:T(8,128)S(1)}, f32[1024,128]{1,0:T(8,128)S(1)}, u32[]{:S(2)}, u32[]{:S(2)}) collective-permute-start(f32[1024,128]{1,0:T(8,128)S(1)} %get-tuple-element.100.refs_3_), channel_id=1, source_target_pairs={{0,8},{4,12},{8,0},{12,4},{16,24},{20,28},{24,16},{28,20},{1,9},{5... | collective-permute-start | bytes 1572872 | tf_op jit(solution)/shard_map/ppermute | solution.py:417
  77.8 27.1 %collective-permute-start.19 = (f32[1024,128]{1,0:T(8,128)S(1)}, f32[1024,128]{1,0:T(8,128)S(1)}, u32[]{:S(2)}, u32[]{:S(2)}) collective-permute-start(f32[1024,128]{1,0:T(8,128)S(1)} %get-tuple-element.100.refs_3_), channel_id=1, source_target_pairs={{0,16},{4,20},{8,24},{12,28},{16,0},{20,4},{24,8},{28,12},{1,17},{... | collective-permute-start | bytes 1572872 | tf_op jit(solution)/shard_map/ppermute | solution.py:417
  79.4 7.6 %copy-start.1 = (bf16[1024,1024]{1,0:T(8,128)(2,1)S(1)}, bf16[1024,1024]{1,0:T(8,128)(2,1)}, u32[]{:S(2)}) copy-start(bf16[1024,1024]{1,0:T(8,128)(2,1)} %copy-done) | copy-start | bytes 6291460
  84.3 23.3 %collective-permute-start.18 = (f32[1024,128]{1,0:T(8,128)S(1)}, f32[1024,128]{1,0:T(8,128)S(1)}, u32[]{:S(2)}, u32[]{:S(2)}) collective-permute-start(f32[1024,128]{1,0:T(8,128)S(1)} %get-tuple-element.99.refs_3_), channel_id=1, source_target_pairs={{0,4},{4,0},{8,12},{12,8},{16,20},{20,16},{24,28},{28,24},{1,5},{5... | collective-permute-start | bytes 1572872 | tf_op jit(solution)/shard_map/ppermute | solution.py:417
  85.0 36.5 %collective-permute-start.17 = (f32[1024,128]{1,0:T(8,128)S(1)}, f32[1024,128]{1,0:T(8,128)S(1)}, u32[]{:S(2)}, u32[]{:S(2)}) collective-permute-start(f32[1024,128]{1,0:T(8,128)S(1)} %get-tuple-element.99.refs_3_), channel_id=1, source_target_pairs={{0,8},{4,12},{8,0},{12,4},{16,24},{20,28},{24,16},{28,20},{1,9},{5... | collective-permute-start | bytes 1572872 | tf_op jit(solution)/shard_map/ppermute | solution.py:417
  86.2 38.3 %collective-permute-start.16 = (f32[1024,128]{1,0:T(8,128)S(1)}, f32[1024,128]{1,0:T(8,128)S(1)}, u32[]{:S(2)}, u32[]{:S(2)}) collective-permute-start(f32[1024,128]{1,0:T(8,128)S(1)} %get-tuple-element.99.refs_3_), channel_id=1, source_target_pairs={{0,16},{4,20},{8,24},{12,28},{16,0},{20,4},{24,8},{28,12},{1,17},{... | collective-permute-start | bytes 1572872 | tf_op jit(solution)/shard_map/ppermute | solution.py:417

commit v3 on v2

--- a/solution.py
+++ b/solution.py
@@ -26,27 +26,29 @@
 
 def call(
     token, kernel, operands, specs, out_specs, out_shape, scratch, name,
-    flops=0, nbytes=0, aliases=None, waits=(),
+    aliases=None, waits=(), last=False,
 ):
     ins, outs = len(operands), len(out_shape)
     first = ins + 1 + len(waits)
+    given = [] if last else [jax.ShapeDtypeStruct(token.shape, f32)]
 
     def body(*refs):
-        refs[first + outs][...] = jnp.zeros(token.shape, f32)
-        kernel(*refs[:ins], *refs[first:first + outs], *refs[first + outs + 1:])
-
-    *results, token = pl.pallas_call(
+        for ref in refs[first + outs:first + outs + len(given)]:
+            ref[...] = jnp.zeros(token.shape, f32)
+        kernel(*refs[:ins], *refs[first:first + outs], *refs[first + outs + len(given):])
+
+    results = pl.pallas_call(
         body,
         in_specs=[*specs, *[pl.BlockSpec(memory_space=pl.ANY)] * (1 + len(waits))],
-        out_specs=[*out_specs, VMEM],
-        out_shape=[*out_shape, jax.ShapeDtypeStruct(token.shape, f32)],
+        out_specs=[*out_specs, *[VMEM] * len(given)],
+        out_shape=[*out_shape, *given],
         scratch_shapes=scratch,
         input_output_aliases=aliases or {},
         compiler_params=PARAMS,
-        cost_estimate=pl.CostEstimate(flops=flops, bytes_accessed=nbytes, transcendentals=0),
+        cost_estimate=pl.CostEstimate(flops=0, bytes_accessed=0, transcendentals=0),
         name=name,
     )(*operands, token, *waits)
-    return results, token
+    return results[:outs], (None if last else results[outs])
 
 
 def in_hbm(x):
@@ -178,7 +180,7 @@
     return out[:-2], out[-2], out[-1], token
 
 
-def meet(token, parts, blocks=()):
+def meet(token, parts, blocks=(), waits=()):
     height = blocks[0].shape[0] if blocks else 0
 
     def kernel(*refs):
@@ -193,7 +195,7 @@
     if blocks:
         shapes.append(array(len(blocks) * height, blocks[0].shape[1]))
     ins = [*parts, *blocks]
-    return call(token, kernel, ins, [VMEM] * len(ins), [VMEM] * len(shapes), shapes, [], "meet")
+    return call(token, kernel, ins, [VMEM] * len(ins), [VMEM] * len(shapes), shapes, [], "meet", waits=waits)
 
 
 def touch(token, waits):
@@ -322,42 +324,51 @@
     base = [refs.pop(0) for _ in range(base_count)]
     if column is not None and column > 0:
         refs.pop(0)
-    out_ref, w_buf, acc, sem = refs
+    out_ref, w_buf, acc, sems = refs
     rows, width = acc.shape
-    for m, (hi, lo, chunks) in enumerate(mats):
+    tiles = 1 if column is None else 4
+    height = rows // tiles
+    if step is not None:
+        s_sum, s_base = scales(bounds_ref, step, (1, width))
+    for m, (_, _, chunks) in enumerate(mats):
         at = 0
         for chunk in chunks:
             u_hi, u_lo = split(chunk[...])
-            w_buf[at:at + chunk.shape[0], :width] = u_hi
-            w_buf[at:at + chunk.shape[0], width:] = u_lo
+            w_buf[m, at:at + chunk.shape[0], :width] = u_hi
+            w_buf[m, at:at + chunk.shape[0], width:] = u_lo
             at += chunk.shape[0]
-        both = dot(hi[...], w_buf[...])
-        part = both[:, :width] + both[:, width:] + dot(lo[...], w_buf[:, :width])
-        if m == 0:
-            acc[...] = part
+    copies = []
+    for t in range(tiles):
+        tile = slice(t * height, (t + 1) * height)
+        for m, (hi, lo, _) in enumerate(mats):
+            both = dot(hi[tile], w_buf[m])
+            part = both[:, :width] + both[:, width:] + dot(lo[tile], w_buf[m, :, :width])
+            if m == 0:
+                acc[tile] = part
+            else:
+                acc[tile] += part
+        result = acc[tile]
+        if step is not None:
+            result = result * s_sum
+        if partial is not None:
+            result = result + partial[tile]
+        for chunk in base:
+            result = result + chunk[tile] * s_base
+        if column is None:
+            out_ref[tile] = result
         else:
-            acc[...] += part
-    if step is not None:
-        s_sum, s_base = scales(bounds_ref, step, (1, width))
-        acc[...] = acc[...] * s_sum
-    if partial is not None:
-        acc[...] += partial[...]
-    at = 0
-    for chunk in base:
-        piece = slice(at, at + chunk.shape[0])
-        acc[piece] += chunk[...] * s_base
-        at += chunk.shape[0]
-    if column is None:
-        out_ref[...] = acc[...]
-    else:
-        c = pltpu.make_async_copy(acc, out_ref.at[:, column:column + width], sem)
-        c.start()
+            acc[tile] = result
+            dst = out_ref.at[tile, column:column + width]
+            copies.append(pltpu.make_async_copy(acc.at[tile], dst, sems.at[t]))
+            copies[-1].start()
+    for c in copies:
         c.wait()
 
 
 def apply(
     token, bounds, mats, step=None, partial=None, base=(), column=None, out_width=None, into=None,
-    late=False, waits=()):
+    waits=(), last=False,
+):
     rows = mats[0][0].shape[0]
     width = mats[0][2][0].shape[1]
     operands = [bounds]
@@ -382,15 +393,11 @@
     (out,), token = call(
         token, kernel, operands, specs, [VMEM if column is None else HBM], [shape],
         [
-            pltpu.VMEM((rows, 2 * width), bf16),
+            pltpu.VMEM((len(mats), rows, 2 * width), bf16),
             pltpu.VMEM((rows, width), f32),
-            pltpu.SemaphoreType.DMA,
+            pltpu.SemaphoreType.DMA((8,)),
         ],
-        "apply",
-        len(mats) * 6 * rows * rows * width if late else 0,
-        len(mats) * rows * rows * 4 if late else 0,
-        aliases,
-        waits,
+        "apply", aliases, waits, last,
     )
     return out, token
 
@@ -447,7 +454,6 @@
     (total, joined), token = meet(token, [own_first, *came], [shares[k] for k in far])
     later = [to_band(gate(c, token), mask) for c, mask in zip(second, masks)]
     field = [total]
-    held = {0: joined, 1: to_band(joined, 1)}
     passed = [to_band(joined, mask) for mask in masks]
 
     def send(part, after=None):
@@ -458,21 +464,24 @@
         out, token = apply(token, bounds, terms, *rest, **options)
         return out
 
-    arrived = [send(total)]
-    (total,), token = meet(token, [own_second, *later])
+    (total,), token = meet(token, [own_second, *later], (), [shares[k] for k in near])
     field.append(total)
+    arrived = [send(field[0], token)]
     local_parts, token = build_local(token, local_blocks, local_cols.reshape(-1), bounds)
-    waits = [shares[k] for k in near] + [held[1]]
+    waits = []
     partial = [part_sum([(*local_parts, [field[0]])], 1, waits=waits)]
     partial.append(part_sum([(*local_parts, [field[1]])], 1))
     token = touch(token, [arrived[0][k] for k in slots])
 
-    for mask, x in zip(masks, passed):
+    total = gate(total, token)
+    arrived.append({k: exchange(total, k) for k in far})
+
+    held = {}
+    for mask, x in zip([0, *masks], [joined, *passed]):
         held[mask] = gate(x, token)
         held[mask ^ 1] = to_band(held[mask], 1)
     for k in near:
         shares[k] = gate(shares[k], token)
-    total = gate(total, token)
     size = coupling_blocks.shape[-1]
     mats = {}
     for k in far + near:
@@ -482,8 +491,8 @@
             at = far.index(k) * heights[k] * stored * size
             places = [(x, at, heights[k], m) for m, x in held.items()]
         mats[k], token = build_couple(token, k, by_bit, flat_cols, partners, blocks, places)
-        if k == far[0]:
-            arrived.append(send(total, token))
+        if k == far[0] and near:
+            arrived[1].update({n: exchange(gate(total, token), n) for n in near})
     first = []
     for h in range(2):
         terms = [(*mats[k], [arrived[h][k]]) for k in slots]
@@ -492,11 +501,11 @@
     out = None
     for h in range(2):
         terms = [(*local_parts, [first[h]])] + [(*mats[k], [arrived[h][k]]) for k in near]
-        early = part_sum(terms, 2, None, [field[h]], late=True)
+        early = part_sum(terms, 2, None, [field[h]])
         for k in far[:-1]:
-            early = part_sum([(*mats[k], [arrived[h][k]])], 2, early, late=True)
+            early = part_sum([(*mats[k], [arrived[h][k]])], 2, early)
         k = far[-1]
-        out = part_sum([(*mats[k], [arrived[h][k]])], 2, early, (), h * half, band, out, late=True)
+        out = part_sum([(*mats[k], [arrived[h][k]])], 2, early, (), h * half, band, out, last=h == 1)
     return out
 
 

time: 129 us -> 127 us (0.984)
  starting transfers between devices: 21.2 us -> 25.9 us
  waiting for transfers between devices: 48 us -> 43.4 us
  Pallas kernels: 55.4 us -> 52.7 us
    ppermute x15, waiting for transfers between devices: 41.3 us -> 36.4 us  [to_row(): return lax.ppermute(x, 'rows', [(i, i ^ 1 << bit) for i in range(n_rows)])]
    ppermute x15, starting transfers between devices: 16.3 us -> 20.8 us  [to_row(): return lax.ppermute(x, 'rows', [(i, i ^ 1 << bit) for i in range(n_rows)])]
    pallas_call x20, Pallas kernels: 55.4 us -> 52.7 us  [call(): pl.pallas_call(body, in_specs=[*specs, *[pl.BlockSpec(memory_space=pl.ANY...]
    unnamed x21 -> x29, local copies, waits for them, and re-layouts: 2.84 us -> 3.63 us
  transfers between devices with their start and end apart: 22 -> 22, of which waited for: 12 -> 11; matrix products, arithmetic and copies ran while one was open for 0% -> 0% of each run, Pallas kernels for 40% -> 39%
where the time goes in v3:
time: 127 us; the launch traced here: 126 us
  Pallas kernels  52.7 us (41%)
  waiting for transfers between devices  43.4 us (34%)
  starting transfers between devices  25.9 us (20%)
  local copies, waits for them, and re-layouts  3.86 us (3%)
    pallas_call x20, Pallas kernels, call(): pl.pallas_call(body, in_specs=[*specs, *[pl.BlockSpec(memory_space=pl.ANY...  52.7 us
    ppermute x15, waiting for transfers between devices, to_row(): return lax.ppermute(x, 'rows', [(i, i ^ 1 << bit) for i in range(n_rows)])  36.4 us
    ppermute x15, starting transfers between devices, to_row(): return lax.ppermute(x, 'rows', [(i, i ^ 1 << bit) for i in range(n_rows)])  20.8 us
    ppermute x7, waiting for transfers between devices, to_band(): return lax.ppermute(x, 'bands', [(i, i ^ mask) for i in range(n_bands)])  6.95 us
    ppermute x7, starting transfers between devices, to_band(): return lax.ppermute(x, 'bands', [(i, i ^ mask) for i in range(n_bands)])  5.1 us
    unnamed x29, local copies, waits for them, and re-layouts  3.63 us
  transfers between devices with their start and end apart: 22, of which 11 were waited for; matrix products, arithmetic and copies ran while one was open for 0% of the time, Pallas kernels for 39%

profile of v3, /device:TPU:0, one launch (start us, length us, event | category | flops | bytes accessed | tf_op | source)
XLA Modules:
  0.0 126.3 jit_solution(3698194535625124292)
XLA Ops:
  0.5 2.6 %begin.1 = (f32[1024,128]{1,0:T(8,128)S(1)}, f32[256,128]{1,0:T(8,128)S(1)}, f32[4,2,128,128]{3,2,1,0:T(8,128)S(1)}, f32[2,2,128,128]{3,2,1,0:T(8,128)S(1)}, f32...) custom-call(s32[3,8]{1,0:T(4,128)} %refs_1_.9, f32[1024,256]{1,0:T(8,128)} %refs_0_.13, f32[1024,1024]{1,0:T(8,128)} %refs_2_.7, ...), custom_call_target="tpu_custom_call" | custom-call | tf_op jit(solution)/shard_map/begin/pallas_call | solution.py:40
  3.1 0.6 rotate_first.1
  3.6 2.8 %collective-permute-start.1 = (f32[1024,128]{1,0:T(8,128)S(1)}, f32[1024,128]{1,0:T(8,128)S(1)}, u32[]{:S(2)}, u32[]{:S(2)}) collective-permute-start(f32[1024,128]{1,0:T(8,128)S(1)} %get-tuple-element.65), channel_id=1, source_target_pairs={{0,2},{1,3},{2,0},{3,1},{4,6},{5,7},{6,4},{7,5},{8,10},{9,11},{10,... | collective-permute-start | bytes 1572872 | tf_op jit(solution)/shard_map/ppermute | solution.py:421
  6.5 1.6 %collective-permute-start.2 = (f32[512,128]{1,0:T(8,128)S(1)}, f32[512,128]{1,0:T(8,128)S(1)}, u32[]{:S(2)}, u32[]{:S(2)}) collective-permute-start(f32[512,128]{1,0:T(8,128)S(1)} %bitcast.5), channel_id=1, source_target_pairs={{0,8},{4,12},{8,0},{12,4},{16,24},{20,28},{24,16},{28,20},{1,9},{5... | collective-permute-start | bytes 786440 | tf_op jit(solution)/shard_map/ppermute | solution.py:424
  8.0 2.6 %collective-permute-start.3 = (f32[512,128]{1,0:T(8,128)S(1)}, f32[512,128]{1,0:T(8,128)S(1)}, u32[]{:S(2)}, u32[]{:S(2)}) collective-permute-start(f32[512,128]{1,0:T(8,128)S(1)} %bitcast.4), channel_id=1, source_target_pairs={{0,16},{4,20},{8,24},{12,28},{16,0},{20,4},{24,8},{28,12},{1,17},{... | collective-permute-start | bytes 786440 | tf_op jit(solution)/shard_map/ppermute | solution.py:424
  10.6 3.3 %rotate_rest.1 = (f32[1024,128]{1,0:T(8,128)S(1)}, f32[1024,128]{1,0:T(8,128)S(1)}, f32[1024,128]{1,0:T(8,128)S(1)}, f32[8,128]{1,0:T(8,128)S(1)}) custom-call(f32[1024,256]{1,0:T(8,128)} %refs_0_.13, f32[1024,256]{1,0:T(8,128)S(1)} %collective-permute-done.refs_1_, f32[1024,1024]{1,0:T(8,128)} %refs_2_.7, f32[8,128]{1,0:T(8,128)S(1)} %get-tuple-element.63.refs_3_), custom_call_target="tpu_custom_call" | custom-call | tf_op jit(solution)/shard_map/rotate_rest/pallas_call | solution.py:40
  13.9 1.6 %collective-permute-start.5 = (f32[1024,128]{1,0:T(8,128)S(1)}, f32[1024,128]{1,0:T(8,128)}, u32[]{:S(2)}, u32[]{:S(2)}) collective-permute-start(f32[1024,128]{1,0:T(8,128)S(1)} %bitcast.3), channel_id=1, source_target_pairs={{0,4},{4,0},{8,12},{12,8},{16,20},{20,16},{24,28},{28,24},{1,5},{5... | collective-permute-start | bytes 1572872 | tf_op jit(solution)/shard_map/ppermute | solution.py:424
  15.5 4.6 %collective-permute-done.2.refs_2_ = f32[512,128]{1,0:T(8,128)S(1)} collective-permute-done((f32[512,128]{1,0:T(8,128)S(1)}, f32[512,128]{1,0:T(8,128)S(1)}, u32[]{:S(2)}, u32[]{:S(2)}) %collective-permute-start.2) | collective-permute-done | bytes 262176 | tf_op jit(solution)/shard_map/ppermute | solution.py:424
  20.1 2.3 %collective-permute-done.3.refs_3_ = f32[512,128]{1,0:T(8,128)S(1)} collective-permute-done((f32[512,128]{1,0:T(8,128)S(1)}, f32[512,128]{1,0:T(8,128)S(1)}, u32[]{:S(2)}, u32[]{:S(2)}) %collective-permute-start.3) | collective-permute-done | bytes 262176 | tf_op jit(solution)/shard_map/ppermute | solution.py:424
  22.5 1.1 meet.2
  23.6 0.5 collective-permute-start.4
  24.6 2.6 %collective-permute-start.8 = (f32[1024,128]{1,0:T(8,128)}, f32[1024,128]{1,0:T(8,128)S(1)}, u32[]{:S(2)}, u32[]{:S(2)}) collective-permute-start(f32[1024,128]{1,0:T(8,128)} %get-tuple-element.84.refs_3_.refs_7_), channel_id=1, source_target_pairs={{0,16},{4,20},{8,24},{12,28},{16,0},{20,4},{24,8},{28,12},{1,17},{... | collective-permute-start | bytes 1572872 | tf_op jit(solution)/shard_map/ppermute | solution.py:424
  27.3 6.9 %collective-permute-done.4.refs_1_ = f32[1024,128]{1,0:T(8,128)S(1)} collective-permute-done((f32[1024,128]{1,0:T(8,128)S(1)}, f32[1024,128]{1,0:T(8,128)S(1)}, u32[]{:S(2)}, u32[]{:S(2)}) %collective-permute-start.4) | collective-permute-done | bytes 524320 | tf_op jit(solution)/shard_map/ppermute | solution.py:421
  34.4 0.8 copy-done.3
  35.1 1.6 %collective-permute-start.6 = (f32[1024,128]{1,0:T(8,128)}, f32[1024,128]{1,0:T(8,128)}, u32[]{:S(2)}, u32[]{:S(2)}) collective-permute-start(f32[1024,128]{1,0:T(8,128)} %get-tuple-element.84.refs_3_.refs_7_), channel_id=1, source_target_pairs={{0,4},{4,0},{8,12},{12,8},{16,20},{20,16},{24,28},{28,24},{1,5},{5... | collective-permute-start | bytes 1572872 | tf_op jit(solution)/shard_map/ppermute | solution.py:424
  36.7 0.6 collective-permute-start.10
  37.5 1.9 %copy-done.2 = f32[8,6,128,128]{3,2,1,0:T(8,128)S(1)} copy-done((f32[8,6,128,128]{3,2,1,0:T(8,128)S(1)}, f32[8,6,128,128]{3,2,1,0:T(8,128)}, u32[]{:S(2)}) %copy-start.2) | copy-done | bytes 3145752
  39.3 3.4 %build_local.1 = (bf16[1024,1024]{1,0:T(8,128)(2,1)S(1)}, bf16[1024,1024]{1,0:T(8,128)(2,1)S(1)}, f32[8,128]{1,0:T(8,128)S(1)}) custom-call(s32[48]{0:T(128)S(1)} %reshape.18.refs_0_, f32[3]{0:T(128)S(1)} %copy-done.10, f32[8,6,128,128]{3,2,1,0:T(8,128)S(1)} %copy-done.2, f32[8,128]{1,0:T(8,128)S(1)} %get-tuple-element.76.refs_3_), custom_call_target="tpu_custom_call" | custom-call | tf_op jit(solution)/shard_map/build_local/pallas_call | solution.py:40
  42.8 2.9 %apply.10 = (f32[1024,128]{1,0:T(8,128)S(1)}, f32[8,128]{1,0:T(8,128)S(1)}) custom-call(f32[3]{0:T(128)S(1)} %copy-done.10, bf16[1024,1024]{1,0:T(8,128)(2,1)S(1)} %get-tuple-element.77.refs_1_, bf16[1024,1024]{1,0:T(8,128)(2,1)S(1)} %get-tuple-element.78.refs_2_, f32[1024,128]{1,0:T(8,128)} %get-tuple-element.84.refs_3_.refs_7_, ...), custom_call_target="tpu_custom_call" | custom-call | tf_op jit(solution)/shard_map/apply/pallas_call | solution.py:40
  45.8 2.0 %apply.11 = (f32[1024,128]{1,0:T(8,128)S(1)}, f32[8,128]{1,0:T(8,128)S(1)}) custom-call(f32[3]{0:T(128)S(1)} %copy-done.10, bf16[1024,1024]{1,0:T(8,128)(2,1)S(1)} %get-tuple-element.77.refs_1_, bf16[1024,1024]{1,0:T(8,128)(2,1)S(1)} %get-tuple-element.78.refs_2_, f32[1024,128]{1,0:T(8,128)S(1)} %copy-done.4, f32[8,128]{1,0:T(8,128)S(1)} %get-tuple-element.82.refs_4_), custom_call_target="tpu_custom_call" | custom-call | tf_op jit(solution)/shard_map/apply/pallas_call | solution.py:40
  47.8 0.8 copy-done.6
  48.6 0.7 collective-permute-done.8.refs_3_.refs_9_
  49.4 0.5 collective-permute-start.9
  50.2 1.9 %collective-permute-start.14 = (f32[1024,128]{1,0:T(8,128)}, f32[1024,128]{1,0:T(8,128)S(1)}, u32[]{:S(2)}, u32[]{:S(2)}) collective-permute-start(f32[1024,128]{1,0:T(8,128)} %copy-done.3), channel_id=1, source_target_pairs={{0,8},{4,12},{8,0},{12,4},{16,24},{20,28},{24,16},{28,20},{1,9},{5... | collective-permute-start | bytes 1572872 | tf_op jit(solution)/shard_map/ppermute | solution.py:424
  52.1 1.6 %collective-permute-start.15 = (f32[1024,128]{1,0:T(8,128)}, f32[1024,128]{1,0:T(8,128)S(1)}, u32[]{:S(2)}, u32[]{:S(2)}) collective-permute-start(f32[1024,128]{1,0:T(8,128)} %copy-done.3), channel_id=1, source_target_pairs={{0,16},{4,20},{8,24},{12,28},{16,0},{20,4},{24,8},{28,12},{1,17},{... | collective-permute-start | bytes 1572872 | tf_op jit(solution)/shard_map/ppermute | solution.py:424
  53.8 3.7 %build_couple.3 = (bf16[1024,1024]{1,0:T(8,128)(2,1)S(1)}, bf16[1024,1024]{1,0:T(8,128)(2,1)S(1)}, f32[8,128]{1,0:T(8,128)S(1)}) custom-call(s32[384]{0:T(512)S(1)} %reshape.15.refs_0_, s32[3,8]{1,0:T(4,128)S(1)} %copy-done.11, f32[3,8,2,128,128]{4,3,2,1,0:T(8,128)} %refs_2_.11, f32[1024,128]{1,0:T(8,128)} %get-tuple-element.85.refs_3_, ...), custom_call_target="tpu_custom_call" | custom-call | tf_op jit(solution)/shard_map/build_couple/pallas_call | solution.py:40
  57.5 0.6 collective-permute-start.13
  58.1 3.7 %build_couple.4 = (bf16[1024,1024]{1,0:T(8,128)(2,1)S(1)}, bf16[1024,1024]{1,0:T(8,128)(2,1)S(1)}, f32[8,128]{1,0:T(8,128)S(1)}) custom-call(s32[384]{0:T(512)S(1)} %reshape.15.refs_0_, s32[3,8]{1,0:T(4,128)S(1)} %copy-done.11, f32[3,8,2,128,128]{4,3,2,1,0:T(8,128)} %refs_2_.11, f32[1024,128]{1,0:T(8,128)} %get-tuple-element.85.refs_3_, ...), custom_call_target="tpu_custom_call" | custom-call | tf_op jit(solution)/shard_map/build_couple/pallas_call | solution.py:40
  61.8 3.9 %build_couple.5 = (bf16[1024,1024]{1,0:T(8,128)(2,1)S(1)}, bf16[1024,1024]{1,0:T(8,128)(2,1)S(1)}, f32[8,128]{1,0:T(8,128)S(1)}) custom-call(s32[384]{0:T(512)S(1)} %reshape.15.refs_0_, s32[3,8]{1,0:T(4,128)S(1)} %copy-done.11, f32[3,8,2,128,128]{4,3,2,1,0:T(8,128)} %refs_2_.11, f32[1024,128]{1,0:T(8,128)} %collective-permute-done.5.refs_3_, ...), custom_call_target="tpu_custom_call" | custom-call | tf_op jit(solution)/shard_map/build_couple/pallas_call | solution.py:40
  65.7 4.9 %apply.12 = (f32[1024,128]{1,0:T(8,128)S(1)}, f32[8,128]{1,0:T(8,128)S(1)}) custom-call(f32[3]{0:T(128)S(1)} %copy-done.10, bf16[1024,1024]{1,0:T(8,128)(2,1)S(1)} %get-tuple-element.92.refs_1_.refs_4_, bf16[1024,1024]{1,0:T(8,128)(2,1)S(1)} %get-tuple-element.93.refs_2_.refs_5_, f32[1024,128]{1,0:T(8,128)} %collective-permute-done.6.refs_1_.refs_3_, ...), custom_call_target="tpu_custom_call" | custom-call | tf_op jit(solution)/shard_map/apply/pallas_call | solution.py:40
  70.7 1.6 %collective-permute-start.21 = (f32[1024,128]{1,0:T(8,128)S(1)}, f32[1024,128]{1,0:T(8,128)S(1)}, u32[]{:S(2)}, u32[]{:S(2)}) collective-permute-start(f32[1024,128]{1,0:T(8,128)S(1)} %get-tuple-element.103.refs_3_), channel_id=1, source_target_pairs={{0,4},{4,0},{8,12},{12,8},{16,20},{20,16},{24,28},{28,24},{1,5},{5... | collective-permute-start | bytes 1572872 | tf_op jit(solution)/shard_map/ppermute | solution.py:424
  72.2 0.5 collective-permute-start.20
  72.8 2.6 %collective-permute-done.14.refs_6_ = f32[1024,128]{1,0:T(8,128)S(1)} collective-permute-done((f32[1024,128]{1,0:T(8,128)}, f32[1024,128]{1,0:T(8,128)S(1)}, u32[]{:S(2)}, u32[]{:S(2)}) %collective-permute-start.14) | collective-permute-done | bytes 524320 | tf_op jit(solution)/shard_map/ppermute | solution.py:424
  75.4 2.0 %collective-permute-start.19 = (f32[1024,128]{1,0:T(8,128)S(1)}, f32[1024,128]{1,0:T(8,128)S(1)}, u32[]{:S(2)}, u32[]{:S(2)}) collective-permute-start(f32[1024,128]{1,0:T(8,128)S(1)} %get-tuple-element.103.refs_3_), channel_id=1, source_target_pairs={{0,16},{4,20},{8,24},{12,28},{16,0},{20,4},{24,8},{28,12},{1,17},{... | collective-permute-start | bytes 1572872 | tf_op jit(solution)/shard_map/ppermute | solution.py:424
  77.3 1.6 %collective-permute-done.15.refs_9_ = f32[1024,128]{1,0:T(8,128)S(1)} collective-permute-done((f32[1024,128]{1,0:T(8,128)}, f32[1024,128]{1,0:T(8,128)S(1)}, u32[]{:S(2)}, u32[]{:S(2)}) %collective-permute-start.15) | collective-permute-done | bytes 524320 | tf_op jit(solution)/shard_map/ppermute | solution.py:424
  78.9 4.4 %apply.13 = (f32[1024,128]{1,0:T(8,128)S(1)}, f32[8,128]{1,0:T(8,128)S(1)}) custom-call(f32[3]{0:T(128)S(1)} %copy-done.10, bf16[1024,1024]{1,0:T(8,128)(2,1)S(1)} %get-tuple-element.92.refs_1_.refs_4_, bf16[1024,1024]{1,0:T(8,128)(2,1)S(1)} %get-tuple-element.93.refs_2_.refs_5_, f32[1024,128]{1,0:T(8,128)S(1)} %collective-permute-done.13.refs_3_, ...), custom_call_target="tpu_custom_call" | custom-call | tf_op jit(solution)/shard_map/apply/pallas_call | solution.py:40
  83.7 1.0 collective-permute-start.17
  84.7 0.8 collective-permute-start.16
  85.5 3.7 %apply.14 = (f32[1024,128]{1,0:T(8,128)S(1)}, f32[8,128]{1,0:T(8,128)S(1)}) custom-call(f32[3]{0:T(128)S(1)} %copy-done.10, bf16[1024,1024]{1,0:T(8,128)(2,1)S(1)} %get-tuple-element.77.refs_1_, bf16[1024,1024]{1,0:T(8,128)(2,1)S(1)} %copy-done.1, f32[1024,128]{1,0:T(8,128)S(1)} %get-tuple-element.103.refs_3_, ...), custom_call_target="tpu_custom_call" | custom-call | tf_op jit(solution)/shard_map/apply/pallas_call | solution.py:40
  89.2 9.1 %collective-permute-done.20.refs_3_ = f32[1024,128]{1,0:T(8,128)S(1)} collective-permute-done((f32[1024,128]{1,0:T(8,128)S(1)}, f32[1024,128]{1,0:T(8,128)S(1)}, u32[]{:S(2)}, u32[]{:S(2)}) %collective-permute-start.20) | collective-permute-done | bytes 524320 | tf_op jit(solution)/shard_map/ppermute | solution.py:424
  98.3 2.0 %apply.15 = (f32[1024,128]{1,0:T(8,128)S(1)}, f32[8,128]{1,0:T(8,128)S(1)}) custom-call(f32[3]{0:T(128)S(1)} %copy-done.10, bf16[1024,1024]{1,0:T(8,128)(2,1)S(1)} %get-tuple-element.96.refs_4_.refs_1_, bf16[1024,1024]{1,0:T(8,128)(2,1)S(1)} %get-tuple-element.97.refs_5_.refs_2_, f32[1024,128]{1,0:T(8,128)S(1)} %collective-permute-done.20.refs_3_, ...), custom_call_target="tpu_custom_call" | custom-call | tf_op jit(solution)/shard_map/apply/pallas_call | solution.py:40
  100.3 2.1 %collective-permute-done.19.refs_3_ = f32[1024,128]{1,0:T(8,128)S(1)} collective-permute-done((f32[1024,128]{1,0:T(8,128)S(1)}, f32[1024,128]{1,0:T(8,128)S(1)}, u32[]{:S(2)}, u32[]{:S(2)}) %collective-permute-start.19) | collective-permute-done | bytes 524320 | tf_op jit(solution)/shard_map/ppermute | solution.py:424
  102.5 2.5 %apply.16 = (f32[1024,256]{1,0:T(8,128)}, f32[8,128]{1,0:T(8,128)S(1)}) custom-call(f32[3]{0:T(128)S(1)} %copy-done.10, bf16[1024,1024]{1,0:T(8,128)(2,1)S(1)} %get-tuple-element.88.refs_7_.refs_1_, bf16[1024,1024]{1,0:T(8,128)(2,1)S(1)} %get-tuple-element.89.refs_8_.refs_2_, f32[1024,128]{1,0:T(8,128)S(1)} %collective-permute-done.19.refs_3_, ...), custom_call_target="tpu_custom_call" | custom-call | tf_op jit(solution)/shard_map/apply/pallas_call | solution.py:40
  105.0 3.4 %apply.17 = (f32[1024,128]{1,0:T(8,128)S(1)}, f32[8,128]{1,0:T(8,128)S(1)}) custom-call(f32[3]{0:T(128)S(1)} %copy-done.10, bf16[1024,1024]{1,0:T(8,128)(2,1)S(1)} %get-tuple-element.77.refs_1_, bf16[1024,1024]{1,0:T(8,128)(2,1)S(1)} %copy-done.1, f32[1024,128]{1,0:T(8,128)S(1)} %get-tuple-element.102.refs_3_, ...), custom_call_target="tpu_custom_call" | custom-call | tf_op jit(solution)/shard_map/apply/pallas_call | solution.py:40
  108.5 11.5 %collective-permute-done.17.refs_3_ = f32[1024,128]{1,0:T(8,128)S(1)} collective-permute-done((f32[1024,128]{1,0:T(8,128)S(1)}, f32[1024,128]{1,0:T(8,128)S(1)}, u32[]{:S(2)}, u32[]{:S(2)}) %collective-permute-start.17) | collective-permute-done | bytes 524320 | tf_op jit(solution)/shard_map/ppermute | solution.py:424
  120.0 2.0 %apply.18 = (f32[1024,128]{1,0:T(8,128)S(1)}, f32[8,128]{1,0:T(8,128)S(1)}) custom-call(f32[3]{0:T(128)S(1)} %copy-done.10, bf16[1024,1024]{1,0:T(8,128)(2,1)S(1)} %get-tuple-element.96.refs_4_.refs_1_, bf16[1024,1024]{1,0:T(8,128)(2,1)S(1)} %get-tuple-element.97.refs_5_.refs_2_, f32[1024,128]{1,0:T(8,128)S(1)} %collective-permute-done.17.refs_3_, ...), custom_call_target="tpu_custom_call" | custom-call | tf_op jit(solution)/shard_map/apply/pallas_call | solution.py:40
  122.0 1.6 %collective-permute-done.16.refs_3_ = f32[1024,128]{1,0:T(8,128)S(1)} collective-permute-done((f32[1024,128]{1,0:T(8,128)S(1)}, f32[1024,128]{1,0:T(8,128)S(1)}, u32[]{:S(2)}, u32[]{:S(2)}) %collective-permute-start.16) | collective-permute-done | bytes 524320 | tf_op jit(solution)/shard_map/ppermute | solution.py:424
  123.6 2.5 %apply.19 = f32[1024,256]{1,0:T(8,128)} custom-call(f32[3]{0:T(128)S(1)} %copy-done.10, bf16[1024,1024]{1,0:T(8,128)(2,1)S(1)} %get-tuple-element.88.refs_7_.refs_1_, bf16[1024,1024]{1,0:T(8,128)(2,1)S(1)} %get-tuple-element.89.refs_8_.refs_2_, f32[1024,128]{1,0:T(8,128)S(1)} %collective-permute-done.16.refs_3_, ...), custom_call_target="tpu_custom_call", output_to_operand_aliasing={{}: (5, {})} | custom-call | tf_op jit(solution)/shard_map/apply/pallas_call | solution.py:40
  (48 shorter events, 2.1 us)
Async XLA Ops:
  0.0 3.1 %collective-permute-start = (f32[1024,256]{1,0:T(8,128)}, f32[1024,256]{1,0:T(8,128)S(1)}, u32[]{:S(2)}, u32[]{:S(2)}) collective-permute-start(f32[1024,256]{1,0:T(8,128)} %refs_0_.13), channel_id=1, source_target_pairs={{0,1},{1,0},{2,3},{3,2},{4,5},{5,4},{6,7},{7,6},{8,9},{9,8},{10,11... | collective-permute-start | bytes 3145736 | tf_op jit(solution)/shard_map/ppermute | solution.py:421
  3.6 18.8 %collective-permute-start.1 = (f32[1024,128]{1,0:T(8,128)S(1)}, f32[1024,128]{1,0:T(8,128)S(1)}, u32[]{:S(2)}, u32[]{:S(2)}) collective-permute-start(f32[1024,128]{1,0:T(8,128)S(1)} %get-tuple-element.65), channel_id=1, source_target_pairs={{0,2},{1,3},{2,0},{3,1},{4,6},{5,7},{6,4},{7,5},{8,10},{9,11},{10,... | collective-permute-start | bytes 1572872 | tf_op jit(solution)/shard_map/ppermute | solution.py:421
  6.5 13.7 %collective-permute-start.2 = (f32[512,128]{1,0:T(8,128)S(1)}, f32[512,128]{1,0:T(8,128)S(1)}, u32[]{:S(2)}, u32[]{:S(2)}) collective-permute-start(f32[512,128]{1,0:T(8,128)S(1)} %bitcast.5), channel_id=1, source_target_pairs={{0,8},{4,12},{8,0},{12,4},{16,24},{20,28},{24,16},{28,20},{1,9},{5... | collective-permute-start | bytes 786440 | tf_op jit(solution)/shard_map/ppermute | solution.py:424
  8.0 14.5 %collective-permute-start.3 = (f32[512,128]{1,0:T(8,128)S(1)}, f32[512,128]{1,0:T(8,128)S(1)}, u32[]{:S(2)}, u32[]{:S(2)}) collective-permute-start(f32[512,128]{1,0:T(8,128)S(1)} %bitcast.4), channel_id=1, source_target_pairs={{0,16},{4,20},{8,24},{12,28},{16,0},{20,4},{24,8},{28,12},{1,17},{... | collective-permute-start | bytes 786440 | tf_op jit(solution)/shard_map/ppermute | solution.py:424
  13.9 23.5 %copy-start.12 = (s32[8,6]{1,0:T(8,128)S(1)}, s32[8,6]{1,0:T(8,128)}, u32[]{:S(2)}) copy-start(s32[8,6]{1,0:T(8,128)} %param.10) | copy-start | bytes 580
  13.9 23.5 %copy-start.10 = (f32[3]{0:T(128)S(1)}, f32[3]{0:T(128)}, u32[]{:S(2)}) copy-start(f32[3]{0:T(128)} %refs_0_.23) | copy-start | bytes 40
  13.9 13.4 %collective-permute-start.5 = (f32[1024,128]{1,0:T(8,128)S(1)}, f32[1024,128]{1,0:T(8,128)}, u32[]{:S(2)}, u32[]{:S(2)}) collective-permute-start(f32[1024,128]{1,0:T(8,128)S(1)} %bitcast.3), channel_id=1, source_target_pairs={{0,4},{4,0},{8,12},{12,8},{16,20},{20,16},{24,28},{28,24},{1,5},{5... | collective-permute-start | bytes 1572872 | tf_op jit(solution)/shard_map/ppermute | solution.py:424
  23.6 10.7 %collective-permute-start.4 = (f32[1024,128]{1,0:T(8,128)S(1)}, f32[1024,128]{1,0:T(8,128)S(1)}, u32[]{:S(2)}, u32[]{:S(2)}) collective-permute-start(f32[1024,128]{1,0:T(8,128)S(1)} %get-tuple-element.73), channel_id=1, source_target_pairs={{0,2},{1,3},{2,0},{3,1},{4,6},{5,7},{6,4},{7,5},{8,10},{9,11},{10,... | collective-permute-start | bytes 1572872 | tf_op jit(solution)/shard_map/ppermute | solution.py:421
  24.1 24.5 %collective-permute-start.7 = (f32[1024,128]{1,0:T(8,128)}, f32[1024,128]{1,0:T(8,128)S(1)}, u32[]{:S(2)}, u32[]{:S(2)}) collective-permute-start(f32[1024,128]{1,0:T(8,128)} %get-tuple-element.84.refs_3_.refs_7_), channel_id=1, source_target_pairs={{0,8},{4,12},{8,0},{12,4},{16,24},{20,28},{24,16},{28,20},{1,9},{5... | collective-permute-start | bytes 1572872 | tf_op jit(solution)/shard_map/ppermute | solution.py:424
  24.6 24.7 %collective-permute-start.8 = (f32[1024,128]{1,0:T(8,128)}, f32[1024,128]{1,0:T(8,128)S(1)}, u32[]{:S(2)}, u32[]{:S(2)}) collective-permute-start(f32[1024,128]{1,0:T(8,128)} %get-tuple-element.84.refs_3_.refs_7_), channel_id=1, source_target_pairs={{0,16},{4,20},{8,24},{12,28},{16,0},{20,4},{24,8},{28,12},{1,17},{... | collective-permute-start | bytes 1572872 | tf_op jit(solution)/shard_map/ppermute | solution.py:424
  34.3 0.8 copy-start.3
  35.1 14.1 %collective-permute-start.6 = (f32[1024,128]{1,0:T(8,128)}, f32[1024,128]{1,0:T(8,128)}, u32[]{:S(2)}, u32[]{:S(2)}) collective-permute-start(f32[1024,128]{1,0:T(8,128)} %get-tuple-element.84.refs_3_.refs_7_), channel_id=1, source_target_pairs={{0,4},{4,0},{8,12},{12,8},{16,20},{20,16},{24,28},{28,24},{1,5},{5... | collective-permute-start | bytes 1572872 | tf_op jit(solution)/shard_map/ppermute | solution.py:424
  36.7 12.6 %collective-permute-start.10 = (f32[1024,128]{1,0:T(8,128)}, f32[1024,128]{1,0:T(8,128)}, u32[]{:S(2)}, u32[]{:S(2)}) collective-permute-start(f32[1024,128]{1,0:T(8,128)} %get-tuple-element.85.refs_3_), channel_id=1, source_target_pairs={{0,2},{1,3},{2,0},{3,1},{4,6},{5,7},{6,4},{7,5},{8,10},{9,11},{10,... | collective-permute-start | bytes 1572872 | tf_op jit(solution)/shard_map/ppermute | solution.py:421
  37.4 1.9 %copy-start.2 = (f32[8,6,128,128]{3,2,1,0:T(8,128)S(1)}, f32[8,6,128,128]{3,2,1,0:T(8,128)}, u32[]{:S(2)}) copy-start(f32[8,6,128,128]{3,2,1,0:T(8,128)} %refs_2_.8) | copy-start | bytes 9437188
  42.7 3.0 %copy-start = (bf16[1024,1024]{1,0:T(8,128)(2,1)}, bf16[1024,1024]{1,0:T(8,128)(2,1)S(1)}, u32[]{:S(2)}) copy-start(bf16[1024,1024]{1,0:T(8,128)(2,1)S(1)} %get-tuple-element.78.refs_2_) | copy-start | bytes 6291460
  42.8 3.0 %copy-start.4 = (f32[1024,128]{1,0:T(8,128)S(1)}, f32[1024,128]{1,0:T(8,128)}, u32[]{:S(2)}) copy-start(f32[1024,128]{1,0:T(8,128)} %copy-done.3) | copy-start | bytes 1572868
  45.7 2.1 %copy-start.8 = (f32[1024,128]{1,0:T(8,128)}, f32[1024,128]{1,0:T(8,128)S(1)}, u32[]{:S(2)}) copy-start(f32[1024,128]{1,0:T(8,128)S(1)} %get-tuple-element.99.refs_10_) | copy-start | bytes 1572868
  45.7 4.2 %copy-start.13 = (s32[3,64,2]{1,2,0:T(2,128)S(1)}, s32[3,64,2]{1,2,0:T(2,128)}, u32[]{:S(2)}) copy-start(s32[3,64,2]{1,2,0:T(2,128)} %param.12) | copy-start | bytes 4612
  45.7 8.0 %copy-start.11 = (s32[3,8]{1,0:T(4,128)S(1)}, s32[3,8]{1,0:T(4,128)}, u32[]{:S(2)}) copy-start(s32[3,8]{1,0:T(4,128)} %refs_1_.9) | copy-start | bytes 292
  47.8 0.8 copy-start.6
  49.3 4.5 %collective-permute-start.11 = (f32[1024,128]{1,0:T(8,128)}, f32[1024,128]{1,0:T(8,128)}, u32[]{:S(2)}, u32[]{:S(2)}) collective-permute-start(f32[1024,128]{1,0:T(8,128)} %collective-permute-done.10.refs_5_), channel_id=1, source_target_pairs={{0,1},{1,0},{2,3},{3,2},{4,5},{5,4},{6,7},{7,6},{8,9},{9,8},{10,11... | collective-permute-start | bytes 1572872 | tf_op jit(solution)/shard_map/ppermute | solution.py:421
  49.4 4.4 %collective-permute-start.9 = (f32[1024,128]{1,0:T(8,128)}, f32[1024,128]{1,0:T(8,128)}, u32[]{:S(2)}, u32[]{:S(2)}) collective-permute-start(f32[1024,128]{1,0:T(8,128)} %get-tuple-element.85.refs_3_), channel_id=1, source_target_pairs={{0,1},{1,0},{2,3},{3,2},{4,5},{5,4},{6,7},{7,6},{8,9},{9,8},{10,11... | collective-permute-start | bytes 1572872 | tf_op jit(solution)/shard_map/ppermute | solution.py:421
  49.9 11.9 %collective-permute-start.12 = (f32[1024,128]{1,0:T(8,128)}, f32[1024,128]{1,0:T(8,128)}, u32[]{:S(2)}, u32[]{:S(2)}) collective-permute-start(f32[1024,128]{1,0:T(8,128)} %collective-permute-done.5.refs_3_), channel_id=1, source_target_pairs={{0,1},{1,0},{2,3},{3,2},{4,5},{5,4},{6,7},{7,6},{8,9},{9,8},{10,11... | collective-permute-start | bytes 1572872 | tf_op jit(solution)/shard_map/ppermute | solution.py:421
  50.2 7.3 %copy-start.5 = (f32[1024,128]{1,0:T(8,128)S(1)}, f32[1024,128]{1,0:T(8,128)}, u32[]{:S(2)}) copy-start(f32[1024,128]{1,0:T(8,128)} %copy-done.3) | copy-start | bytes 1572868
  50.2 25.2 %collective-permute-start.14 = (f32[1024,128]{1,0:T(8,128)}, f32[1024,128]{1,0:T(8,128)S(1)}, u32[]{:S(2)}, u32[]{:S(2)}) collective-permute-start(f32[1024,128]{1,0:T(8,128)} %copy-done.3), channel_id=1, source_target_pairs={{0,8},{4,12},{8,0},{12,4},{16,24},{20,28},{24,16},{28,20},{1,9},{5... | collective-permute-start | bytes 1572872 | tf_op jit(solution)/shard_map/ppermute | solution.py:424
  52.1 26.8 %collective-permute-start.15 = (f32[1024,128]{1,0:T(8,128)}, f32[1024,128]{1,0:T(8,128)S(1)}, u32[]{:S(2)}, u32[]{:S(2)}) collective-permute-start(f32[1024,128]{1,0:T(8,128)} %copy-done.3), channel_id=1, source_target_pairs={{0,16},{4,20},{8,24},{12,28},{16,0},{20,4},{24,8},{28,12},{1,17},{... | collective-permute-start | bytes 1572872 | tf_op jit(solution)/shard_map/ppermute | solution.py:424
  57.5 21.4 %collective-permute-start.13 = (f32[1024,128]{1,0:T(8,128)S(1)}, f32[1024,128]{1,0:T(8,128)S(1)}, u32[]{:S(2)}, u32[]{:S(2)}) collective-permute-start(f32[1024,128]{1,0:T(8,128)S(1)} %copy-done.5), channel_id=1, source_target_pairs={{0,4},{4,0},{8,12},{12,8},{16,20},{20,16},{24,28},{28,24},{1,5},{5... | collective-permute-start | bytes 1572872 | tf_op jit(solution)/shard_map/ppermute | solution.py:424
  61.8 3.9 %copy-start.9 = (f32[1024,128]{1,0:T(8,128)S(1)}, f32[1024,128]{1,0:T(8,128)}, u32[]{:S(2)}) copy-start(f32[1024,128]{1,0:T(8,128)} %copy-done.8) | copy-start | bytes 1572868
  65.7 13.2 %copy-start.7 = (f32[1024,128]{1,0:T(8,128)S(1)}, f32[1024,128]{1,0:T(8,128)}, u32[]{:S(2)}) copy-start(f32[1024,128]{1,0:T(8,128)} %copy-done.6) | copy-start | bytes 1572868
  70.7 14.1 %collective-permute-start.21 = (f32[1024,128]{1,0:T(8,128)S(1)}, f32[1024,128]{1,0:T(8,128)S(1)}, u32[]{:S(2)}, u32[]{:S(2)}) collective-permute-start(f32[1024,128]{1,0:T(8,128)S(1)} %get-tuple-element.103.refs_3_), channel_id=1, source_target_pairs={{0,4},{4,0},{8,12},{12,8},{16,20},{20,16},{24,28},{28,24},{1,5},{5... | collective-permute-start | bytes 1572872 | tf_op jit(solution)/shard_map/ppermute | solution.py:424
  72.2 26.1 %collective-permute-start.20 = (f32[1024,128]{1,0:T(8,128)S(1)}, f32[1024,128]{1,0:T(8,128)S(1)}, u32[]{:S(2)}, u32[]{:S(2)}) collective-permute-start(f32[1024,128]{1,0:T(8,128)S(1)} %get-tuple-element.103.refs_3_), channel_id=1, source_target_pairs={{0,8},{4,12},{8,0},{12,4},{16,24},{20,28},{24,16},{28,20},{1,9},{5... | collective-permute-start | bytes 1572872 | tf_op jit(solution)/shard_map/ppermute | solution.py:424
  75.4 27.1 %collective-permute-start.19 = (f32[1024,128]{1,0:T(8,128)S(1)}, f32[1024,128]{1,0:T(8,128)S(1)}, u32[]{:S(2)}, u32[]{:S(2)}) collective-permute-start(f32[1024,128]{1,0:T(8,128)S(1)} %get-tuple-element.103.refs_3_), channel_id=1, source_target_pairs={{0,16},{4,20},{8,24},{12,28},{16,0},{20,4},{24,8},{28,12},{1,17},{... | collective-permute-start | bytes 1572872 | tf_op jit(solution)/shard_map/ppermute | solution.py:424
  78.9 6.6 %copy-start.1 = (bf16[1024,1024]{1,0:T(8,128)(2,1)S(1)}, bf16[1024,1024]{1,0:T(8,128)(2,1)}, u32[]{:S(2)}) copy-start(bf16[1024,1024]{1,0:T(8,128)(2,1)} %copy-done) | copy-start | bytes 6291460
  83.3 21.7 %collective-permute-start.18 = (f32[1024,128]{1,0:T(8,128)S(1)}, f32[1024,128]{1,0:T(8,128)S(1)}, u32[]{:S(2)}, u32[]{:S(2)}) collective-permute-start(f32[1024,128]{1,0:T(8,128)S(1)} %get-tuple-element.102.refs_3_), channel_id=1, source_target_pairs={{0,4},{4,0},{8,12},{12,8},{16,20},{20,16},{24,28},{28,24},{1,5},{5... | collective-permute-start | bytes 1572872 | tf_op jit(solution)/shard_map/ppermute | solution.py:424
  83.7 36.3 %collective-permute-start.17 = (f32[1024,128]{1,0:T(8,128)S(1)}, f32[1024,128]{1,0:T(8,128)S(1)}, u32[]{:S(2)}, u32[]{:S(2)}) collective-permute-start(f32[1024,128]{1,0:T(8,128)S(1)} %get-tuple-element.102.refs_3_), channel_id=1, source_target_pairs={{0,8},{4,12},{8,0},{12,4},{16,24},{20,28},{24,16},{28,20},{1,9},{5... | collective-permute-start | bytes 1572872 | tf_op jit(solution)/shard_map/ppermute | solution.py:424
  84.7 38.9 %collective-permute-start.16 = (f32[1024,128]{1,0:T(8,128)S(1)}, f32[1024,128]{1,0:T(8,128)S(1)}, u32[]{:S(2)}, u32[]{:S(2)}) collective-permute-start(f32[1024,128]{1,0:T(8,128)S(1)} %get-tuple-element.102.refs_3_), channel_id=1, source_target_pairs={{0,16},{4,20},{8,24},{12,28},{16,0},{20,4},{24,8},{28,12},{1,17},{... | collective-permute-start | bytes 1572872 | tf_op jit(solution)/shard_map/ppermute | solution.py:424

commit v4 on v3

--- a/solution.py
+++ b/solution.py
@@ -470,7 +470,6 @@
     local_parts, token = build_local(token, local_blocks, local_cols.reshape(-1), bounds)
     waits = []
     partial = [part_sum([(*local_parts, [field[0]])], 1, waits=waits)]
-    partial.append(part_sum([(*local_parts, [field[1]])], 1))
     token = touch(token, [arrived[0][k] for k in slots])
 
     total = gate(total, token)
@@ -495,6 +494,8 @@
             arrived[1].update({n: exchange(gate(total, token), n) for n in near})
     first = []
     for h in range(2):
+        if h == 1:
+            partial.append(part_sum([(*local_parts, [field[1]])], 1))
         terms = [(*mats[k], [arrived[h][k]]) for k in slots]
         first.append(part_sum(terms, 1, partial[h]))
     arrived = [send(f) for f in first]

time: 127 us -> 127 us (level)
    unnamed x29 -> x23, local copies, waits for them, and re-layouts: 3.63 us -> 3.63 us
where the time goes in v4:
time: 127 us; the launch traced here: 126 us
  Pallas kernels  52.8 us (42%)
  waiting for transfers between devices  44.5 us (35%)
  starting transfers between devices  24.7 us (19%)
  local copies, waits for them, and re-layouts  3.85 us (3%)
    pallas_call x20, Pallas kernels, call(): pl.pallas_call(body, in_specs=[*specs, *[pl.BlockSpec(memory_space=pl.ANY...  52.8 us
    ppermute x15, waiting for transfers between devices, to_row(): return lax.ppermute(x, 'rows', [(i, i ^ 1 << bit) for i in range(n_rows)])  37.6 us
    ppermute x15, starting transfers between devices, to_row(): return lax.ppermute(x, 'rows', [(i, i ^ 1 << bit) for i in range(n_rows)])  19.6 us
    ppermute x7, waiting for transfers between devices, to_band(): return lax.ppermute(x, 'bands', [(i, i ^ mask) for i in range(n_bands)])  6.94 us
    ppermute x7, starting transfers between devices, to_band(): return lax.ppermute(x, 'bands', [(i, i ^ mask) for i in range(n_bands)])  5.1 us
    unnamed x23, local copies, waits for them, and re-layouts  3.63 us
  transfers between devices with their start and end apart: 22, of which 11 were waited for; matrix products, arithmetic and copies ran while one was open for 0% of the time, Pallas kernels for 39%

profile of v4, /device:TPU:0, one launch (start us, length us, event | category | flops | bytes accessed | tf_op | source)
XLA Modules:
  0.0 126.3 jit_solution(9854908762606797157)
XLA Ops:
  0.0 0.5 collective-permute-start
  0.5 2.6 %begin.1 = (f32[1024,128]{1,0:T(8,128)S(1)}, f32[256,128]{1,0:T(8,128)S(1)}, f32[4,2,128,128]{3,2,1,0:T(8,128)S(1)}, f32[2,2,128,128]{3,2,1,0:T(8,128)S(1)}, f32...) custom-call(s32[3,8]{1,0:T(4,128)} %refs_1_.9, f32[1024,256]{1,0:T(8,128)} %refs_0_.13, f32[1024,1024]{1,0:T(8,128)} %refs_2_.7, ...), custom_call_target="tpu_custom_call" | custom-call | tf_op jit(solution)/shard_map/begin/pallas_call | solution.py:40
  3.1 0.6 rotate_first.1
  3.6 2.8 %collective-permute-start.1 = (f32[1024,128]{1,0:T(8,128)S(1)}, f32[1024,128]{1,0:T(8,128)S(1)}, u32[]{:S(2)}, u32[]{:S(2)}) collective-permute-start(f32[1024,128]{1,0:T(8,128)S(1)} %get-tuple-element.65), channel_id=1, source_target_pairs={{0,2},{1,3},{2,0},{3,1},{4,6},{5,7},{6,4},{7,5},{8,10},{9,11},{10,... | collective-permute-start | bytes 1572872 | tf_op jit(solution)/shard_map/ppermute | solution.py:421
  6.5 1.6 %collective-permute-start.2 = (f32[512,128]{1,0:T(8,128)S(1)}, f32[512,128]{1,0:T(8,128)S(1)}, u32[]{:S(2)}, u32[]{:S(2)}) collective-permute-start(f32[512,128]{1,0:T(8,128)S(1)} %bitcast.5), channel_id=1, source_target_pairs={{0,8},{4,12},{8,0},{12,4},{16,24},{20,28},{24,16},{28,20},{1,9},{5... | collective-permute-start | bytes 786440 | tf_op jit(solution)/shard_map/ppermute | solution.py:424
  8.0 2.6 %collective-permute-start.3 = (f32[512,128]{1,0:T(8,128)S(1)}, f32[512,128]{1,0:T(8,128)S(1)}, u32[]{:S(2)}, u32[]{:S(2)}) collective-permute-start(f32[512,128]{1,0:T(8,128)S(1)} %bitcast.4), channel_id=1, source_target_pairs={{0,16},{4,20},{8,24},{12,28},{16,0},{20,4},{24,8},{28,12},{1,17},{... | collective-permute-start | bytes 786440 | tf_op jit(solution)/shard_map/ppermute | solution.py:424
  10.6 3.3 %rotate_rest.1 = (f32[1024,128]{1,0:T(8,128)S(1)}, f32[1024,128]{1,0:T(8,128)S(1)}, f32[1024,128]{1,0:T(8,128)S(1)}, f32[8,128]{1,0:T(8,128)S(1)}) custom-call(f32[1024,256]{1,0:T(8,128)} %refs_0_.13, f32[1024,256]{1,0:T(8,128)S(1)} %collective-permute-done.refs_1_, f32[1024,1024]{1,0:T(8,128)} %refs_2_.7, f32[8,128]{1,0:T(8,128)S(1)} %get-tuple-element.63.refs_3_), custom_call_target="tpu_custom_call" | custom-call | tf_op jit(solution)/shard_map/rotate_rest/pallas_call | solution.py:40
  13.9 1.6 %collective-permute-start.5 = (f32[1024,128]{1,0:T(8,128)S(1)}, f32[1024,128]{1,0:T(8,128)}, u32[]{:S(2)}, u32[]{:S(2)}) collective-permute-start(f32[1024,128]{1,0:T(8,128)S(1)} %bitcast.3), channel_id=1, source_target_pairs={{0,4},{4,0},{8,12},{12,8},{16,20},{20,16},{24,28},{28,24},{1,5},{5... | collective-permute-start | bytes 1572872 | tf_op jit(solution)/shard_map/ppermute | solution.py:424
  15.5 4.6 %collective-permute-done.2.refs_2_ = f32[512,128]{1,0:T(8,128)S(1)} collective-permute-done((f32[512,128]{1,0:T(8,128)S(1)}, f32[512,128]{1,0:T(8,128)S(1)}, u32[]{:S(2)}, u32[]{:S(2)}) %collective-permute-start.2) | collective-permute-done | bytes 262176 | tf_op jit(solution)/shard_map/ppermute | solution.py:424
  20.1 2.3 %collective-permute-done.3.refs_3_ = f32[512,128]{1,0:T(8,128)S(1)} collective-permute-done((f32[512,128]{1,0:T(8,128)S(1)}, f32[512,128]{1,0:T(8,128)S(1)}, u32[]{:S(2)}, u32[]{:S(2)}) %collective-permute-start.3) | collective-permute-done | bytes 262176 | tf_op jit(solution)/shard_map/ppermute | solution.py:424
  22.5 1.1 meet.2
  23.6 0.5 collective-permute-start.4
  24.1 0.4 collective-permute-start.7
  24.5 2.6 %collective-permute-start.8 = (f32[1024,128]{1,0:T(8,128)}, f32[1024,128]{1,0:T(8,128)S(1)}, u32[]{:S(2)}, u32[]{:S(2)}) collective-permute-start(f32[1024,128]{1,0:T(8,128)} %get-tuple-element.82.refs_3_.refs_7_), channel_id=1, source_target_pairs={{0,16},{4,20},{8,24},{12,28},{16,0},{20,4},{24,8},{28,12},{1,17},{... | collective-permute-start | bytes 1572872 | tf_op jit(solution)/shard_map/ppermute | solution.py:424
  27.3 6.9 %collective-permute-done.4.refs_1_ = f32[1024,128]{1,0:T(8,128)S(1)} collective-permute-done((f32[1024,128]{1,0:T(8,128)S(1)}, f32[1024,128]{1,0:T(8,128)S(1)}, u32[]{:S(2)}, u32[]{:S(2)}) %collective-permute-start.4) | collective-permute-done | bytes 524320 | tf_op jit(solution)/shard_map/ppermute | solution.py:421
  34.3 0.8 copy-done.3
  35.1 1.6 %collective-permute-start.6 = (f32[1024,128]{1,0:T(8,128)}, f32[1024,128]{1,0:T(8,128)}, u32[]{:S(2)}, u32[]{:S(2)}) collective-permute-start(f32[1024,128]{1,0:T(8,128)} %get-tuple-element.82.refs_3_.refs_7_), channel_id=1, source_target_pairs={{0,4},{4,0},{8,12},{12,8},{16,20},{20,16},{24,28},{28,24},{1,5},{5... | collective-permute-start | bytes 1572872 | tf_op jit(solution)/shard_map/ppermute | solution.py:424
  36.7 0.6 collective-permute-start.10
  37.5 1.9 %copy-done.2 = f32[8,6,128,128]{3,2,1,0:T(8,128)S(1)} copy-done((f32[8,6,128,128]{3,2,1,0:T(8,128)S(1)}, f32[8,6,128,128]{3,2,1,0:T(8,128)}, u32[]{:S(2)}) %copy-start.2) | copy-done | bytes 3145752
  39.3 3.4 %build_local.1 = (bf16[1024,1024]{1,0:T(8,128)(2,1)S(1)}, bf16[1024,1024]{1,0:T(8,128)(2,1)S(1)}, f32[8,128]{1,0:T(8,128)S(1)}) custom-call(s32[48]{0:T(128)S(1)} %reshape.18.refs_0_, f32[3]{0:T(128)S(1)} %copy-done.7, f32[8,6,128,128]{3,2,1,0:T(8,128)S(1)} %copy-done.2, f32[8,128]{1,0:T(8,128)S(1)} %get-tuple-element.76.refs_3_), custom_call_target="tpu_custom_call" | custom-call | tf_op jit(solution)/shard_map/build_local/pallas_call | solution.py:40
  42.8 3.0 %apply.10 = (f32[1024,128]{1,0:T(8,128)S(1)}, f32[8,128]{1,0:T(8,128)S(1)}) custom-call(f32[3]{0:T(128)S(1)} %copy-done.7, bf16[1024,1024]{1,0:T(8,128)(2,1)S(1)} %get-tuple-element.77.refs_1_, bf16[1024,1024]{1,0:T(8,128)(2,1)S(1)} %get-tuple-element.78.refs_2_, f32[1024,128]{1,0:T(8,128)} %get-tuple-element.82.refs_3_.refs_7_, ...), custom_call_target="tpu_custom_call" | custom-call | tf_op jit(solution)/shard_map/apply/pallas_call | solution.py:40
  45.8 0.8 copy-done.5
  46.6 2.7 %collective-permute-done.8.refs_3_.refs_9_ = f32[1024,128]{1,0:T(8,128)S(1)} collective-permute-done((f32[1024,128]{1,0:T(8,128)}, f32[1024,128]{1,0:T(8,128)S(1)}, u32[]{:S(2)}, u32[]{:S(2)}) %collective-permute-start.8) | collective-permute-done | bytes 524320 | tf_op jit(solution)/shard_map/ppermute | solution.py:424
  49.4 0.5 collective-permute-start.9
  50.2 1.9 %collective-permute-start.14 = (f32[1024,128]{1,0:T(8,128)}, f32[1024,128]{1,0:T(8,128)S(1)}, u32[]{:S(2)}, u32[]{:S(2)}) collective-permute-start(f32[1024,128]{1,0:T(8,128)} %copy-done.3), channel_id=1, source_target_pairs={{0,8},{4,12},{8,0},{12,4},{16,24},{20,28},{24,16},{28,20},{1,9},{5... | collective-permute-start | bytes 1572872 | tf_op jit(solution)/shard_map/ppermute | solution.py:424
  52.4 3.7 %build_couple.3 = (bf16[1024,1024]{1,0:T(8,128)(2,1)S(1)}, bf16[1024,1024]{1,0:T(8,128)(2,1)S(1)}, f32[8,128]{1,0:T(8,128)S(1)}) custom-call(s32[384]{0:T(512)S(1)} %reshape.15.refs_0_, s32[3,8]{1,0:T(4,128)S(1)} %copy-done.8, f32[3,8,2,128,128]{4,3,2,1,0:T(8,128)} %refs_2_.11, f32[1024,128]{1,0:T(8,128)} %get-tuple-element.83.refs_3_, ...), custom_call_target="tpu_custom_call" | custom-call | tf_op jit(solution)/shard_map/build_couple/pallas_call | solution.py:40
  56.2 1.6 %collective-permute-start.13 = (f32[1024,128]{1,0:T(8,128)S(1)}, f32[1024,128]{1,0:T(8,128)S(1)}, u32[]{:S(2)}, u32[]{:S(2)}) collective-permute-start(f32[1024,128]{1,0:T(8,128)S(1)} %copy-done.4), channel_id=1, source_target_pairs={{0,4},{4,0},{8,12},{12,8},{16,20},{20,16},{24,28},{28,24},{1,5},{5... | collective-permute-start | bytes 1572872 | tf_op jit(solution)/shard_map/ppermute | solution.py:424
  57.7 3.7 %build_couple.4 = (bf16[1024,1024]{1,0:T(8,128)(2,1)S(1)}, bf16[1024,1024]{1,0:T(8,128)(2,1)S(1)}, f32[8,128]{1,0:T(8,128)S(1)}) custom-call(s32[384]{0:T(512)S(1)} %reshape.15.refs_0_, s32[3,8]{1,0:T(4,128)S(1)} %copy-done.8, f32[3,8,2,128,128]{4,3,2,1,0:T(8,128)} %refs_2_.11, f32[1024,128]{1,0:T(8,128)} %get-tuple-element.83.refs_3_, ...), custom_call_target="tpu_custom_call" | custom-call | tf_op jit(solution)/shard_map/build_couple/pallas_call | solution.py:40
  61.5 3.9 %build_couple.5 = (bf16[1024,1024]{1,0:T(8,128)(2,1)S(1)}, bf16[1024,1024]{1,0:T(8,128)(2,1)S(1)}, f32[8,128]{1,0:T(8,128)S(1)}) custom-call(s32[384]{0:T(512)S(1)} %reshape.15.refs_0_, s32[3,8]{1,0:T(4,128)S(1)} %copy-done.8, f32[3,8,2,128,128]{4,3,2,1,0:T(8,128)} %refs_2_.11, f32[1024,128]{1,0:T(8,128)} %collective-permute-done.5.refs_3_, ...), custom_call_target="tpu_custom_call" | custom-call | tf_op jit(solution)/shard_map/build_couple/pallas_call | solution.py:40
  65.4 5.0 %apply.11 = (f32[1024,128]{1,0:T(8,128)S(1)}, f32[8,128]{1,0:T(8,128)S(1)}) custom-call(f32[3]{0:T(128)S(1)} %copy-done.7, bf16[1024,1024]{1,0:T(8,128)(2,1)S(1)} %get-tuple-element.90.refs_1_.refs_4_, bf16[1024,1024]{1,0:T(8,128)(2,1)S(1)} %get-tuple-element.91.refs_2_.refs_5_, f32[1024,128]{1,0:T(8,128)} %collective-permute-done.6.refs_1_.refs_3_, ...), custom_call_target="tpu_custom_call" | custom-call | tf_op jit(solution)/shard_map/apply/pallas_call | solution.py:40
  70.4 0.6 collective-permute-start.21
  71.0 1.9 %collective-permute-start.20 = (f32[1024,128]{1,0:T(8,128)S(1)}, f32[1024,128]{1,0:T(8,128)S(1)}, u32[]{:S(2)}, u32[]{:S(2)}) collective-permute-start(f32[1024,128]{1,0:T(8,128)S(1)} %get-tuple-element.103.refs_3_), channel_id=1, source_target_pairs={{0,8},{4,12},{8,0},{12,4},{16,24},{20,28},{24,16},{28,20},{1,9},{5... | collective-permute-start | bytes 1572872 | tf_op jit(solution)/shard_map/ppermute | solution.py:424
  72.8 2.0 %apply.12 = (f32[1024,128]{1,0:T(8,128)S(1)}, f32[8,128]{1,0:T(8,128)S(1)}) custom-call(f32[3]{0:T(128)S(1)} %copy-done.7, bf16[1024,1024]{1,0:T(8,128)(2,1)S(1)} %get-tuple-element.77.refs_1_, bf16[1024,1024]{1,0:T(8,128)(2,1)S(1)} %copy-done.1, f32[1024,128]{1,0:T(8,128)S(1)} %copy-done.4, f32[8,128]{1,0:T(8,128)S(1)} %get-tuple-element.99.refs_4_), custom_call_target="tpu_custom_call" | custom-call | tf_op jit(solution)/shard_map/apply/pallas_call | solution.py:40
  75.3 0.8 collective-permute-start.19
  76.1 2.9 %collective-permute-done.15.refs_9_ = f32[1024,128]{1,0:T(8,128)S(1)} collective-permute-done((f32[1024,128]{1,0:T(8,128)}, f32[1024,128]{1,0:T(8,128)S(1)}, u32[]{:S(2)}, u32[]{:S(2)}) %collective-permute-start.15) | collective-permute-done | bytes 524320 | tf_op jit(solution)/shard_map/ppermute | solution.py:424
  79.0 4.4 %apply.13 = (f32[1024,128]{1,0:T(8,128)S(1)}, f32[8,128]{1,0:T(8,128)S(1)}) custom-call(f32[3]{0:T(128)S(1)} %copy-done.7, bf16[1024,1024]{1,0:T(8,128)(2,1)S(1)} %get-tuple-element.90.refs_1_.refs_4_, bf16[1024,1024]{1,0:T(8,128)(2,1)S(1)} %get-tuple-element.91.refs_2_.refs_5_, f32[1024,128]{1,0:T(8,128)S(1)} %collective-permute-done.13.refs_3_, ...), custom_call_target="tpu_custom_call" | custom-call | tf_op jit(solution)/shard_map/apply/pallas_call | solution.py:40
  83.7 0.8 collective-permute-start.17
  84.5 1.1 collective-permute-start.16
  85.6 3.7 %apply.14 = (f32[1024,128]{1,0:T(8,128)S(1)}, f32[8,128]{1,0:T(8,128)S(1)}) custom-call(f32[3]{0:T(128)S(1)} %copy-done.7, bf16[1024,1024]{1,0:T(8,128)(2,1)S(1)} %get-tuple-element.77.refs_1_, bf16[1024,1024]{1,0:T(8,128)(2,1)S(1)} %copy-done.1, f32[1024,128]{1,0:T(8,128)S(1)} %get-tuple-element.103.refs_3_, ...), custom_call_target="tpu_custom_call" | custom-call | tf_op jit(solution)/shard_map/apply/pallas_call | solution.py:40
  89.3 8.4 %collective-permute-done.20.refs_3_ = f32[1024,128]{1,0:T(8,128)S(1)} collective-permute-done((f32[1024,128]{1,0:T(8,128)S(1)}, f32[1024,128]{1,0:T(8,128)S(1)}, u32[]{:S(2)}, u32[]{:S(2)}) %collective-permute-start.20) | collective-permute-done | bytes 524320 | tf_op jit(solution)/shard_map/ppermute | solution.py:424
  97.7 2.0 %apply.15 = (f32[1024,128]{1,0:T(8,128)S(1)}, f32[8,128]{1,0:T(8,128)S(1)}) custom-call(f32[3]{0:T(128)S(1)} %copy-done.7, bf16[1024,1024]{1,0:T(8,128)(2,1)S(1)} %get-tuple-element.95.refs_4_.refs_1_, bf16[1024,1024]{1,0:T(8,128)(2,1)S(1)} %get-tuple-element.96.refs_5_.refs_2_, f32[1024,128]{1,0:T(8,128)S(1)} %collective-permute-done.20.refs_3_, ...), custom_call_target="tpu_custom_call" | custom-call | tf_op jit(solution)/shard_map/apply/pallas_call | solution.py:40
  99.7 2.6 %collective-permute-done.19.refs_3_ = f32[1024,128]{1,0:T(8,128)S(1)} collective-permute-done((f32[1024,128]{1,0:T(8,128)S(1)}, f32[1024,128]{1,0:T(8,128)S(1)}, u32[]{:S(2)}, u32[]{:S(2)}) %collective-permute-start.19) | collective-permute-done | bytes 524320 | tf_op jit(solution)/shard_map/ppermute | solution.py:424
  102.4 2.8 %apply.16 = (f32[1024,256]{1,0:T(8,128)}, f32[8,128]{1,0:T(8,128)S(1)}) custom-call(f32[3]{0:T(128)S(1)} %copy-done.7, bf16[1024,1024]{1,0:T(8,128)(2,1)S(1)} %get-tuple-element.86.refs_7_.refs_1_, bf16[1024,1024]{1,0:T(8,128)(2,1)S(1)} %get-tuple-element.87.refs_8_.refs_2_, f32[1024,128]{1,0:T(8,128)S(1)} %collective-permute-done.19.refs_3_, ...), custom_call_target="tpu_custom_call" | custom-call | tf_op jit(solution)/shard_map/apply/pallas_call | solution.py:40
  105.1 3.2 %apply.17 = (f32[1024,128]{1,0:T(8,128)S(1)}, f32[8,128]{1,0:T(8,128)S(1)}) custom-call(f32[3]{0:T(128)S(1)} %copy-done.7, bf16[1024,1024]{1,0:T(8,128)(2,1)S(1)} %get-tuple-element.77.refs_1_, bf16[1024,1024]{1,0:T(8,128)(2,1)S(1)} %copy-done.1, f32[1024,128]{1,0:T(8,128)S(1)} %get-tuple-element.102.refs_3_, ...), custom_call_target="tpu_custom_call" | custom-call | tf_op jit(solution)/shard_map/apply/pallas_call | solution.py:40
  108.3 11.5 %collective-permute-done.17.refs_3_ = f32[1024,128]{1,0:T(8,128)S(1)} collective-permute-done((f32[1024,128]{1,0:T(8,128)S(1)}, f32[1024,128]{1,0:T(8,128)S(1)}, u32[]{:S(2)}, u32[]{:S(2)}) %collective-permute-start.17) | collective-permute-done | bytes 524320 | tf_op jit(solution)/shard_map/ppermute | solution.py:424
  119.9 2.0 %apply.18 = (f32[1024,128]{1,0:T(8,128)S(1)}, f32[8,128]{1,0:T(8,128)S(1)}) custom-call(f32[3]{0:T(128)S(1)} %copy-done.7, bf16[1024,1024]{1,0:T(8,128)(2,1)S(1)} %get-tuple-element.95.refs_4_.refs_1_, bf16[1024,1024]{1,0:T(8,128)(2,1)S(1)} %get-tuple-element.96.refs_5_.refs_2_, f32[1024,128]{1,0:T(8,128)S(1)} %collective-permute-done.17.refs_3_, ...), custom_call_target="tpu_custom_call" | custom-call | tf_op jit(solution)/shard_map/apply/pallas_call | solution.py:40
  121.9 1.7 %collective-permute-done.16.refs_3_ = f32[1024,128]{1,0:T(8,128)S(1)} collective-permute-done((f32[1024,128]{1,0:T(8,128)S(1)}, f32[1024,128]{1,0:T(8,128)S(1)}, u32[]{:S(2)}, u32[]{:S(2)}) %collective-permute-start.16) | collective-permute-done | bytes 524320 | tf_op jit(solution)/shard_map/ppermute | solution.py:424
  123.6 2.5 %apply.19 = f32[1024,256]{1,0:T(8,128)} custom-call(f32[3]{0:T(128)S(1)} %copy-done.7, bf16[1024,1024]{1,0:T(8,128)(2,1)S(1)} %get-tuple-element.86.refs_7_.refs_1_, bf16[1024,1024]{1,0:T(8,128)(2,1)S(1)} %get-tuple-element.87.refs_8_.refs_2_, f32[1024,128]{1,0:T(8,128)S(1)} %collective-permute-done.16.refs_3_, ...), custom_call_target="tpu_custom_call", output_to_operand_aliasing={{}: (5, {})} | custom-call | tf_op jit(solution)/shard_map/apply/pallas_call | solution.py:40
  (42 shorter events, 1.8 us)
Async XLA Ops:
  0.0 3.1 %collective-permute-start = (f32[1024,256]{1,0:T(8,128)}, f32[1024,256]{1,0:T(8,128)S(1)}, u32[]{:S(2)}, u32[]{:S(2)}) collective-permute-start(f32[1024,256]{1,0:T(8,128)} %refs_0_.13), channel_id=1, source_target_pairs={{0,1},{1,0},{2,3},{3,2},{4,5},{5,4},{6,7},{7,6},{8,9},{9,8},{10,11... | collective-permute-start | bytes 3145736 | tf_op jit(solution)/shard_map/ppermute | solution.py:421
  3.6 18.8 %collective-permute-start.1 = (f32[1024,128]{1,0:T(8,128)S(1)}, f32[1024,128]{1,0:T(8,128)S(1)}, u32[]{:S(2)}, u32[]{:S(2)}) collective-permute-start(f32[1024,128]{1,0:T(8,128)S(1)} %get-tuple-element.65), channel_id=1, source_target_pairs={{0,2},{1,3},{2,0},{3,1},{4,6},{5,7},{6,4},{7,5},{8,10},{9,11},{10,... | collective-permute-start | bytes 1572872 | tf_op jit(solution)/shard_map/ppermute | solution.py:421
  6.5 13.7 %collective-permute-start.2 = (f32[512,128]{1,0:T(8,128)S(1)}, f32[512,128]{1,0:T(8,128)S(1)}, u32[]{:S(2)}, u32[]{:S(2)}) collective-permute-start(f32[512,128]{1,0:T(8,128)S(1)} %bitcast.5), channel_id=1, source_target_pairs={{0,8},{4,12},{8,0},{12,4},{16,24},{20,28},{24,16},{28,20},{1,9},{5... | collective-permute-start | bytes 786440 | tf_op jit(solution)/shard_map/ppermute | solution.py:424
  8.0 14.5 %collective-permute-start.3 = (f32[512,128]{1,0:T(8,128)S(1)}, f32[512,128]{1,0:T(8,128)S(1)}, u32[]{:S(2)}, u32[]{:S(2)}) collective-permute-start(f32[512,128]{1,0:T(8,128)S(1)} %bitcast.4), channel_id=1, source_target_pairs={{0,16},{4,20},{8,24},{12,28},{16,0},{20,4},{24,8},{28,12},{1,17},{... | collective-permute-start | bytes 786440 | tf_op jit(solution)/shard_map/ppermute | solution.py:424
  13.9 23.5 %copy-start.9 = (s32[8,6]{1,0:T(8,128)S(1)}, s32[8,6]{1,0:T(8,128)}, u32[]{:S(2)}) copy-start(s32[8,6]{1,0:T(8,128)} %param.10) | copy-start | bytes 580
  13.9 23.5 %copy-start.7 = (f32[3]{0:T(128)S(1)}, f32[3]{0:T(128)}, u32[]{:S(2)}) copy-start(f32[3]{0:T(128)} %refs_0_.23) | copy-start | bytes 40
  13.9 13.4 %collective-permute-start.5 = (f32[1024,128]{1,0:T(8,128)S(1)}, f32[1024,128]{1,0:T(8,128)}, u32[]{:S(2)}, u32[]{:S(2)}) collective-permute-start(f32[1024,128]{1,0:T(8,128)S(1)} %bitcast.3), channel_id=1, source_target_pairs={{0,4},{4,0},{8,12},{12,8},{16,20},{20,16},{24,28},{28,24},{1,5},{5... | collective-permute-start | bytes 1572872 | tf_op jit(solution)/shard_map/ppermute | solution.py:424
  23.6 10.7 %collective-permute-start.4 = (f32[1024,128]{1,0:T(8,128)S(1)}, f32[1024,128]{1,0:T(8,128)S(1)}, u32[]{:S(2)}, u32[]{:S(2)}) collective-permute-start(f32[1024,128]{1,0:T(8,128)S(1)} %get-tuple-element.73), channel_id=1, source_target_pairs={{0,2},{1,3},{2,0},{3,1},{4,6},{5,7},{6,4},{7,5},{8,10},{9,11},{10,... | collective-permute-start | bytes 1572872 | tf_op jit(solution)/shard_map/ppermute | solution.py:421
  24.1 22.5 %collective-permute-start.7 = (f32[1024,128]{1,0:T(8,128)}, f32[1024,128]{1,0:T(8,128)S(1)}, u32[]{:S(2)}, u32[]{:S(2)}) collective-permute-start(f32[1024,128]{1,0:T(8,128)} %get-tuple-element.82.refs_3_.refs_7_), channel_id=1, source_target_pairs={{0,8},{4,12},{8,0},{12,4},{16,24},{20,28},{24,16},{28,20},{1,9},{5... | collective-permute-start | bytes 1572872 | tf_op jit(solution)/shard_map/ppermute | solution.py:424
  24.5 24.7 %collective-permute-start.8 = (f32[1024,128]{1,0:T(8,128)}, f32[1024,128]{1,0:T(8,128)S(1)}, u32[]{:S(2)}, u32[]{:S(2)}) collective-permute-start(f32[1024,128]{1,0:T(8,128)} %get-tuple-element.82.refs_3_.refs_7_), channel_id=1, source_target_pairs={{0,16},{4,20},{8,24},{12,28},{16,0},{20,4},{24,8},{28,12},{1,17},{... | collective-permute-start | bytes 1572872 | tf_op jit(solution)/shard_map/ppermute | solution.py:424
  34.3 0.8 copy-start.3
  35.1 14.1 %collective-permute-start.6 = (f32[1024,128]{1,0:T(8,128)}, f32[1024,128]{1,0:T(8,128)}, u32[]{:S(2)}, u32[]{:S(2)}) collective-permute-start(f32[1024,128]{1,0:T(8,128)} %get-tuple-element.82.refs_3_.refs_7_), channel_id=1, source_target_pairs={{0,4},{4,0},{8,12},{12,8},{16,20},{20,16},{24,28},{28,24},{1,5},{5... | collective-permute-start | bytes 1572872 | tf_op jit(solution)/shard_map/ppermute | solution.py:424
  36.7 12.6 %collective-permute-start.10 = (f32[1024,128]{1,0:T(8,128)}, f32[1024,128]{1,0:T(8,128)}, u32[]{:S(2)}, u32[]{:S(2)}) collective-permute-start(f32[1024,128]{1,0:T(8,128)} %get-tuple-element.83.refs_3_), channel_id=1, source_target_pairs={{0,2},{1,3},{2,0},{3,1},{4,6},{5,7},{6,4},{7,5},{8,10},{9,11},{10,... | collective-permute-start | bytes 1572872 | tf_op jit(solution)/shard_map/ppermute | solution.py:421
  37.4 1.9 %copy-start.2 = (f32[8,6,128,128]{3,2,1,0:T(8,128)S(1)}, f32[8,6,128,128]{3,2,1,0:T(8,128)}, u32[]{:S(2)}) copy-start(f32[8,6,128,128]{3,2,1,0:T(8,128)} %refs_2_.8) | copy-start | bytes 9437188
  42.7 3.0 %copy-start = (bf16[1024,1024]{1,0:T(8,128)(2,1)}, bf16[1024,1024]{1,0:T(8,128)(2,1)S(1)}, u32[]{:S(2)}) copy-start(bf16[1024,1024]{1,0:T(8,128)(2,1)S(1)} %get-tuple-element.78.refs_2_) | copy-start | bytes 6291460
  42.7 7.2 %copy-start.10 = (s32[3,64,2]{1,2,0:T(2,128)S(1)}, s32[3,64,2]{1,2,0:T(2,128)}, u32[]{:S(2)}) copy-start(s32[3,64,2]{1,2,0:T(2,128)} %param.12) | copy-start | bytes 4612
  42.8 9.7 %copy-start.8 = (s32[3,8]{1,0:T(4,128)S(1)}, s32[3,8]{1,0:T(4,128)}, u32[]{:S(2)}) copy-start(s32[3,8]{1,0:T(4,128)} %refs_1_.9) | copy-start | bytes 292
  45.8 0.8 copy-start.5
  49.3 3.1 %collective-permute-start.11 = (f32[1024,128]{1,0:T(8,128)}, f32[1024,128]{1,0:T(8,128)}, u32[]{:S(2)}, u32[]{:S(2)}) collective-permute-start(f32[1024,128]{1,0:T(8,128)} %collective-permute-done.10.refs_5_), channel_id=1, source_target_pairs={{0,1},{1,0},{2,3},{3,2},{4,5},{5,4},{6,7},{7,6},{8,9},{9,8},{10,11... | collective-permute-start | bytes 1572872 | tf_op jit(solution)/shard_map/ppermute | solution.py:421
  49.4 3.1 %collective-permute-start.9 = (f32[1024,128]{1,0:T(8,128)}, f32[1024,128]{1,0:T(8,128)}, u32[]{:S(2)}, u32[]{:S(2)}) collective-permute-start(f32[1024,128]{1,0:T(8,128)} %get-tuple-element.83.refs_3_), channel_id=1, source_target_pairs={{0,1},{1,0},{2,3},{3,2},{4,5},{5,4},{6,7},{7,6},{8,9},{9,8},{10,11... | collective-permute-start | bytes 1572872 | tf_op jit(solution)/shard_map/ppermute | solution.py:421
  49.9 11.6 %collective-permute-start.12 = (f32[1024,128]{1,0:T(8,128)}, f32[1024,128]{1,0:T(8,128)}, u32[]{:S(2)}, u32[]{:S(2)}) collective-permute-start(f32[1024,128]{1,0:T(8,128)} %collective-permute-done.5.refs_3_), channel_id=1, source_target_pairs={{0,1},{1,0},{2,3},{3,2},{4,5},{5,4},{6,7},{7,6},{8,9},{9,8},{10,11... | collective-permute-start | bytes 1572872 | tf_op jit(solution)/shard_map/ppermute | solution.py:421
  50.2 6.0 %copy-start.4 = (f32[1024,128]{1,0:T(8,128)S(1)}, f32[1024,128]{1,0:T(8,128)}, u32[]{:S(2)}) copy-start(f32[1024,128]{1,0:T(8,128)} %copy-done.3) | copy-start | bytes 1572868
  50.2 25.1 %collective-permute-start.14 = (f32[1024,128]{1,0:T(8,128)}, f32[1024,128]{1,0:T(8,128)S(1)}, u32[]{:S(2)}, u32[]{:S(2)}) collective-permute-start(f32[1024,128]{1,0:T(8,128)} %copy-done.3), channel_id=1, source_target_pairs={{0,8},{4,12},{8,0},{12,4},{16,24},{20,28},{24,16},{28,20},{1,9},{5... | collective-permute-start | bytes 1572872 | tf_op jit(solution)/shard_map/ppermute | solution.py:424
  52.1 26.9 %collective-permute-start.15 = (f32[1024,128]{1,0:T(8,128)}, f32[1024,128]{1,0:T(8,128)S(1)}, u32[]{:S(2)}, u32[]{:S(2)}) collective-permute-start(f32[1024,128]{1,0:T(8,128)} %copy-done.3), channel_id=1, source_target_pairs={{0,16},{4,20},{8,24},{12,28},{16,0},{20,4},{24,8},{28,12},{1,17},{... | collective-permute-start | bytes 1572872 | tf_op jit(solution)/shard_map/ppermute | solution.py:424
  56.2 22.8 %collective-permute-start.13 = (f32[1024,128]{1,0:T(8,128)S(1)}, f32[1024,128]{1,0:T(8,128)S(1)}, u32[]{:S(2)}, u32[]{:S(2)}) collective-permute-start(f32[1024,128]{1,0:T(8,128)S(1)} %copy-done.4), channel_id=1, source_target_pairs={{0,4},{4,0},{8,12},{12,8},{16,20},{20,16},{24,28},{28,24},{1,5},{5... | collective-permute-start | bytes 1572872 | tf_op jit(solution)/shard_map/ppermute | solution.py:424
  61.5 3.9 %copy-start.6 = (f32[1024,128]{1,0:T(8,128)S(1)}, f32[1024,128]{1,0:T(8,128)}, u32[]{:S(2)}) copy-start(f32[1024,128]{1,0:T(8,128)} %copy-done.5) | copy-start | bytes 1572868
  65.4 7.5 %copy-start.1 = (bf16[1024,1024]{1,0:T(8,128)(2,1)S(1)}, bf16[1024,1024]{1,0:T(8,128)(2,1)}, u32[]{:S(2)}) copy-start(bf16[1024,1024]{1,0:T(8,128)(2,1)} %copy-done) | copy-start | bytes 6291460
  70.4 14.1 %collective-permute-start.21 = (f32[1024,128]{1,0:T(8,128)S(1)}, f32[1024,128]{1,0:T(8,128)S(1)}, u32[]{:S(2)}, u32[]{:S(2)}) collective-permute-start(f32[1024,128]{1,0:T(8,128)S(1)} %get-tuple-element.103.refs_3_), channel_id=1, source_target_pairs={{0,4},{4,0},{8,12},{12,8},{16,20},{20,16},{24,28},{28,24},{1,5},{5... | collective-permute-start | bytes 1572872 | tf_op jit(solution)/shard_map/ppermute | solution.py:424
  71.0 26.8 %collective-permute-start.20 = (f32[1024,128]{1,0:T(8,128)S(1)}, f32[1024,128]{1,0:T(8,128)S(1)}, u32[]{:S(2)}, u32[]{:S(2)}) collective-permute-start(f32[1024,128]{1,0:T(8,128)S(1)} %get-tuple-element.103.refs_3_), channel_id=1, source_target_pairs={{0,8},{4,12},{8,0},{12,4},{16,24},{20,28},{24,16},{28,20},{1,9},{5... | collective-permute-start | bytes 1572872 | tf_op jit(solution)/shard_map/ppermute | solution.py:424
  75.3 27.1 %collective-permute-start.19 = (f32[1024,128]{1,0:T(8,128)S(1)}, f32[1024,128]{1,0:T(8,128)S(1)}, u32[]{:S(2)}, u32[]{:S(2)}) collective-permute-start(f32[1024,128]{1,0:T(8,128)S(1)} %get-tuple-element.103.refs_3_), channel_id=1, source_target_pairs={{0,16},{4,20},{8,24},{12,28},{16,0},{20,4},{24,8},{28,12},{1,17},{... | collective-permute-start | bytes 1572872 | tf_op jit(solution)/shard_map/ppermute | solution.py:424
  83.4 21.7 %collective-permute-start.18 = (f32[1024,128]{1,0:T(8,128)S(1)}, f32[1024,128]{1,0:T(8,128)S(1)}, u32[]{:S(2)}, u32[]{:S(2)}) collective-permute-start(f32[1024,128]{1,0:T(8,128)S(1)} %get-tuple-element.102.refs_3_), channel_id=1, source_target_pairs={{0,4},{4,0},{8,12},{12,8},{16,20},{20,16},{24,28},{28,24},{1,5},{5... | collective-permute-start | bytes 1572872 | tf_op jit(solution)/shard_map/ppermute | solution.py:424
  83.7 36.2 %collective-permute-start.17 = (f32[1024,128]{1,0:T(8,128)S(1)}, f32[1024,128]{1,0:T(8,128)S(1)}, u32[]{:S(2)}, u32[]{:S(2)}) collective-permute-start(f32[1024,128]{1,0:T(8,128)S(1)} %get-tuple-element.102.refs_3_), channel_id=1, source_target_pairs={{0,8},{4,12},{8,0},{12,4},{16,24},{20,28},{24,16},{28,20},{1,9},{5... | collective-permute-start | bytes 1572872 | tf_op jit(solution)/shard_map/ppermute | solution.py:424
  84.5 39.1 %collective-permute-start.16 = (f32[1024,128]{1,0:T(8,128)S(1)}, f32[1024,128]{1,0:T(8,128)S(1)}, u32[]{:S(2)}, u32[]{:S(2)}) collective-permute-start(f32[1024,128]{1,0:T(8,128)S(1)} %get-tuple-element.102.refs_3_), channel_id=1, source_target_pairs={{0,16},{4,20},{8,24},{12,28},{16,0},{20,4},{24,8},{28,12},{1,17},{... | collective-permute-start | bytes 1572872 | tf_op jit(solution)/shard_map/ppermute | solution.py:424
